TPU v7x, 256 devices: a whole 4x4x8 slice. The times are simulated.
256 devices in a mesh: dp: 16 (over x_lo, y, core), feat: 16 (over x_hi, z).
Axes of the slice: x: 4 (x_hi: 2, x_lo: 2; x = x_hi * 2 + x_lo), y: 4, z: 8, core: 2. Of those that a mesh axis runs over, the one named last changes fastest.
Arguments:
- view_a: bfloat16 [2048, 16384], P('dp', 'feat'), may hold values from -240 to 240
- view_b: bfloat16 [2048, 16384], P('dp', 'feat'), may hold values from -240 to 240
Outputs:
- grad_a: bfloat16 [2048, 16384], P('dp', 'feat')
- grad_b: bfloat16 [2048, 16384], P('dp', 'feat')
All inputs are finite; a program needn't handle non-finite values.
Results may differ from a plain program's by a relative error of at most 0.028.
Values may be sent and summed in bfloat16 or wider, within the bound.
No kernel may reach another device: no remote copies, remote signals or barrier semaphores. Data moves between devices by JAX's collectives and lax.ppermute only.
A program may use at most 128 MiB of HBM per device.

v0:
```python
import jax
import jax.numpy as jnp
from jax import lax
from jax.sharding import PartitionSpec as P

off_weight = 0.0051
epsilon = 1e-05


def normalize(view):
    values = view.astype(jnp.float32)
    col_mean = jnp.mean(values, 0)
    centered = values - col_mean
    spread = jnp.sqrt(jnp.mean(centered * centered, 0) + epsilon)
    return ((centered / spread).astype(jnp.bfloat16), spread)


def backward_feature_major(upward, normed_t, spread):
    normal_f = normed_t.astype(jnp.float32)
    first_mean = jnp.mean(upward, 1, keepdims=True)
    second_mean = jnp.mean(upward * normal_f, 1, keepdims=True)
    return ((upward - first_mean - normal_f * second_mean) / spread[:, None]).astype(jnp.bfloat16)


def on_device(view_a, view_b):
    row_count = view_a.shape[0]
    col_width = view_a.shape[1]
    dp_count = lax.axis_size("dp")
    feat_count = lax.axis_size("feat")
    batch_size = row_count * dp_count
    sub_width = col_width // dp_count
    dp_index = lax.axis_index("dp")
    feat_index = lax.axis_index("feat")
    values = view_a.astype(jnp.float32)
    col_mean = lax.psum(jnp.sum(values, 0), "dp") / batch_size
    centered = values - col_mean
    variance = lax.psum(jnp.sum(centered * centered, 0), "dp") / batch_size
    spread_a = jnp.sqrt(variance + epsilon)
    normed_local = (centered / spread_a).astype(jnp.bfloat16)
    full_a = lax.all_gather(normed_local, "dp", axis=0, tiled=True)
    cols_b = lax.all_to_all(view_b, "dp", split_axis=1, concat_axis=0, tiled=True)
    normed_sub_b, spread_b = normalize(cols_b)
    gathered_b = lax.all_gather(normed_sub_b, "feat", axis=1, tiled=True)
    corr = lax.dot_general(
        full_a, gathered_b, (((0,), (0,)), ((), ())), preferred_element_type=jnp.float32
    ) * (1.0 / batch_size)
    tile_cols = feat_count * sub_width
    row_ids = feat_index * col_width + lax.broadcasted_iota(jnp.int32, (col_width, tile_cols), 0)
    col_pos = lax.broadcasted_iota(jnp.int32, (col_width, tile_cols), 1)
    col_ids = col_pos // sub_width * col_width + dp_index * sub_width + col_pos % sub_width
    corr_grad = jnp.where(row_ids == col_ids, 2.0 * (corr - 1.0), 2.0 * off_weight * corr).astype(
        jnp.bfloat16
    )
    section = corr_grad
    up_b = lax.psum_scatter(
        lax.dot_general(
            section, full_a, (((0,), (1,)), ((), ())), preferred_element_type=jnp.float32
        ),
        "feat",
        scatter_dimension=0,
        tiled=True,
    )
    out_b = backward_feature_major(up_b, normed_sub_b.T, spread_b)
    grad_b = lax.all_to_all(out_b, "dp", split_axis=1, concat_axis=0, tiled=True).T
    section = gathered_b
    up_a = lax.psum_scatter(
        lax.dot_general(
            section, corr_grad, (((1,), (1,)), ((), ())), preferred_element_type=jnp.float32
        ).astype(jnp.bfloat16),
        "dp",
        scatter_dimension=0,
        tiled=True,
    ).astype(jnp.float32)
    normal_f = normed_local.astype(jnp.float32)
    first_sum, second_sum = lax.psum((jnp.sum(up_a, 0), jnp.sum(up_a * normal_f, 0)), "dp")
    grad_a = (
        (up_a - first_sum / batch_size - normal_f * (second_sum / batch_size)) / spread_a
    ).astype(jnp.bfloat16)
    return (grad_a, grad_b)


def solution(mesh):
    in_specs = (P("dp", "feat"), P("dp", "feat"))
    out_specs = (P("dp", "feat"), P("dp", "feat"))
    return jax.shard_map(
        on_device, mesh=mesh, in_specs=in_specs, out_specs=out_specs, check_vma=False
    )
```

profile of v0, /device:TPU:1, one launch (start us, length us, event | category | flops | bytes accessed | tf_op | source)
XLA Modules:
  0.0 544.3 jit_solution(3774871995365809456)
XLA Ops:
  7.2 0.0 all-gather.5.cloned.1.call-start
  7.2 1.0 convert_reduce_fusion.2
  8.2 29.7 %psum.28 = f32[1024]{0:T(1024)S(1)} all-reduce(f32[1024]{0:T(1024)S(1)} %convert_reduce_fusion.2), channel_id=1, replica_groups=mesh['dp'=16,'feat'=16] {'dp'}, use_global_device_ids=true, to_apply=%region_3.0 | all-reduce | flops 1024 | bytes 8192 | tf_op jit(solution)/shard_map/psum | solution.py:35
  38.0 1.0 fusion.29
  39.0 28.8 %psum.29 = f32[1024]{0:T(1024)S(1)} all-reduce(f32[1024]{0:T(1024)S(1)} %fusion.29), channel_id=1, replica_groups=mesh['dp'=16,'feat'=16] {'dp'}, use_global_device_ids=true, to_apply=%region_5.0 | all-reduce | flops 1024 | bytes 8192 | tf_op jit(solution)/shard_map/psum | solution.py:37
  67.8 1.7 fusion.30
  69.5 0.0 all-gather.5.cloned.1.call-update
  69.5 0.0 all-gather.3.cloned.1.call-start
  69.6 1.1 copy.6
  70.7 10.3 %all_to_all.32 = bf16[128,16,64]{0,2,1:T(8,128)(2,1)S(1)} all-to-all(bf16[128,16,64]{0,2,1:T(8,128)(2,1)S(1)} %bitcast.48), channel_id=1, replica_groups=mesh['dp'=16,'feat'=16] {'dp'}, dimensions={1} | all-to-all | bytes 524288 | tf_op jit(solution)/shard_map/all_to_all | solution.py:41
  81.0 0.1 convert_reduce_fusion
  81.2 0.2 fusion.36
  81.4 0.8 fusion.38
  82.3 0.0 all-gather.3.cloned.1.call-update
  82.3 0.0 reduce-scatter.3.cloned.1.call-start
  82.4 27.6 %all-gather.5.cloned.1.call-done = bf16[2048,1024]{1,0:T(8,128)(2,1)} async-done(((bf16[128,1024]{1,0:T(8,128)(2,1)}), bf16[2048,1024]{1,0:T(8,128)(2,1)}) %all-gather.5.cloned.1.call-update) | async-done | bytes 4194320 | tf_op jit(solution)/shard_map/all_gather | solution.py:40
  110.0 99.6 %all-gather.3.cloned.1.call-done = bf16[2048,1024]{0,1:T(8,128)(2,1)} async-done(((bf16[2048,64]{0,1:T(8,128)(2,1)}), bf16[2048,1024]{0,1:T(8,128)(2,1)}) %all-gather.3.cloned.1.call-update) | async-done | bytes 4194320 | tf_op jit(solution)/shard_map/all_gather | solution.py:43
  209.6 0.0 copy-start.1
  209.6 7.8 %fusion.61 = f32[1024,1024]{1,0:T(8,128)S(1)} fusion(bf16[2048,1024]{1,0:T(8,128)(2,1)} %all-gather.5.cloned.1.call-done, bf16[2048,1024]{0,1:T(8,128)(2,1)} %all-gather.3.cloned.1.call-done), kind=kOutput, calls=%fused_computation.90 | convolution fusion | flops 4294967296 | bytes 12582912 | tf_op jit(solution)/shard_map/dot_general | solution.py:44
  217.4 0.0 copy-start.2
  217.4 1.9 copy-done.2
  219.3 0.0 copy-done.1
  219.3 7.3 %convolution_convert_fusion = bf16[2048,1024]{1,0:T(8,128)(2,1)} fusion(bf16[2048,1024]{0,1:T(8,128)(2,1)S(1)} %copy-done.1, f32[1024,1024]{1,0:T(8,128)S(1)} %fusion.61, s32[1024]{0:T(1024)S(1)} %get-tuple-element.11, s32[1024]{0:T(1024)S(1)} %get-tuple-element.12, s32[]{:T(128)S(6)} %mul.64, s32[1024]{0:T(1024)S(1)} %get-tuple-element.10, ...), kind=kOutput, calls=%fused_computation.2 | convolution fusion | flops 4309647360 | bytes 12605444 | tf_op jit(solution)/shard_map/dot_general | solution.py:67
  226.7 0.0 reduce-scatter.3.cloned.1.call-update
  226.7 0.0 reduce-scatter.5.cloned.1.call-start
  226.7 11.7 %fusion = f32[1024,2048]{1,0:T(8,128)} fusion(bf16[2048,1024]{1,0:T(8,128)(2,1)} %all-gather.5.cloned.1.call-done, f32[1024,1024]{1,0:T(8,128)} %copy-done.2, s32[1024]{0:T(1024)S(1)} %get-tuple-element.11, s32[1024]{0:T(1024)S(1)} %get-tuple-element.12, s32[]{:T(128)S(6)} %mul.64, s32[1024]{0:T(1024)S(1)} %get-tuple-element.10, ...), kind=kOutput, calls=%fused_computation.3 | convolution fusion | flops 4307550208 | bytes 16799748 | tf_op jit(solution)/shard_map/dot_general | solution.py:56
  238.5 0.0 copy-start
  238.5 0.0 reduce-scatter.5.cloned.1.call-update
  238.5 53.9 %reduce-scatter.3.cloned.1.call-done = bf16[128,1024]{1,0:T(8,128)(2,1)} async-done(((bf16[2048,1024]{1,0:T(8,128)(2,1)}), bf16[128,1024]{1,0:T(8,128)(2,1)}) %reduce-scatter.3.cloned.1.call-update) | async-done | bytes 262160 | tf_op jit(solution)/shard_map/reduce_scatter | solution.py:66
  292.4 0.0 copy-done
  292.4 1.1 convert_reduce_fusion.1
  293.5 31.3 %all-reduce = (f32[1024]{0:T(1024)S(1)}, f32[1024]{0:T(1024)S(1)}) all-reduce(f32[1024]{0:T(1024)S(1)} %get-tuple-element.7, f32[1024]{0:T(1024)S(1)} %get-tuple-element.6), channel_id=1, replica_groups=mesh['dp'=16,'feat'=16] {'dp'}, use_global_device_ids=true, to_apply=%region_10.11 | all-reduce | flops 2048 | bytes 16384 | tf_op jit(solution)/shard_map/psum | solution.py:75
  324.8 192.4 %reduce-scatter.5.cloned.1.call-done = f32[64,2048]{1,0:T(8,128)} async-done(((f32[1024,2048]{1,0:T(8,128)}), f32[64,2048]{1,0:T(8,128)}) %reduce-scatter.5.cloned.1.call-update) | async-done | bytes 524304 | tf_op jit(solution)/shard_map/reduce_scatter | solution.py:55
  517.2 1.3 fusion.60
  518.6 2.0 copy_bitcast_fusion
  520.6 9.2 %all-to-all-start.1 = ((bf16[64,16,128]{2,0,1:T(8,128)(2,1)}), bf16[64,16,128]{2,0,1:T(8,128)(2,1)S(1)}, u32[]{:S(2)}, u32[]{:S(2)}) async-start(bf16[64,16,128]{2,0,1:T(8,128)(2,1)} %copy_bitcast_fusion), calls=%async_computation.3 | async-start | bytes 524288 | tf_op jit(solution)/shard_map/all_to_all | solution.py:64
  529.7 1.8 fusion.33
  531.5 5.4 all-to-all-done.1
  536.9 0.9 copy.9
  (12 shorter events, 0.1 us)
Async XLA Ops:
  7.2 102.9 %all-gather.5.cloned.1.call-start = ((), (), s32[]{:S(2)}) async-start(), calls=%async_computation.5 | async-start | bytes 4456448 | tf_op jit(solution)/shard_map/all_gather | solution.py:40
  69.5 140.1 %all-gather.3.cloned.1.call-start = ((), (), s32[]{:S(2)}) async-start(), calls=%async_computation.4 | async-start | bytes 4456448 | tf_op jit(solution)/shard_map/all_gather | solution.py:43
  82.3 210.1 %reduce-scatter.3.cloned.1.call-start = ((), (), s32[]{:S(2)}) async-start(), calls=%async_computation.6 | async-start | bytes 4456448 | tf_op jit(solution)/shard_map/reduce_scatter | solution.py:66
  209.6 9.7 %copy-start.1 = (bf16[2048,1024]{0,1:T(8,128)(2,1)S(1)}, bf16[2048,1024]{0,1:T(8,128)(2,1)}, u32[]{:S(2)}) copy-start(bf16[2048,1024]{0,1:T(8,128)(2,1)} %all-gather.3.cloned.1.call-done) | copy-start | bytes 12582916
  217.4 1.9 copy-start.2
  226.7 290.6 %reduce-scatter.5.cloned.1.call-start = ((), (), s32[]{:S(2)}) async-start(), calls=%async_computation.7 | async-start | bytes 8912896 | tf_op jit(solution)/shard_map/reduce_scatter | solution.py:55
  238.5 53.9 %copy-start = (bf16[128,1024]{1,0:T(8,128)(2,1)S(1)}, bf16[128,1024]{1,0:T(8,128)(2,1)}, u32[]{:S(2)}) copy-start(bf16[128,1024]{1,0:T(8,128)(2,1)} %param.2) | copy-start | bytes 786436
  520.6 16.3 %all-to-all-start.1 = ((bf16[64,16,128]{2,0,1:T(8,128)(2,1)}), bf16[64,16,128]{2,0,1:T(8,128)(2,1)S(1)}, u32[]{:S(2)}, u32[]{:S(2)}) async-start(bf16[64,16,128]{2,0,1:T(8,128)(2,1)} %copy_bitcast_fusion), calls=%async_computation.3 | async-start | bytes 524288 | tf_op jit(solution)/shard_map/all_to_all | solution.py:64
Sparse Core Ops, SparseCore 0:
  69.7 40.3 all-gather.4
  113.2 96.3 all-gather.2
  226.8 65.5 reduce-scatter.2
  296.4 220.8 reduce-scatter.4
where the time goes:
time: 545 us; the launch traced here: 544 us
  waiting for transfers between devices  379 us (70%)
  blocking collectives  100 us (18%)
  matrix products  26.8 us (5%)
  between operations  13.9 us (3%)
  other arithmetic  11.3 us (2%)
  starting transfers between devices  9.32 us (2%)
    reduce_scatter x1, waiting for transfers between devices, on_device(): lax.psum_scatter(lax.dot_general(section, full_a, (((0,), (1,)), ((), ())...  192 us
    all_gather x1, waiting for transfers between devices, on_device(): gathered_b = lax.all_gather(normed_sub_b, 'feat', axis=1, tiled=True)  99.6 us
    reduce_scatter x1, waiting for transfers between devices, on_device(): lax.psum_scatter(lax.dot_general(section, corr_grad, (((1,), (1,)), ((),...  53.9 us
    psum x1, blocking collectives, on_device(): lax.psum((jnp.sum(up_a, 0), jnp.sum(up_a * normal_f, 0)), 'dp')  31.3 us
    psum x1, blocking collectives, on_device(): col_mean = lax.psum(jnp.sum(values, 0), 'dp') / batch_size  29.7 us
    psum x1, blocking collectives, on_device(): variance = lax.psum(jnp.sum(centered * centered, 0), 'dp') / batch_size  28.8 us
    all_gather x1, waiting for transfers between devices, on_device(): full_a = lax.all_gather(normed_local, 'dp', axis=0, tiled=True)  27.6 us
    dot_general x1, matrix products, on_device(): lax.dot_general(section, full_a, (((0,), (1,)), ((), ())), preferred_elem...  11.7 us
  transfers between devices with their start and end apart: 5, of which 5 were waited for; matrix products, arithmetic and copies ran while one was open for 3% of the time, Pallas kernels for 0%

commit v1 on v0

v1 whole, which is shorter than its diff:
```python
import functools

import jax
import jax.numpy as jnp
from jax import lax
from jax.experimental import pallas as pl
from jax.experimental.pallas import tpu as pltpu
from jax.sharding import PartitionSpec as P

off_weight = 0.0051
epsilon = 1e-05
f32 = jnp.float32
bf16 = jnp.bfloat16

X_LO, Y, CORES = 2, 4, 2


def dp_perm(move):
    def index(x, y, c):
        return (x * Y + y) * CORES + c

    return [
        (index(x, y, c), index(*move(x, y, c)))
        for x in range(X_LO)
        for y in range(Y)
        for c in range(CORES)
    ]


TO_CORE = dp_perm(lambda x, y, c: (x, y, 1 - c))
TO_X = dp_perm(lambda x, y, c: (1 - x, y, c))
TO_UP = dp_perm(lambda x, y, c: (x, (y + 1) % Y, c))
TO_DOWN = dp_perm(lambda x, y, c: (x, (y - 1) % Y, c))


def call(body, outs, *args, flops=0):
    def size(s):
        return s.size * s.dtype.itemsize

    return pl.pallas_call(
        body,
        out_shape=outs,
        in_specs=[pl.BlockSpec(memory_space=pltpu.VMEM)] * len(args),
        out_specs=jax.tree.map(lambda _: pl.BlockSpec(memory_space=pltpu.VMEM), outs),
        compiler_params=pltpu.CompilerParams(vmem_limit_bytes=40 * 2**20),
        cost_estimate=pl.CostEstimate(
            flops=flops,
            bytes_accessed=sum(size(a) for a in args) + sum(size(o) for o in jax.tree.leaves(outs)),
            transcendentals=0,
        ),
    )(*args)


def shape(*dims, dtype=f32):
    return jax.ShapeDtypeStruct(dims, dtype)


def gather_chips(view):
    half = view.shape[1] // 2
    from_down = lax.ppermute(view, "dp", TO_UP)
    from_up = lax.ppermute(view, "dp", TO_DOWN)
    from_x = lax.ppermute(view, "dp", TO_X)
    far_left = lax.ppermute(from_down[:, :half], "dp", TO_UP)
    far_right = lax.ppermute(from_up[:, half:], "dp", TO_DOWN)
    x_down = lax.ppermute(from_x, "dp", TO_UP)
    x_up = lax.ppermute(from_x, "dp", TO_DOWN)
    far = jnp.concatenate([far_left, far_right], 1)
    x_far = lax.ppermute(far, "dp", TO_X)
    return [view, from_down, from_up, from_x, far, x_down, x_up, x_far]


def moments_body(*refs):
    pieces, out = refs[:-1], refs[-1]
    count = sum(p.shape[0] for p in pieces)
    total = sum(jnp.sum(p[...].astype(f32), 0, keepdims=True) for p in pieces)
    mean = total / count
    square = 0.0
    for p in pieces:
        centered = p[...].astype(f32) - mean
        square = square + jnp.sum(centered * centered, 0, keepdims=True)
    out[0:1, :] = mean
    out[1:2, :] = square


def gram_body(batch, *refs):
    *pieces, sib, own_m, sib_m, normed, normed_sib, spread_out, gram = refs
    mean = 0.5 * (own_m[0:1, :] + sib_m[0:1, :])
    gap = own_m[0:1, :] - sib_m[0:1, :]
    square = own_m[1:2, :] + sib_m[1:2, :] + gap * gap * (batch / 4)
    spread = jnp.sqrt(square / batch + epsilon)
    spread_out[...] = spread
    rows = sib.shape[0]
    normed_sib[...] = ((sib[...].astype(f32) - mean) / spread).astype(bf16)
    for i, p in enumerate(pieces):
        normed[i * rows : (i + 1) * rows, :] = ((p[...].astype(f32) - mean) / spread).astype(bf16)
    groups, part = gram.shape[0], gram.shape[1]
    nt = (((1,), (1,)), ((), ()))
    for i in range(len(pieces)):
        block = normed[i * rows : (i + 1) * rows, :]
        top = lax.dot_general(normed[0:rows, :], block, nt, preferred_element_type=f32)
        low = lax.dot_general(normed_sib[...], block, nt, preferred_element_type=f32)
        gram[0 : groups // 2, :, i * rows : (i + 1) * rows] = top.astype(bf16).reshape(
            groups // 2, part, rows
        )
        gram[groups // 2 :, :, i * rows : (i + 1) * rows] = low.astype(bf16).reshape(
            groups // 2, part, rows
        )


def diag_body(a, b, out):
    total = 0.0
    step = 128
    for i in range(a.shape[0] // step):
        s = slice(i * step, (i + 1) * step)
        total = total + jnp.sum(a[s, :].astype(f32) * b[s, :].astype(f32), 0, keepdims=True)
    out[...] = total


def reduce_body(parts, out):
    total = parts[0].astype(f32)
    for i in range(1, parts.shape[0]):
        total = total + parts[i].astype(f32)
    total = total.astype(bf16)
    for i in range(out.shape[0]):
        out[i] = total


def apply_body(scale, gram, normed, own, other):
    rows = own.shape[0]
    own[...] = scale * jnp.dot(gram[0:rows, :], normed[...], preferred_element_type=f32)
    other[...] = scale * jnp.dot(gram[rows:, :], normed[...], preferred_element_type=f32)


def upward_body(batch, own, recv, normed_other, normed_self, diag_own, diag_sib, up_out, sums):
    rows = own.shape[0]
    corr = (diag_own[...] + diag_sib[...]) / batch
    diag = 2.0 * (corr - 1.0) - 2.0 * off_weight * corr
    up = own[...] + recv[...] + normed_other[0:rows, :].astype(f32) * diag
    up_out[...] = up
    first = jnp.sum(up, 0, keepdims=True)
    second = jnp.sum(up * normed_self[0:rows, :].astype(f32), 0, keepdims=True)
    for i in range(sums.shape[0]):
        sums[i, 0:1, :] = first
        sums[i, 1:2, :] = second


def final_body(batch, up, normed_self, sums, spread, out):
    rows = up.shape[0]
    total = sums[0]
    for i in range(1, sums.shape[0]):
        total = total + sums[i]
    total = total / batch
    normal = normed_self[0:rows, :].astype(f32)
    out[...] = ((up[...] - total[0:1, :] - normal * total[1:2, :]) / spread[...]).astype(bf16)


def on_device(view_a, view_b):
    rows, cols = view_a.shape
    dp_count = lax.axis_size("dp")
    feat_count = lax.axis_size("feat")
    batch = rows * dp_count
    half = batch // CORES
    part = CORES * rows // feat_count
    scale = 2.0 * off_weight / batch

    def prepare(view):
        pieces = gather_chips(view)
        sib = lax.ppermute(view, "dp", TO_CORE)
        moments = call(moments_body, shape(2, cols), *pieces)
        moments_sib = lax.ppermute(moments, "dp", TO_CORE)
        return call(
            functools.partial(gram_body, batch),
            (
                shape(half, cols, dtype=bf16),
                shape(rows, cols, dtype=bf16),
                shape(1, cols),
                shape(feat_count, part, half, dtype=bf16),
            ),
            *pieces,
            sib,
            moments,
            moments_sib,
            flops=2 * CORES * rows * half * cols,
        )

    def reduce(gram):
        parts = lax.all_to_all(gram, "feat", 0, 0)
        total = call(reduce_body, shape(feat_count, part, half, dtype=bf16), parts)
        whole = lax.all_to_all(total, "feat", 0, 0)
        return whole.reshape(CORES * rows, half)

    def upward(gram, normed_self, normed_other, diag, diag_sib):
        own, other = call(
            functools.partial(apply_body, scale),
            (shape(rows, cols), shape(rows, cols)),
            gram,
            normed_self,
            flops=2 * CORES * rows * half * cols,
        )
        recv = lax.ppermute(other, "dp", TO_CORE)
        return call(
            functools.partial(upward_body, batch),
            (shape(rows, cols), shape(dp_count, 2, cols)),
            own,
            recv,
            normed_other,
            normed_self,
            diag,
            diag_sib,
        )

    def finish(up, sums, normed_self, spread):
        sums = lax.all_to_all(sums, "dp", 0, 0)
        return call(
            functools.partial(final_body, batch),
            shape(rows, cols, dtype=bf16),
            up,
            normed_self,
            sums,
            spread,
        )

    normed_a, _, spread_a, part_a = prepare(view_a)
    gram_a = reduce(part_a)
    normed_b, _, spread_b, part_b = prepare(view_b)
    gram_b = reduce(part_b)
    diag = call(diag_body, shape(1, cols), normed_a, normed_b)
    diag_sib = lax.ppermute(diag, "dp", TO_CORE)
    up_b, sums_b = upward(gram_a, normed_b, normed_a, diag, diag_sib)
    grad_b = finish(up_b, sums_b, normed_b, spread_b)
    up_a, sums_a = upward(gram_b, normed_a, normed_b, diag, diag_sib)
    grad_a = finish(up_a, sums_a, normed_a, spread_a)
    return (grad_a, grad_b)


def solution(mesh):
    spec = P("dp", "feat")
    return jax.shard_map(
        on_device, mesh=mesh, in_specs=(spec, spec), out_specs=(spec, spec), check_vma=False
    )
```

time: 545 us -> 173 us (0.32)
  waiting for transfers between devices: 379 us -> 61.6 us
  blocking collectives: 100 us -> 0 us
  starting transfers between devices: 9.32 us -> 80.2 us
  matrix products: 26.8 us -> 0 us
  Pallas kernels: 0 us -> 13.9 us
  between operations: 13.9 us -> 0.89 us
  local copies, waits for them, and re-layouts: 3.89 us -> 15.8 us
  other arithmetic: 11.3 us -> 0 us
    reduce_scatter x2 -> x0, waiting for transfers between devices: 246 us -> none  [the longest x1 192 us: on_device(): lax.psum_scatter(lax.dot_general(section, full_a, (((0,), (1,)), ((), ())...]
    all_gather x2 -> x0, waiting for transfers between devices: 127 us -> none  [the longest x1 99.6 us: on_device(): gathered_b = lax.all_gather(normed_sub_b, 'feat', axis=1, tiled=True)]
    psum x3 -> x0, blocking collectives: 89.8 us -> none  [the longest x1 31.3 us: on_device(): lax.psum((jnp.sum(up_a, 0), jnp.sum(up_a * normal_f, 0)), 'dp')]
    ppermute x0 -> x23, starting transfers between devices: none -> 38.7 us  [the longest x2 6.74 us: prepare(): moments_sib = lax.ppermute(moments, 'dp', TO_CORE)]
    all_to_all x1 -> x6, waiting for transfers between devices: 5.36 us -> 42 us  [the longest x2 22.1 us: reduce(): whole = lax.all_to_all(total, 'feat', 0, 0)]
    all_to_all x1 -> x6, starting transfers between devices: 9.15 us -> 41.5 us  [the longest x2 20.9 us: reduce(): parts = lax.all_to_all(gram, 'feat', 0, 0)]
    dot_general x3 -> x0, matrix products: 26.8 us -> none  [the longest x1 11.7 us: on_device(): lax.dot_general(section, full_a, (((0,), (1,)), ((), ())), preferred_elem...]
    ppermute x0 -> x23, waiting for transfers between devices: none -> 19.6 us  [the longest x2 8.35 us: gather_chips(): from_down = lax.ppermute(view, 'dp', TO_UP)]
  transfers between devices with their start and end apart: 5 -> 29, of which waited for: 5 -> 15; matrix products, arithmetic and copies ran while one was open for 3% -> 0% of each run, Pallas kernels for 0% -> 6%
where the time goes in v1:
time: 173 us; the launch traced here: 172 us
  starting transfers between devices  80.2 us (46%)
  waiting for transfers between devices  61.6 us (36%)
  local copies, waits for them, and re-layouts  15.8 us (9%)
  Pallas kernels  13.9 us (8%)
    all_to_all x2, waiting for transfers between devices, reduce(): whole = lax.all_to_all(total, 'feat', 0, 0)  22.1 us
    all_to_all x2, starting transfers between devices, reduce(): parts = lax.all_to_all(gram, 'feat', 0, 0)  20.9 us
    unnamed x40, local copies, waits for them, and re-layouts  15.8 us
    all_to_all x2, waiting for transfers between devices, reduce(): parts = lax.all_to_all(gram, 'feat', 0, 0)  14.3 us
    pallas_call x13, Pallas kernels, call(): pl.pallas_call(body, out_shape=outs, in_specs=[pl.BlockSpec(memory_space=...  13.9 us
    all_to_all x2, starting transfers between devices, reduce(): whole = lax.all_to_all(total, 'feat', 0, 0)  12.9 us
    ppermute x2, waiting for transfers between devices, gather_chips(): from_down = lax.ppermute(view, 'dp', TO_UP)  8.35 us
    all_to_all x2, starting transfers between devices, finish(): sums = lax.all_to_all(sums, 'dp', 0, 0)  7.64 us
  transfers between devices with their start and end apart: 29, of which 15 were waited for; matrix products, arithmetic and copies ran while one was open for 0% of the time, Pallas kernels for 6%

profile of v1, /device:TPU:1, one launch (start us, length us, event | category | flops | bytes accessed | tf_op | source)
XLA Modules:
  0.0 172.4 jit_solution(15339747937024400834)
XLA Ops:
  0.6 2.2 %collective-permute-start = (bf16[128,1024]{1,0:T(8,128)(2,1)}, bf16[128,1024]{1,0:T(8,128)(2,1)S(1)}, u32[]{:S(2)}, u32[]{:S(2)}) collective-permute-start(bf16[128,1024]{1,0:T(8,128)(2,1)} %refs_0_.5), channel_id=1, source_target_pairs={{0,32},{16,48},{32,64},{48,80},{64,96},{80,112},{96,0},{112,16},{1... | collective-permute-start | bytes 786440 | tf_op jit(solution)/shard_map/ppermute | solution.py:60
  2.8 1.5 collective-permute-start.1
  4.4 1.2 collective-permute-start.2
  5.6 2.7 %collective-permute-done.refs_1_ = bf16[128,1024]{1,0:T(8,128)(2,1)S(1)} collective-permute-done((bf16[128,1024]{1,0:T(8,128)(2,1)}, bf16[128,1024]{1,0:T(8,128)(2,1)S(1)}, u32[]{:S(2)}, u32[]{:S(2)}) %collective-permute-start) | collective-permute-done | bytes 262176 | tf_op jit(solution)/shard_map/ppermute | solution.py:60
  8.3 1.9 %collective-permute-start.3 = (bf16[128,512]{1,0:T(8,128)(2,1)S(1)}, bf16[128,512]{1,0:T(8,128)(2,1)S(1)}, u32[]{:S(2)}, u32[]{:S(2)}) collective-permute-start(bf16[128,512]{1,0:T(8,128)(2,1)S(1)} %slice.16), channel_id=1, source_target_pairs={{0,32},{16,48},{32,64},{48,80},{64,96},{80,112},{96,0},{112,16},{1... | collective-permute-start | bytes 393224 | tf_op jit(solution)/shard_map/ppermute | solution.py:63
  10.1 1.7 %collective-permute-start.4 = (bf16[128,512]{1,0:T(8,128)(2,1)S(1)}, bf16[128,512]{1,0:T(8,128)(2,1)S(1)}, u32[]{:S(2)}, u32[]{:S(2)}) collective-permute-start(bf16[128,512]{1,0:T(8,128)(2,1)S(1)} %slice.17), channel_id=1, source_target_pairs={{0,96},{16,112},{32,0},{48,16},{64,32},{80,48},{96,64},{112,80},{1... | collective-permute-start | bytes 393224 | tf_op jit(solution)/shard_map/ppermute | solution.py:64
  11.9 1.4 collective-permute-start.6
  14.2 2.6 %collective-permute-start.7 = (bf16[128,1024]{1,0:T(8,128)(2,1)S(1)}, bf16[128,1024]{1,0:T(8,128)(2,1)S(1)}, u32[]{:S(2)}, u32[]{:S(2)}) collective-permute-start(bf16[128,1024]{1,0:T(8,128)(2,1)S(1)} %constant_dynamic-update-slice_fusion.refs_4_), channel_id=1, source_target_pairs={{0,128},{16,144},{32,160},{48,176},{64,192},{80,208},{96,224},{112... | collective-permute-start | bytes 786440 | tf_op jit(solution)/shard_map/ppermute | solution.py:68
  16.7 4.0 %collective-permute-start.8 = (bf16[128,1024]{1,0:T(8,128)(2,1)}, bf16[128,1024]{1,0:T(8,128)(2,1)S(1)}, u32[]{:S(2)}, u32[]{:S(2)}) collective-permute-start(bf16[128,1024]{1,0:T(8,128)(2,1)} %refs_0_.5), channel_id=1, source_target_pairs={{0,16},{16,0},{32,48},{48,32},{64,80},{80,64},{96,112},{112,96},{1... | collective-permute-start | bytes 786440 | tf_op jit(solution)/shard_map/ppermute | solution.py:168
  20.8 0.9 copy-done.9
  21.8 1.3 shard_map.41.refs_9_
  23.0 4.4 %collective-permute-start.9 = (f32[2,1024]{1,0:T(2,128)S(1)}, f32[2,1024]{1,0:T(2,128)S(1)}, u32[]{:S(2)}, u32[]{:S(2)}) collective-permute-start(f32[2,1024]{1,0:T(2,128)S(1)} %shard_map.41.refs_9_), channel_id=1, source_target_pairs={{0,16},{16,0},{32,48},{48,32},{64,80},{80,64},{96,112},{112,96},{1... | collective-permute-start | bytes 24584 | tf_op jit(solution)/shard_map/ppermute | solution.py:170
  28.2 2.1 %shard_map.42 = (bf16[1024,1024]{1,0:T(8,128)(2,1)S(1)}, bf16[128,1024]{1,0:T(8,128)(2,1)}, f32[1,1024]{1,0:T(1,128)S(1)}, bf16[16,16,1024]{2,1,0:T(8,128)(2,1)}) custom-call(bf16[128,1024]{1,0:T(8,128)(2,1)S(1)} %copy-done.10, bf16[128,1024]{1,0:T(8,128)(2,1)S(1)} %collective-permute-done.refs_1_, bf16[128,1024]{1,0:T(8,128)(2,1)S(1)} %collective-permute-done.1.refs_2_, ...), custom_call_target="tpu_custom_call" | custom-call | flops 536870912 | bytes 5263360 | tf_op jit(solution)/shard_map/pallas_call | solution.py:40
  30.3 11.3 %all-to-all-start = ((bf16[16,16,1024]{2,1,0:T(8,128)(2,1)}), bf16[16,16,1024]{2,1,0:T(8,128)(2,1)S(1)}, u32[]{:S(2)}, u32[]{:S(2)}) async-start(bf16[16,16,1024]{2,1,0:T(8,128)(2,1)} %get-tuple-element.16), calls=%async_computation | async-start | bytes 1048576 | tf_op jit(solution)/shard_map/all_to_all | solution.py:187
  42.5 2.7 %collective-permute-start.11 = (bf16[128,1024]{1,0:T(8,128)(2,1)S(1)}, bf16[128,1024]{1,0:T(8,128)(2,1)S(1)}, u32[]{:S(2)}, u32[]{:S(2)}) collective-permute-start(bf16[128,1024]{1,0:T(8,128)(2,1)S(1)} %copy-done.11), channel_id=1, source_target_pairs={{0,96},{16,112},{32,0},{48,16},{64,32},{80,48},{96,64},{112,80},{1... | collective-permute-start | bytes 786440 | tf_op jit(solution)/shard_map/ppermute | solution.py:61
  45.5 5.7 %collective-permute-done.10.refs_1_ = bf16[128,1024]{1,0:T(8,128)(2,1)S(1)} collective-permute-done((bf16[128,1024]{1,0:T(8,128)(2,1)S(1)}, bf16[128,1024]{1,0:T(8,128)(2,1)S(1)}, u32[]{:S(2)}, u32[]{:S(2)}) %collective-permute-start.10) | collective-permute-done | bytes 262176 | tf_op jit(solution)/shard_map/ppermute | solution.py:60
  51.5 2.7 %collective-permute-start.14 = (bf16[128,512]{1,0:T(8,128)(2,1)S(1)}, bf16[128,512]{1,0:T(8,128)(2,1)S(1)}, u32[]{:S(2)}, u32[]{:S(2)}) collective-permute-start(bf16[128,512]{1,0:T(8,128)(2,1)S(1)} %slice.19), channel_id=1, source_target_pairs={{0,96},{16,112},{32,0},{48,16},{64,32},{80,48},{96,64},{112,80},{1... | collective-permute-start | bytes 393224 | tf_op jit(solution)/shard_map/ppermute | solution.py:64
  54.2 3.1 %collective-permute-done.12.refs_3_ = bf16[128,1024]{1,0:T(8,128)(2,1)S(1)} collective-permute-done((bf16[128,1024]{1,0:T(8,128)(2,1)S(1)}, bf16[128,1024]{1,0:T(8,128)(2,1)S(1)}, u32[]{:S(2)}, u32[]{:S(2)}) %collective-permute-start.12) | collective-permute-done | bytes 262176 | tf_op jit(solution)/shard_map/ppermute | solution.py:62
  57.3 1.5 collective-permute-start.15
  58.9 2.0 %collective-permute-start.18 = (bf16[128,1024]{1,0:T(8,128)(2,1)S(1)}, bf16[128,1024]{1,0:T(8,128)(2,1)S(1)}, u32[]{:S(2)}, u32[]{:S(2)}) collective-permute-start(bf16[128,1024]{1,0:T(8,128)(2,1)S(1)} %copy-done.11), channel_id=1, source_target_pairs={{0,16},{16,0},{32,48},{48,32},{64,80},{80,64},{96,112},{112,96},{1... | collective-permute-start | bytes 786440 | tf_op jit(solution)/shard_map/ppermute | solution.py:168
  60.9 3.4 %collective-permute-done.16.refs_6_ = bf16[128,1024]{1,0:T(8,128)(2,1)S(1)} collective-permute-done((bf16[128,1024]{1,0:T(8,128)(2,1)S(1)}, bf16[128,1024]{1,0:T(8,128)(2,1)S(1)}, u32[]{:S(2)}, u32[]{:S(2)}) %collective-permute-start.16) | collective-permute-done | bytes 262176 | tf_op jit(solution)/shard_map/ppermute | solution.py:66
  64.3 1.0 collective-permute-done.17.refs_7_
  65.3 1.3 shard_map.44.refs_9_
  66.6 2.4 %collective-permute-start.19 = (f32[2,1024]{1,0:T(2,128)S(1)}, f32[2,1024]{1,0:T(2,128)S(1)}, u32[]{:S(2)}, u32[]{:S(2)}) collective-permute-start(f32[2,1024]{1,0:T(2,128)S(1)} %shard_map.44.refs_9_), channel_id=1, source_target_pairs={{0,16},{16,0},{32,48},{48,32},{64,80},{80,64},{96,112},{112,96},{1... | collective-permute-start | bytes 24584 | tf_op jit(solution)/shard_map/ppermute | solution.py:170
  69.8 1.3 shard_map.45
  71.1 1.3 copy-done
  73.3 9.7 %all-to-all-start.3 = ((bf16[16,16,1024]{2,1,0:T(8,128)(2,1)}), bf16[16,16,1024]{2,1,0:T(8,128)(2,1)S(1)}, u32[]{:S(2)}, u32[]{:S(2)}) async-start(bf16[16,16,1024]{2,1,0:T(8,128)(2,1)} %copy-done.14), calls=%async_computation.3 | async-start | bytes 1048576 | tf_op jit(solution)/shard_map/all_to_all | solution.py:187
  83.8 14.2 %all-to-all-done.3.parts = bf16[16,16,1024]{2,1,0:T(8,128)(2,1)S(1)} async-done(((bf16[16,16,1024]{2,1,0:T(8,128)(2,1)}), bf16[16,16,1024]{2,1,0:T(8,128)(2,1)S(1)}, u32[]{:S(2)}, u32[]{:S(2)}) %all-to-all-start.3) | async-done | bytes 524320 | tf_op jit(solution)/shard_map/all_to_all | solution.py:187
  98.9 6.7 %all-to-all-start.1 = ((bf16[16,16,1024]{2,1,0:T(8,128)(2,1)}), bf16[16,16,1024]{2,1,0:T(8,128)(2,1)S(1)}, u32[]{:S(2)}, u32[]{:S(2)}) async-start(bf16[16,16,1024]{2,1,0:T(8,128)(2,1)} %copy-done.8), calls=%async_computation.1 | async-start | bytes 1048576 | tf_op jit(solution)/shard_map/all_to_all | solution.py:189
  105.6 1.0 copy-done.7
  107.5 13.2 %all-to-all-done.1 = bf16[16,16,1024]{2,1,0:T(8,128)(2,1)S(1)} async-done(((bf16[16,16,1024]{2,1,0:T(8,128)(2,1)}), bf16[16,16,1024]{2,1,0:T(8,128)(2,1)S(1)}, u32[]{:S(2)}, u32[]{:S(2)}) %all-to-all-start.1) | async-done | bytes 524320 | tf_op jit(solution)/shard_map/all_to_all | solution.py:189
  120.7 6.2 %all-to-all-start.4 = ((bf16[16,16,1024]{2,1,0:T(8,128)(2,1)}), bf16[16,16,1024]{2,1,0:T(8,128)(2,1)S(1)}, u32[]{:S(2)}, u32[]{:S(2)}) async-start(bf16[16,16,1024]{2,1,0:T(8,128)(2,1)} %copy-done.5), calls=%async_computation.4 | async-start | bytes 1048576 | tf_op jit(solution)/shard_map/all_to_all | solution.py:189
  127.0 1.6 copy-done.1
  128.5 1.5 shard_map.46
  130.8 1.4 collective-permute-start.20
  132.2 8.9 %all-to-all-done.4 = bf16[16,16,1024]{2,1,0:T(8,128)(2,1)S(1)} async-done(((bf16[16,16,1024]{2,1,0:T(8,128)(2,1)}), bf16[16,16,1024]{2,1,0:T(8,128)(2,1)S(1)}, u32[]{:S(2)}, u32[]{:S(2)}) %all-to-all-start.4) | async-done | bytes 524320 | tf_op jit(solution)/shard_map/all_to_all | solution.py:189
  141.1 1.5 shard_map.51
  142.6 3.5 %collective-permute-start.22 = (f32[128,1024]{1,0:T(8,128)}, f32[128,1024]{1,0:T(8,128)S(1)}, u32[]{:S(2)}, u32[]{:S(2)}) collective-permute-start(f32[128,1024]{1,0:T(8,128)} %get-tuple-element.26), channel_id=1, source_target_pairs={{0,16},{16,0},{32,48},{48,32},{64,80},{80,64},{96,112},{112,96},{1... | collective-permute-start | bytes 1572872 | tf_op jit(solution)/shard_map/ppermute | solution.py:200
  146.5 1.2 collective-permute-done.21.diag_sib
  147.7 2.0 %shard_map.48 = (f32[128,1024]{1,0:T(8,128)S(1)}, f32[16,2,1024]{2,1,0:T(2,128)}) custom-call(f32[128,1024]{1,0:T(8,128)S(1)} %copy-done.13, f32[128,1024]{1,0:T(8,128)} %collective-permute-done.20.recv, bf16[1024,1024]{1,0:T(8,128)(2,1)S(1)} %get-tuple-element.20.b.normed_other.normed.normed_self, bf16[1024,1024]{1,0:T(8,128)(2,1)S(1)} %copy-done.2, ...), custom_call_target="tpu_custom_call" | custom-call | bytes 5906432 | tf_op jit(solution)/shard_map/pallas_call | solution.py:40
  150.4 3.7 %all-to-all-start.2 = ((f32[16,2,1024]{2,1,0:T(2,128)}), f32[16,2,1024]{2,1,0:T(2,128)S(1)}, u32[]{:S(2)}, u32[]{:S(2)}) async-start(f32[16,2,1024]{2,1,0:T(2,128)} %get-tuple-element.22), calls=%async_computation.2 | async-start | bytes 262144 | tf_op jit(solution)/shard_map/all_to_all | solution.py:213
  154.1 1.6 copy-done.3
  157.4 2.9 %all-to-all-done.2.sums = f32[16,2,1024]{2,1,0:T(2,128)S(1)} async-done(((f32[16,2,1024]{2,1,0:T(2,128)}), f32[16,2,1024]{2,1,0:T(2,128)S(1)}, u32[]{:S(2)}, u32[]{:S(2)}) %all-to-all-start.2) | async-done | bytes 131104 | tf_op jit(solution)/shard_map/all_to_all | solution.py:213
  160.3 4.0 %all-to-all-start.5 = ((f32[16,2,1024]{2,1,0:T(2,128)}), f32[16,2,1024]{2,1,0:T(2,128)S(1)}, u32[]{:S(2)}, u32[]{:S(2)}) async-start(f32[16,2,1024]{2,1,0:T(2,128)} %get-tuple-element.28), calls=%async_computation.5 | async-start | bytes 262144 | tf_op jit(solution)/shard_map/all_to_all | solution.py:213
  164.3 1.6 copy-done.4
  165.9 1.0 copy-done.16
  167.7 2.8 %all-to-all-done.5.sums = f32[16,2,1024]{2,1,0:T(2,128)S(1)} async-done(((f32[16,2,1024]{2,1,0:T(2,128)}), f32[16,2,1024]{2,1,0:T(2,128)S(1)}, u32[]{:S(2)}, u32[]{:S(2)}) %all-to-all-start.5) | async-done | bytes 131104 | tf_op jit(solution)/shard_map/all_to_all | solution.py:213
  170.5 1.0 copy-done.18
  (69 shorter events, 12.9 us)
Async XLA Ops:
  0.6 27.6 %copy-start.10 = (bf16[128,1024]{1,0:T(8,128)(2,1)S(1)}, bf16[128,1024]{1,0:T(8,128)(2,1)}, u32[]{:S(2)}) copy-start(bf16[128,1024]{1,0:T(8,128)(2,1)} %refs_0_.5) | copy-start | bytes 786436
  0.6 7.6 %collective-permute-start = (bf16[128,1024]{1,0:T(8,128)(2,1)}, bf16[128,1024]{1,0:T(8,128)(2,1)S(1)}, u32[]{:S(2)}, u32[]{:S(2)}) collective-permute-start(bf16[128,1024]{1,0:T(8,128)(2,1)} %refs_0_.5), channel_id=1, source_target_pairs={{0,32},{16,48},{32,64},{48,80},{64,96},{80,112},{96,0},{112,16},{1... | collective-permute-start | bytes 786440 | tf_op jit(solution)/shard_map/ppermute | solution.py:60
  2.8 7.3 %collective-permute-start.1 = (bf16[128,1024]{1,0:T(8,128)(2,1)}, bf16[128,1024]{1,0:T(8,128)(2,1)S(1)}, u32[]{:S(2)}, u32[]{:S(2)}) collective-permute-start(bf16[128,1024]{1,0:T(8,128)(2,1)} %refs_0_.5), channel_id=1, source_target_pairs={{0,96},{16,112},{32,0},{48,16},{64,32},{80,48},{96,64},{112,80},{1... | collective-permute-start | bytes 786440 | tf_op jit(solution)/shard_map/ppermute | solution.py:61
  4.4 7.5 %collective-permute-start.2 = (bf16[128,1024]{1,0:T(8,128)(2,1)}, bf16[128,1024]{1,0:T(8,128)(2,1)S(1)}, u32[]{:S(2)}, u32[]{:S(2)}) collective-permute-start(bf16[128,1024]{1,0:T(8,128)(2,1)} %refs_0_.5), channel_id=1, source_target_pairs={{0,128},{16,144},{32,160},{48,176},{64,192},{80,208},{96,224},{112... | collective-permute-start | bytes 786440 | tf_op jit(solution)/shard_map/ppermute | solution.py:62
  8.3 5.8 %collective-permute-start.3 = (bf16[128,512]{1,0:T(8,128)(2,1)S(1)}, bf16[128,512]{1,0:T(8,128)(2,1)S(1)}, u32[]{:S(2)}, u32[]{:S(2)}) collective-permute-start(bf16[128,512]{1,0:T(8,128)(2,1)S(1)} %slice.16), channel_id=1, source_target_pairs={{0,32},{16,48},{32,64},{48,80},{64,96},{80,112},{96,0},{112,16},{1... | collective-permute-start | bytes 393224 | tf_op jit(solution)/shard_map/ppermute | solution.py:63
  10.1 4.0 %collective-permute-start.4 = (bf16[128,512]{1,0:T(8,128)(2,1)S(1)}, bf16[128,512]{1,0:T(8,128)(2,1)S(1)}, u32[]{:S(2)}, u32[]{:S(2)}) collective-permute-start(bf16[128,512]{1,0:T(8,128)(2,1)S(1)} %slice.17), channel_id=1, source_target_pairs={{0,96},{16,112},{32,0},{48,16},{64,32},{80,48},{96,64},{112,80},{1... | collective-permute-start | bytes 393224 | tf_op jit(solution)/shard_map/ppermute | solution.py:64
  11.9 8.8 %collective-permute-start.6 = (bf16[128,1024]{1,0:T(8,128)(2,1)S(1)}, bf16[128,1024]{1,0:T(8,128)(2,1)S(1)}, u32[]{:S(2)}, u32[]{:S(2)}) collective-permute-start(bf16[128,1024]{1,0:T(8,128)(2,1)S(1)} %collective-permute-done.2.refs_3_), channel_id=1, source_target_pairs={{0,96},{16,112},{32,0},{48,16},{64,32},{80,48},{96,64},{112,80},{1... | collective-permute-start | bytes 786440 | tf_op jit(solution)/shard_map/ppermute | solution.py:66
  13.3 7.4 %collective-permute-start.5 = (bf16[128,1024]{1,0:T(8,128)(2,1)S(1)}, bf16[128,1024]{1,0:T(8,128)(2,1)S(1)}, u32[]{:S(2)}, u32[]{:S(2)}) collective-permute-start(bf16[128,1024]{1,0:T(8,128)(2,1)S(1)} %collective-permute-done.2.refs_3_), channel_id=1, source_target_pairs={{0,32},{16,48},{32,64},{48,80},{64,96},{80,112},{96,0},{112,16},{1... | collective-permute-start | bytes 786440 | tf_op jit(solution)/shard_map/ppermute | solution.py:65
  14.2 6.6 %collective-permute-start.7 = (bf16[128,1024]{1,0:T(8,128)(2,1)S(1)}, bf16[128,1024]{1,0:T(8,128)(2,1)S(1)}, u32[]{:S(2)}, u32[]{:S(2)}) collective-permute-start(bf16[128,1024]{1,0:T(8,128)(2,1)S(1)} %constant_dynamic-update-slice_fusion.refs_4_), channel_id=1, source_target_pairs={{0,128},{16,144},{32,160},{48,176},{64,192},{80,208},{96,224},{112... | collective-permute-start | bytes 786440 | tf_op jit(solution)/shard_map/ppermute | solution.py:68
  16.7 10.6 %collective-permute-start.8 = (bf16[128,1024]{1,0:T(8,128)(2,1)}, bf16[128,1024]{1,0:T(8,128)(2,1)S(1)}, u32[]{:S(2)}, u32[]{:S(2)}) collective-permute-start(bf16[128,1024]{1,0:T(8,128)(2,1)} %refs_0_.5), channel_id=1, source_target_pairs={{0,16},{16,0},{32,48},{48,32},{64,80},{80,64},{96,112},{112,96},{1... | collective-permute-start | bytes 786440 | tf_op jit(solution)/shard_map/ppermute | solution.py:168
  20.8 1.0 copy-start.9
  23.0 18.6 %copy-start.11 = (bf16[128,1024]{1,0:T(8,128)(2,1)S(1)}, bf16[128,1024]{1,0:T(8,128)(2,1)}, u32[]{:S(2)}) copy-start(bf16[128,1024]{1,0:T(8,128)(2,1)} %refs_0_.7) | copy-start | bytes 786436
  23.0 5.2 %collective-permute-start.9 = (f32[2,1024]{1,0:T(2,128)S(1)}, f32[2,1024]{1,0:T(2,128)S(1)}, u32[]{:S(2)}, u32[]{:S(2)}) collective-permute-start(f32[2,1024]{1,0:T(2,128)S(1)} %shard_map.41.refs_9_), channel_id=1, source_target_pairs={{0,16},{16,0},{32,48},{48,32},{64,80},{80,64},{96,112},{112,96},{1... | collective-permute-start | bytes 24584 | tf_op jit(solution)/shard_map/ppermute | solution.py:170
  30.3 43.0 %all-to-all-start = ((bf16[16,16,1024]{2,1,0:T(8,128)(2,1)}), bf16[16,16,1024]{2,1,0:T(8,128)(2,1)S(1)}, u32[]{:S(2)}, u32[]{:S(2)}) async-start(bf16[16,16,1024]{2,1,0:T(8,128)(2,1)} %get-tuple-element.16), calls=%async_computation | async-start | bytes 1048576 | tf_op jit(solution)/shard_map/all_to_all | solution.py:187
  41.6 9.6 %collective-permute-start.10 = (bf16[128,1024]{1,0:T(8,128)(2,1)S(1)}, bf16[128,1024]{1,0:T(8,128)(2,1)S(1)}, u32[]{:S(2)}, u32[]{:S(2)}) collective-permute-start(bf16[128,1024]{1,0:T(8,128)(2,1)S(1)} %copy-done.11), channel_id=1, source_target_pairs={{0,32},{16,48},{32,64},{48,80},{64,96},{80,112},{96,0},{112,16},{1... | collective-permute-start | bytes 786440 | tf_op jit(solution)/shard_map/ppermute | solution.py:60
  42.5 8.9 %collective-permute-start.11 = (bf16[128,1024]{1,0:T(8,128)(2,1)S(1)}, bf16[128,1024]{1,0:T(8,128)(2,1)S(1)}, u32[]{:S(2)}, u32[]{:S(2)}) collective-permute-start(bf16[128,1024]{1,0:T(8,128)(2,1)S(1)} %copy-done.11), channel_id=1, source_target_pairs={{0,96},{16,112},{32,0},{48,16},{64,32},{80,48},{96,64},{112,80},{1... | collective-permute-start | bytes 786440 | tf_op jit(solution)/shard_map/ppermute | solution.py:61
  45.2 12.1 %collective-permute-start.12 = (bf16[128,1024]{1,0:T(8,128)(2,1)S(1)}, bf16[128,1024]{1,0:T(8,128)(2,1)S(1)}, u32[]{:S(2)}, u32[]{:S(2)}) collective-permute-start(bf16[128,1024]{1,0:T(8,128)(2,1)S(1)} %copy-done.11), channel_id=1, source_target_pairs={{0,128},{16,144},{32,160},{48,176},{64,192},{80,208},{96,224},{112... | collective-permute-start | bytes 786440 | tf_op jit(solution)/shard_map/ppermute | solution.py:62
  51.2 7.6 %collective-permute-start.13 = (bf16[128,512]{1,0:T(8,128)(2,1)S(1)}, bf16[128,512]{1,0:T(8,128)(2,1)S(1)}, u32[]{:S(2)}, u32[]{:S(2)}) collective-permute-start(bf16[128,512]{1,0:T(8,128)(2,1)S(1)} %slice.18), channel_id=1, source_target_pairs={{0,32},{16,48},{32,64},{48,80},{64,96},{80,112},{96,0},{112,16},{1... | collective-permute-start | bytes 393224 | tf_op jit(solution)/shard_map/ppermute | solution.py:63
  51.5 7.3 %collective-permute-start.14 = (bf16[128,512]{1,0:T(8,128)(2,1)S(1)}, bf16[128,512]{1,0:T(8,128)(2,1)S(1)}, u32[]{:S(2)}, u32[]{:S(2)}) collective-permute-start(bf16[128,512]{1,0:T(8,128)(2,1)S(1)} %slice.19), channel_id=1, source_target_pairs={{0,96},{16,112},{32,0},{48,16},{64,32},{80,48},{96,64},{112,80},{1... | collective-permute-start | bytes 393224 | tf_op jit(solution)/shard_map/ppermute | solution.py:64
  57.3 7.0 %collective-permute-start.16 = (bf16[128,1024]{1,0:T(8,128)(2,1)S(1)}, bf16[128,1024]{1,0:T(8,128)(2,1)S(1)}, u32[]{:S(2)}, u32[]{:S(2)}) collective-permute-start(bf16[128,1024]{1,0:T(8,128)(2,1)S(1)} %collective-permute-done.12.refs_3_), channel_id=1, source_target_pairs={{0,96},{16,112},{32,0},{48,16},{64,32},{80,48},{96,64},{112,80},{1... | collective-permute-start | bytes 786440 | tf_op jit(solution)/shard_map/ppermute | solution.py:66
  57.3 7.0 %collective-permute-start.15 = (bf16[128,1024]{1,0:T(8,128)(2,1)S(1)}, bf16[128,1024]{1,0:T(8,128)(2,1)S(1)}, u32[]{:S(2)}, u32[]{:S(2)}) collective-permute-start(bf16[128,1024]{1,0:T(8,128)(2,1)S(1)} %collective-permute-done.12.refs_3_), channel_id=1, source_target_pairs={{0,32},{16,48},{32,64},{48,80},{64,96},{80,112},{96,0},{112,16},{1... | collective-permute-start | bytes 786440 | tf_op jit(solution)/shard_map/ppermute | solution.py:65
  58.8 6.5 %collective-permute-start.17 = (bf16[128,1024]{1,0:T(8,128)(2,1)S(1)}, bf16[128,1024]{1,0:T(8,128)(2,1)S(1)}, u32[]{:S(2)}, u32[]{:S(2)}) collective-permute-start(bf16[128,1024]{1,0:T(8,128)(2,1)S(1)} %constant_dynamic-update-slice_fusion.2.refs_4_), channel_id=1, source_target_pairs={{0,128},{16,144},{32,160},{48,176},{64,192},{80,208},{96,224},{112... | collective-permute-start | bytes 786440 | tf_op jit(solution)/shard_map/ppermute | solution.py:68
  58.9 10.1 %collective-permute-start.18 = (bf16[128,1024]{1,0:T(8,128)(2,1)S(1)}, bf16[128,1024]{1,0:T(8,128)(2,1)S(1)}, u32[]{:S(2)}, u32[]{:S(2)}) collective-permute-start(bf16[128,1024]{1,0:T(8,128)(2,1)S(1)} %copy-done.11), channel_id=1, source_target_pairs={{0,16},{16,0},{32,48},{48,32},{64,80},{80,64},{96,112},{112,96},{1... | collective-permute-start | bytes 786440 | tf_op jit(solution)/shard_map/ppermute | solution.py:168
  66.6 3.2 %collective-permute-start.19 = (f32[2,1024]{1,0:T(2,128)S(1)}, f32[2,1024]{1,0:T(2,128)S(1)}, u32[]{:S(2)}, u32[]{:S(2)}) collective-permute-start(f32[2,1024]{1,0:T(2,128)S(1)} %shard_map.44.refs_9_), channel_id=1, source_target_pairs={{0,16},{16,0},{32,48},{48,32},{64,80},{80,64},{96,112},{112,96},{1... | collective-permute-start | bytes 24584 | tf_op jit(solution)/shard_map/ppermute | solution.py:170
  71.1 1.4 copy-start
  72.5 0.8 copy-start.14
  73.3 24.8 %all-to-all-start.3 = ((bf16[16,16,1024]{2,1,0:T(8,128)(2,1)}), bf16[16,16,1024]{2,1,0:T(8,128)(2,1)S(1)}, u32[]{:S(2)}, u32[]{:S(2)}) async-start(bf16[16,16,1024]{2,1,0:T(8,128)(2,1)} %copy-done.14), calls=%async_computation.3 | async-start | bytes 1048576 | tf_op jit(solution)/shard_map/all_to_all | solution.py:187
  83.0 0.8 copy-start.8
  98.1 0.8 copy-start.6
  98.9 21.9 %all-to-all-start.1 = ((bf16[16,16,1024]{2,1,0:T(8,128)(2,1)}), bf16[16,16,1024]{2,1,0:T(8,128)(2,1)S(1)}, u32[]{:S(2)}, u32[]{:S(2)}) async-start(bf16[16,16,1024]{2,1,0:T(8,128)(2,1)} %copy-done.8), calls=%async_computation.1 | async-start | bytes 1048576 | tf_op jit(solution)/shard_map/all_to_all | solution.py:189
  105.6 1.0 copy-start.7
  106.7 0.8 copy-start.5
  120.7 20.4 %all-to-all-start.4 = ((bf16[16,16,1024]{2,1,0:T(8,128)(2,1)}), bf16[16,16,1024]{2,1,0:T(8,128)(2,1)S(1)}, u32[]{:S(2)}, u32[]{:S(2)}) async-start(bf16[16,16,1024]{2,1,0:T(8,128)(2,1)} %copy-done.5), calls=%async_computation.4 | async-start | bytes 1048576 | tf_op jit(solution)/shard_map/all_to_all | solution.py:189
  126.9 1.6 copy-start.1
  130.0 0.8 copy-start.12
  130.8 16.8 %collective-permute-start.20 = (f32[128,1024]{1,0:T(8,128)}, f32[128,1024]{1,0:T(8,128)}, u32[]{:S(2)}, u32[]{:S(2)}) collective-permute-start(f32[128,1024]{1,0:T(8,128)} %get-tuple-element.19), channel_id=1, source_target_pairs={{0,16},{16,0},{32,48},{48,32},{64,80},{80,64},{96,112},{112,96},{1... | collective-permute-start | bytes 1572872 | tf_op jit(solution)/shard_map/ppermute | solution.py:200
  141.1 5.0 %copy-start.2 = (bf16[1024,1024]{1,0:T(8,128)(2,1)S(1)}, bf16[1024,1024]{1,0:T(8,128)(2,1)}, u32[]{:S(2)}) copy-start(bf16[1024,1024]{1,0:T(8,128)(2,1)} %copy-done) | copy-start | bytes 6291460
  142.6 5.0 %copy-start.13 = (f32[128,1024]{1,0:T(8,128)S(1)}, f32[128,1024]{1,0:T(8,128)}, u32[]{:S(2)}) copy-start(f32[128,1024]{1,0:T(8,128)} %copy-done.12) | copy-start | bytes 1572868
  142.6 11.5 %collective-permute-start.22 = (f32[128,1024]{1,0:T(8,128)}, f32[128,1024]{1,0:T(8,128)S(1)}, u32[]{:S(2)}, u32[]{:S(2)}) collective-permute-start(f32[128,1024]{1,0:T(8,128)} %get-tuple-element.26), channel_id=1, source_target_pairs={{0,16},{16,0},{32,48},{48,32},{64,80},{80,64},{96,112},{112,96},{1... | collective-permute-start | bytes 1572872 | tf_op jit(solution)/shard_map/ppermute | solution.py:200
  146.3 1.3 collective-permute-start.21
  149.6 0.8 copy-start.15
  150.4 9.9 %all-to-all-start.2 = ((f32[16,2,1024]{2,1,0:T(2,128)}), f32[16,2,1024]{2,1,0:T(2,128)S(1)}, u32[]{:S(2)}, u32[]{:S(2)}) async-start(f32[16,2,1024]{2,1,0:T(2,128)} %get-tuple-element.22), calls=%async_computation.2 | async-start | bytes 262144 | tf_op jit(solution)/shard_map/all_to_all | solution.py:213
  154.1 1.6 copy-start.3
  156.6 0.8 copy-start.17
  160.3 10.2 %all-to-all-start.5 = ((f32[16,2,1024]{2,1,0:T(2,128)}), f32[16,2,1024]{2,1,0:T(2,128)S(1)}, u32[]{:S(2)}, u32[]{:S(2)}) async-start(f32[16,2,1024]{2,1,0:T(2,128)} %get-tuple-element.28), calls=%async_computation.5 | async-start | bytes 262144 | tf_op jit(solution)/shard_map/all_to_all | solution.py:213
  164.3 1.6 copy-start.4
  165.9 1.0 copy-start.16
  170.5 1.0 copy-start.18

commit v2 on v1

v2 whole, which is shorter than its diff:
```python
import functools

import jax
import jax.numpy as jnp
from jax import lax
from jax.experimental import pallas as pl
from jax.experimental.pallas import tpu as pltpu
from jax.sharding import PartitionSpec as P

off_weight = 0.0051
epsilon = 1e-05
f32 = jnp.float32
bf16 = jnp.bfloat16

X_LO, Y, CORES = 2, 4, 2


def dp_perm(move):
    def index(x, y, c):
        return (x * Y + y) * CORES + c

    return [
        (index(x, y, c), index(*move(x, y, c)))
        for x in range(X_LO)
        for y in range(Y)
        for c in range(CORES)
    ]


TO_CORE = dp_perm(lambda x, y, c: (x, y, 1 - c))
TO_X = dp_perm(lambda x, y, c: (1 - x, y, c))
TO_UP = dp_perm(lambda x, y, c: (x, (y + 1) % Y, c))
TO_DOWN = dp_perm(lambda x, y, c: (x, (y - 1) % Y, c))


def call(body, outs, *args, flops=0):
    def size(s):
        return s.size * s.dtype.itemsize

    return pl.pallas_call(
        body,
        out_shape=outs,
        in_specs=[pl.BlockSpec(memory_space=pltpu.VMEM)] * len(args),
        out_specs=jax.tree.map(lambda _: pl.BlockSpec(memory_space=pltpu.VMEM), outs),
        compiler_params=pltpu.CompilerParams(vmem_limit_bytes=24 * 2**20),
        cost_estimate=pl.CostEstimate(
            flops=flops,
            bytes_accessed=sum(size(a) for a in args) + sum(size(o) for o in jax.tree.leaves(outs)),
            transcendentals=0,
        ),
    )(*args)


def shape(*dims, dtype=f32):
    return jax.ShapeDtypeStruct(dims, dtype)


def gather_chips(view):
    half = view.shape[1] // 2
    from_down = lax.ppermute(view, "dp", TO_UP)
    from_up = lax.ppermute(view, "dp", TO_DOWN)
    from_x = lax.ppermute(view, "dp", TO_X)
    far_left = lax.ppermute(from_down[:, :half], "dp", TO_UP)
    far_right = lax.ppermute(from_up[:, half:], "dp", TO_DOWN)
    x_down = lax.ppermute(from_x, "dp", TO_UP)
    x_up = lax.ppermute(from_x, "dp", TO_DOWN)
    far = jnp.concatenate([far_left, far_right], 1)
    x_far = lax.ppermute(far, "dp", TO_X)
    return [view, from_down, from_up, from_x, far, x_down, x_up, x_far]


def moments_body(*refs):
    pieces, out = refs[:-1], refs[-1]
    for v in range(2):
        view = pieces[v * len(pieces) // 2 : (v + 1) * len(pieces) // 2]
        count = sum(p.shape[0] for p in view)
        total = sum(jnp.sum(p[...].astype(f32), 0, keepdims=True) for p in view)
        mean = total / count
        square = 0.0
        for p in view:
            centered = p[...].astype(f32) - mean
            square = square + jnp.sum(centered * centered, 0, keepdims=True)
        out[2 * v : 2 * v + 1, :] = mean
        out[2 * v + 1 : 2 * v + 2, :] = square


def gram_body(batch, *refs):
    *pieces, own_m, sib_m, normed_a, normed_b, spread_out, diag, gram = refs
    rows = pieces[0].shape[0]
    groups, part = gram.shape[0], gram.shape[2]
    nt = (((1,), (1,)), ((), ()))
    for v, normed in enumerate((normed_a, normed_b)):
        view = pieces[v * len(pieces) // 2 : (v + 1) * len(pieces) // 2]
        m, q = slice(2 * v, 2 * v + 1), slice(2 * v + 1, 2 * v + 2)
        mean = 0.5 * (own_m[m, :] + sib_m[m, :])
        gap = own_m[m, :] - sib_m[m, :]
        square = own_m[q, :] + sib_m[q, :] + gap * gap * (batch / 4)
        spread = jnp.sqrt(square / batch + epsilon)
        spread_out[v : v + 1, :] = spread
        for i, p in enumerate(view):
            normed[i * rows : (i + 1) * rows, :] = ((p[...].astype(f32) - mean) / spread).astype(bf16)
        sib = normed[len(view) * rows - rows :, :]
        for i in range(len(view) - 1):
            block = normed[i * rows : (i + 1) * rows, :]
            top = lax.dot_general(normed[0:rows, :], block, nt, preferred_element_type=f32)
            low = lax.dot_general(sib, block, nt, preferred_element_type=f32)
            c = slice(i * rows, (i + 1) * rows)
            gram[0 : groups // 2, v, :, c] = top.astype(bf16).reshape(groups // 2, part, rows)
            gram[groups // 2 :, v, :, c] = low.astype(bf16).reshape(groups // 2, part, rows)
    total = 0.0
    for i in range(len(pieces) // 2 - 1):
        c = slice(i * rows, (i + 1) * rows)
        total = total + jnp.sum(
            normed_a[c, :].astype(f32) * normed_b[c, :].astype(f32), 0, keepdims=True
        )
    diag[...] = total


def reduce_body(parts, out):
    total = parts[0].astype(f32)
    for i in range(1, parts.shape[0]):
        total = total + parts[i].astype(f32)
    total = total.astype(bf16)
    for i in range(out.shape[0]):
        out[i] = total


def apply_body(scale, gram, normed_a, normed_b, own, other):
    groups = gram.shape[0]
    half, rows = gram.shape[3], own.shape[1]
    for v, normed in enumerate((normed_b, normed_a)):
        for part, out in enumerate((own, other)):
            block = gram[part * groups // 2 : (part + 1) * groups // 2, v].reshape(rows, half)
            out[v] = scale * jnp.dot(block, normed[0:half, :], preferred_element_type=f32)


def upward_body(batch, own, recv, normed_a, normed_b, diag_own, diag_sib, up_out, sums):
    rows = own.shape[1]
    corr = (diag_own[...] + diag_sib[...]) / batch
    diag = 2.0 * (corr - 1.0) - 2.0 * off_weight * corr
    for v, (other, same) in enumerate(((normed_a, normed_b), (normed_b, normed_a))):
        up = own[v] + recv[v] + other[0:rows, :].astype(f32) * diag
        up_out[v] = up
        first = jnp.sum(up, 0, keepdims=True)
        second = jnp.sum(up * same[0:rows, :].astype(f32), 0, keepdims=True)
        for i in range(sums.shape[0]):
            sums[i, 2 * v : 2 * v + 1, :] = first
            sums[i, 2 * v + 1 : 2 * v + 2, :] = second


def final_body(batch, up, normed_a, normed_b, sums, spread, grad_a, grad_b):
    rows = up.shape[1]
    total = sums[0]
    for i in range(1, sums.shape[0]):
        total = total + sums[i]
    total = total / batch
    for v, (same, out) in enumerate(((normed_b, grad_b), (normed_a, grad_a))):
        normal = same[0:rows, :].astype(f32)
        first, second = total[2 * v : 2 * v + 1, :], total[2 * v + 1 : 2 * v + 2, :]
        divisor = spread[1 - v : 2 - v, :]
        out[...] = ((up[v] - first - normal * second) / divisor).astype(bf16)


def on_device(view_a, view_b):
    rows, cols = view_a.shape
    dp_count = lax.axis_size("dp")
    feat_count = lax.axis_size("feat")
    batch = rows * dp_count
    half = batch // CORES
    part = CORES * rows // feat_count
    scale = 2.0 * off_weight / batch
    work = 2 * 2 * CORES * rows * half * cols

    pieces_a, pieces_b = gather_chips(view_a), gather_chips(view_b)
    sib_a = lax.ppermute(view_a, "dp", TO_CORE)
    sib_b = lax.ppermute(view_b, "dp", TO_CORE)
    moments = call(moments_body, shape(4, cols), *pieces_a, *pieces_b)
    moments_sib = lax.ppermute(moments, "dp", TO_CORE)
    normed_a, normed_b, spread, diag, gram = call(
        functools.partial(gram_body, batch),
        (
            shape(half + rows, cols, dtype=bf16),
            shape(half + rows, cols, dtype=bf16),
            shape(2, cols),
            shape(1, cols),
            shape(feat_count, 2, part, half, dtype=bf16),
        ),
        *pieces_a,
        sib_a,
        *pieces_b,
        sib_b,
        moments,
        moments_sib,
        flops=work,
    )
    diag_sib = lax.ppermute(diag, "dp", TO_CORE)
    parts = lax.all_to_all(gram, "feat", 0, 0)
    total = call(reduce_body, shape(feat_count, 2, part, half, dtype=bf16), parts)
    whole = lax.all_to_all(total, "feat", 0, 0)
    own, other = call(
        functools.partial(apply_body, scale),
        (shape(2, rows, cols), shape(2, rows, cols)),
        whole,
        normed_a,
        normed_b,
        flops=work,
    )
    recv = lax.ppermute(other, "dp", TO_CORE)
    up, sums = call(
        functools.partial(upward_body, batch),
        (shape(2, rows, cols), shape(dp_count, 4, cols)),
        own,
        recv,
        normed_a,
        normed_b,
        diag,
        diag_sib,
    )
    sums = lax.all_to_all(sums, "dp", 0, 0)
    return call(
        functools.partial(final_body, batch),
        (shape(rows, cols, dtype=bf16), shape(rows, cols, dtype=bf16)),
        up,
        normed_a,
        normed_b,
        sums,
        spread,
    )


def solution(mesh):
    spec = P("dp", "feat")
    return jax.shard_map(
        on_device, mesh=mesh, in_specs=(spec, spec), out_specs=(spec, spec), check_vma=False
    )
```

time: 173 us -> 139 us (0.80)
  blocking collectives: 0 us -> 81.9 us
  waiting for transfers between devices: 61.6 us -> 10.3 us
  starting transfers between devices: 80.2 us -> 35.7 us
  local copies, waits for them, and re-layouts: 15.8 us -> 1.97 us
  Pallas kernels: 13.9 us -> 7.8 us
    all_to_all x0 -> x3, blocking collectives: none -> 81.9 us  [the longest x1 37 us: on_device(): parts = lax.all_to_all(gram, 'feat', 0, 0)]
    all_to_all x6 -> x0, waiting for transfers between devices: 42 us -> none  [the longest x2 22.1 us: reduce(): whole = lax.all_to_all(total, 'feat', 0, 0)]
    all_to_all x6 -> x0, starting transfers between devices: 41.5 us -> none  [the longest x2 20.9 us: reduce(): parts = lax.all_to_all(gram, 'feat', 0, 0)]
    unnamed x40 -> x6, local copies, waits for them, and re-layouts: 15.8 us -> 1.91 us
    pallas_call x13 -> x6, Pallas kernels: 13.9 us -> 7.8 us  [call(): pl.pallas_call(body, out_shape=outs, in_specs=[pl.BlockSpec(memory_space=...]
    ppermute x6 -> x4, starting transfers between devices: 17.5 us -> 12.7 us  [the longest x1 4.77 us: on_device(): sib_a = lax.ppermute(view_a, 'dp', TO_CORE)]
    ppermute x2, waiting for transfers between devices: 8.35 us -> 3.8 us  [gather_chips(): from_down = lax.ppermute(view, 'dp', TO_UP)]
    ppermute x2, waiting for transfers between devices: 3.09 us -> 0.01 us  [gather_chips(): from_x = lax.ppermute(view, 'dp', TO_X)]
  transfers between devices with their start and end apart: 29 -> 21, of which waited for: 15 -> 6; matrix products, arithmetic and copies ran while one was open for 0% -> 0% of each run, Pallas kernels for 6% -> 2%
where the time goes in v2:
time: 139 us; the launch traced here: 138 us
  blocking collectives  81.9 us (59%)
  starting transfers between devices  35.7 us (26%)
  waiting for transfers between devices  10.3 us (7%)
  Pallas kernels  7.8 us (6%)
  local copies, waits for them, and re-layouts  1.97 us (1%)
    all_to_all x1, blocking collectives, on_device(): parts = lax.all_to_all(gram, 'feat', 0, 0)  37 us
    all_to_all x1, blocking collectives, on_device(): whole = lax.all_to_all(total, 'feat', 0, 0)  32.9 us
    all_to_all x1, blocking collectives, on_device(): sums = lax.all_to_all(sums, 'dp', 0, 0)  11.9 us
    pallas_call x6, Pallas kernels, call(): pl.pallas_call(body, out_shape=outs, in_specs=[pl.BlockSpec(memory_space=...  7.8 us
    ppermute x1, starting transfers between devices, on_device(): sib_a = lax.ppermute(view_a, 'dp', TO_CORE)  4.77 us
    ppermute x2, starting transfers between devices, gather_chips(): from_x = lax.ppermute(view, 'dp', TO_X)  4.45 us
    ppermute x2, starting transfers between devices, gather_chips(): x_up = lax.ppermute(from_x, 'dp', TO_DOWN)  4.39 us
    ppermute x2, waiting for transfers between devices, gather_chips(): from_down = lax.ppermute(view, 'dp', TO_UP)  3.8 us
  transfers between devices with their start and end apart: 21, of which 6 were waited for; matrix products, arithmetic and copies ran while one was open for 0% of the time, Pallas kernels for 2%

profile of v2, /device:TPU:1, one launch (start us, length us, event | category | flops | bytes accessed | tf_op | source)
XLA Modules:
  0.0 138.4 jit_solution(17935234335154800277)
XLA Ops:
  0.6 2.2 %collective-permute-start = (bf16[128,1024]{1,0:T(8,128)(2,1)}, bf16[128,1024]{1,0:T(8,128)(2,1)S(1)}, u32[]{:S(2)}, u32[]{:S(2)}) collective-permute-start(bf16[128,1024]{1,0:T(8,128)(2,1)} %refs_0_.3), channel_id=1, source_target_pairs={{0,32},{16,48},{32,64},{48,80},{64,96},{80,112},{96,0},{112,16},{1... | collective-permute-start | bytes 786440 | tf_op jit(solution)/shard_map/ppermute | solution.py:60
  2.8 1.3 collective-permute-start.9
  4.1 1.4 collective-permute-start.1
  5.5 0.3 collective-permute-start.10
  5.8 1.2 collective-permute-start.2
  7.0 1.2 collective-permute-done.refs_1_
  8.2 3.2 %collective-permute-start.11 = (bf16[128,1024]{1,0:T(8,128)(2,1)}, bf16[128,1024]{1,0:T(8,128)(2,1)S(1)}, u32[]{:S(2)}, u32[]{:S(2)}) collective-permute-start(bf16[128,1024]{1,0:T(8,128)(2,1)} %refs_9_.1), channel_id=1, source_target_pairs={{0,128},{16,144},{32,160},{48,176},{64,192},{80,208},{96,224},{112... | collective-permute-start | bytes 786440 | tf_op jit(solution)/shard_map/ppermute | solution.py:62
  11.5 2.6 %collective-permute-done.9.refs_9_.refs_10_ = bf16[128,1024]{1,0:T(8,128)(2,1)S(1)} collective-permute-done((bf16[128,1024]{1,0:T(8,128)(2,1)}, bf16[128,1024]{1,0:T(8,128)(2,1)S(1)}, u32[]{:S(2)}, u32[]{:S(2)}) %collective-permute-start.9) | collective-permute-done | bytes 262176 | tf_op jit(solution)/shard_map/ppermute | solution.py:60
  14.1 1.6 %collective-permute-start.3 = (bf16[128,512]{1,0:T(8,128)(2,1)S(1)}, bf16[128,512]{1,0:T(8,128)(2,1)S(1)}, u32[]{:S(2)}, u32[]{:S(2)}) collective-permute-start(bf16[128,512]{1,0:T(8,128)(2,1)S(1)} %slice.16), channel_id=1, source_target_pairs={{0,32},{16,48},{32,64},{48,80},{64,96},{80,112},{96,0},{112,16},{1... | collective-permute-start | bytes 393224 | tf_op jit(solution)/shard_map/ppermute | solution.py:63
  15.7 0.0 collective-permute-done.1.refs_2_
  15.7 1.6 %collective-permute-start.12 = (bf16[128,512]{1,0:T(8,128)(2,1)S(1)}, bf16[128,512]{1,0:T(8,128)(2,1)S(1)}, u32[]{:S(2)}, u32[]{:S(2)}) collective-permute-start(bf16[128,512]{1,0:T(8,128)(2,1)S(1)} %slice.18), channel_id=1, source_target_pairs={{0,32},{16,48},{32,64},{48,80},{64,96},{80,112},{96,0},{112,16},{1... | collective-permute-start | bytes 393224 | tf_op jit(solution)/shard_map/ppermute | solution.py:63
  17.2 0.0 collective-permute-done.10.refs_10_.refs_11_
  17.3 1.6 %collective-permute-start.4 = (bf16[128,512]{1,0:T(8,128)(2,1)S(1)}, bf16[128,512]{1,0:T(8,128)(2,1)S(1)}, u32[]{:S(2)}, u32[]{:S(2)}) collective-permute-start(bf16[128,512]{1,0:T(8,128)(2,1)S(1)} %slice.17), channel_id=1, source_target_pairs={{0,96},{16,112},{32,0},{48,16},{64,32},{80,48},{96,64},{112,80},{1... | collective-permute-start | bytes 393224 | tf_op jit(solution)/shard_map/ppermute | solution.py:64
  18.9 0.0 collective-permute-done.2.refs_3_
  18.9 0.2 collective-permute-start.13
  19.1 0.6 collective-permute-done.3
  19.6 1.7 %collective-permute-start.6 = (bf16[128,1024]{1,0:T(8,128)(2,1)S(1)}, bf16[128,1024]{1,0:T(8,128)(2,1)S(1)}, u32[]{:S(2)}, u32[]{:S(2)}) collective-permute-start(bf16[128,1024]{1,0:T(8,128)(2,1)S(1)} %collective-permute-done.2.refs_3_), channel_id=1, source_target_pairs={{0,96},{16,112},{32,0},{48,16},{64,32},{80,48},{96,64},{112,80},{1... | collective-permute-start | bytes 786440 | tf_op jit(solution)/shard_map/ppermute | solution.py:66
  21.4 0.1 collective-permute-start.5
  21.5 2.7 %collective-permute-start.15 = (bf16[128,1024]{1,0:T(8,128)(2,1)S(1)}, bf16[128,1024]{1,0:T(8,128)(2,1)S(1)}, u32[]{:S(2)}, u32[]{:S(2)}) collective-permute-start(bf16[128,1024]{1,0:T(8,128)(2,1)S(1)} %collective-permute-done.11.refs_11_.refs_12_), channel_id=1, source_target_pairs={{0,96},{16,112},{32,0},{48,16},{64,32},{80,48},{96,64},{112,80},{1... | collective-permute-start | bytes 786440 | tf_op jit(solution)/shard_map/ppermute | solution.py:66
  24.2 0.1 collective-permute-start.14
  24.3 2.0 %collective-permute-start.7 = (bf16[128,1024]{1,0:T(8,128)(2,1)S(1)}, bf16[128,1024]{1,0:T(8,128)(2,1)S(1)}, u32[]{:S(2)}, u32[]{:S(2)}) collective-permute-start(bf16[128,1024]{1,0:T(8,128)(2,1)S(1)} %constant_dynamic-update-slice_fusion.refs_4_), channel_id=1, source_target_pairs={{0,128},{16,144},{32,160},{48,176},{64,192},{80,208},{96,224},{112... | collective-permute-start | bytes 786440 | tf_op jit(solution)/shard_map/ppermute | solution.py:68
  26.3 2.8 %collective-permute-done.6.refs_6_ = bf16[128,1024]{1,0:T(8,128)(2,1)S(1)} collective-permute-done((bf16[128,1024]{1,0:T(8,128)(2,1)S(1)}, bf16[128,1024]{1,0:T(8,128)(2,1)S(1)}, u32[]{:S(2)}, u32[]{:S(2)}) %collective-permute-start.6) | collective-permute-done | bytes 262176 | tf_op jit(solution)/shard_map/ppermute | solution.py:66
  29.2 1.7 %collective-permute-start.16 = (bf16[128,1024]{1,0:T(8,128)(2,1)S(1)}, bf16[128,1024]{1,0:T(8,128)(2,1)S(1)}, u32[]{:S(2)}, u32[]{:S(2)}) collective-permute-start(bf16[128,1024]{1,0:T(8,128)(2,1)S(1)} %constant_dynamic-update-slice_fusion.2.refs_12_.refs_13_), channel_id=1, source_target_pairs={{0,128},{16,144},{32,160},{48,176},{64,192},{80,208},{96,224},{112... | collective-permute-start | bytes 786440 | tf_op jit(solution)/shard_map/ppermute | solution.py:68
  30.9 0.0 collective-permute-done.5.refs_5_
  30.9 4.8 %collective-permute-start.8 = (bf16[128,1024]{1,0:T(8,128)(2,1)}, bf16[128,1024]{1,0:T(8,128)(2,1)S(1)}, u32[]{:S(2)}, u32[]{:S(2)}) collective-permute-start(bf16[128,1024]{1,0:T(8,128)(2,1)} %refs_0_.3), channel_id=1, source_target_pairs={{0,16},{16,0},{32,48},{48,32},{64,80},{80,64},{96,112},{112,96},{1... | collective-permute-start | bytes 786440 | tf_op jit(solution)/shard_map/ppermute | solution.py:175
  35.7 0.0 collective-permute-done.15.refs_14_.refs_15_
  35.7 1.8 %collective-permute-start.17 = (bf16[128,1024]{1,0:T(8,128)(2,1)}, bf16[128,1024]{1,0:T(8,128)(2,1)S(1)}, u32[]{:S(2)}, u32[]{:S(2)}) collective-permute-start(bf16[128,1024]{1,0:T(8,128)(2,1)} %refs_9_.1), channel_id=1, source_target_pairs={{0,16},{16,0},{32,48},{48,32},{64,80},{80,64},{96,112},{112,96},{1... | collective-permute-start | bytes 786440 | tf_op jit(solution)/shard_map/ppermute | solution.py:176
  37.5 0.0 collective-permute-done.14.refs_13_.refs_14_
  37.5 0.0 collective-permute-done.7.refs_7_
  37.5 0.0 collective-permute-done.16.refs_15_.refs_16_
  37.5 0.0 copy-start
  37.5 0.9 copy-done
  38.5 0.9 copy-done.1
  39.4 2.5 %shard_map.41.refs_18_ = f32[4,1024]{1,0:T(4,128)S(1)} custom-call(bf16[128,1024]{1,0:T(8,128)(2,1)S(1)} %copy-done, bf16[128,1024]{1,0:T(8,128)(2,1)S(1)} %collective-permute-done.refs_1_, bf16[128,1024]{1,0:T(8,128)(2,1)S(1)} %collective-permute-done.1.refs_2_, bf16[128,1024]{1,0:T(8,128)(2,1)S(1)} %collective-permute-done.2.refs_3_, ...), custom_call_target="tpu_custom_call" | custom-call | bytes 4210688 | tf_op jit(solution)/shard_map/pallas_call | solution.py:40
  41.9 3.2 %collective-permute-start.18 = (f32[4,1024]{1,0:T(4,128)S(1)}, f32[4,1024]{1,0:T(4,128)S(1)}, u32[]{:S(2)}, u32[]{:S(2)}) collective-permute-start(f32[4,1024]{1,0:T(4,128)S(1)} %shard_map.41.refs_18_), channel_id=1, source_target_pairs={{0,16},{16,0},{32,48},{48,32},{64,80},{80,64},{96,112},{112,96},{1... | collective-permute-start | bytes 49160 | tf_op jit(solution)/shard_map/ppermute | solution.py:178
  45.1 0.0 collective-permute-done.8.refs_8_
  45.1 0.8 collective-permute-done.18.refs_19_
  45.9 2.5 %shard_map.42 = (bf16[1152,1024]{1,0:T(8,128)(2,1)S(1)}, bf16[1152,1024]{1,0:T(8,128)(2,1)S(1)}, f32[2,1024]{1,0:T(2,128)S(1)}, f32[1,1024]{1,0:T(1,128)S(1)}, bf16[16,2,16,1024]{3,2,1,0:T(8,128)(2,1)S(1)}) custom-call(bf16[128,1024]{1,0:T(8,128)(2,1)S(1)} %copy-done, bf16[128,1024]{1,0:T(8,128)(2,1)S(1)} %collective-permute-done.refs_1_, ...), custom_call_target="tpu_custom_call" | custom-call | flops 1073741824 | bytes 10530816 | tf_op jit(solution)/shard_map/pallas_call | solution.py:40
  48.5 37.0 %all_to_all.15.parts = bf16[16,2,16,1024]{3,2,1,0:T(8,128)(2,1)S(1)} all-to-all(bf16[16,2,16,1024]{3,2,1,0:T(8,128)(2,1)S(1)} %get-tuple-element.11), channel_id=1, replica_groups=mesh['dp'=16,'feat'=16] {'feat'}, dimensions={0} | all-to-all | bytes 2097152 | tf_op jit(solution)/shard_map/all_to_all | solution.py:197
  85.5 0.2 shard_map.43
  85.7 32.9 %all_to_all.16.gram = bf16[16,2,16,1024]{3,2,1,0:T(8,128)(2,1)S(1)} all-to-all(bf16[16,2,16,1024]{3,2,1,0:T(8,128)(2,1)S(1)} %shard_map.43), channel_id=1, replica_groups=mesh['dp'=16,'feat'=16] {'feat'}, dimensions={0} | all-to-all | bytes 2097152 | tf_op jit(solution)/shard_map/all_to_all | solution.py:199
  118.6 1.3 shard_map.44
  119.9 2.9 %collective-permute-start.19 = (f32[2,128,1024]{2,1,0:T(8,128)S(1)}, f32[2,128,1024]{2,1,0:T(8,128)S(1)}, u32[]{:S(2)}, u32[]{:S(2)}) collective-permute-start(f32[2,128,1024]{2,1,0:T(8,128)S(1)} %get-tuple-element.15), channel_id=1, source_target_pairs={{0,16},{16,0},{32,48},{48,32},{64,80},{80,64},{96,112},{112,96},{1... | collective-permute-start | bytes 3145736 | tf_op jit(solution)/shard_map/ppermute | solution.py:208
  122.9 0.1 collective-permute-start.20
  123.0 2.2 %collective-permute-done.20.diag_sib = f32[1,1024]{1,0:T(1,128)S(1)} collective-permute-done((f32[1,1024]{1,0:T(1,128)S(1)}, f32[1,1024]{1,0:T(1,128)S(1)}, u32[]{:S(2)}, u32[]{:S(2)}) %collective-permute-start.20) | collective-permute-done | bytes 4128 | tf_op jit(solution)/shard_map/ppermute | solution.py:196
  125.2 0.4 shard_map.45
  125.5 11.9 %all_to_all.17.sums = f32[16,4,1024]{2,1,0:T(4,128)S(1)} all-to-all(f32[16,4,1024]{2,1,0:T(4,128)S(1)} %get-tuple-element.18), channel_id=1, replica_groups=mesh['dp'=16,'feat'=16] {'dp'}, dimensions={0} | all-to-all | bytes 524288 | tf_op jit(solution)/shard_map/all_to_all | solution.py:219
  137.4 0.9 shard_map.46
  (15 shorter events, 0.1 us)
Async XLA Ops:
  0.6 7.6 %collective-permute-start = (bf16[128,1024]{1,0:T(8,128)(2,1)}, bf16[128,1024]{1,0:T(8,128)(2,1)S(1)}, u32[]{:S(2)}, u32[]{:S(2)}) collective-permute-start(bf16[128,1024]{1,0:T(8,128)(2,1)} %refs_0_.3), channel_id=1, source_target_pairs={{0,32},{16,48},{32,64},{48,80},{64,96},{80,112},{96,0},{112,16},{1... | collective-permute-start | bytes 786440 | tf_op jit(solution)/shard_map/ppermute | solution.py:60
  2.8 11.3 %collective-permute-start.9 = (bf16[128,1024]{1,0:T(8,128)(2,1)}, bf16[128,1024]{1,0:T(8,128)(2,1)S(1)}, u32[]{:S(2)}, u32[]{:S(2)}) collective-permute-start(bf16[128,1024]{1,0:T(8,128)(2,1)} %refs_9_.1), channel_id=1, source_target_pairs={{0,32},{16,48},{32,64},{48,80},{64,96},{80,112},{96,0},{112,16},{1... | collective-permute-start | bytes 786440 | tf_op jit(solution)/shard_map/ppermute | solution.py:60
  4.1 11.5 %collective-permute-start.1 = (bf16[128,1024]{1,0:T(8,128)(2,1)}, bf16[128,1024]{1,0:T(8,128)(2,1)S(1)}, u32[]{:S(2)}, u32[]{:S(2)}) collective-permute-start(bf16[128,1024]{1,0:T(8,128)(2,1)} %refs_0_.3), channel_id=1, source_target_pairs={{0,96},{16,112},{32,0},{48,16},{64,32},{80,48},{96,64},{112,80},{1... | collective-permute-start | bytes 786440 | tf_op jit(solution)/shard_map/ppermute | solution.py:61
  5.5 11.7 %collective-permute-start.10 = (bf16[128,1024]{1,0:T(8,128)(2,1)}, bf16[128,1024]{1,0:T(8,128)(2,1)S(1)}, u32[]{:S(2)}, u32[]{:S(2)}) collective-permute-start(bf16[128,1024]{1,0:T(8,128)(2,1)} %refs_9_.1), channel_id=1, source_target_pairs={{0,96},{16,112},{32,0},{48,16},{64,32},{80,48},{96,64},{112,80},{1... | collective-permute-start | bytes 786440 | tf_op jit(solution)/shard_map/ppermute | solution.py:61
  5.8 13.0 %collective-permute-start.2 = (bf16[128,1024]{1,0:T(8,128)(2,1)}, bf16[128,1024]{1,0:T(8,128)(2,1)S(1)}, u32[]{:S(2)}, u32[]{:S(2)}) collective-permute-start(bf16[128,1024]{1,0:T(8,128)(2,1)} %refs_0_.3), channel_id=1, source_target_pairs={{0,128},{16,144},{32,160},{48,176},{64,192},{80,208},{96,224},{112... | collective-permute-start | bytes 786440 | tf_op jit(solution)/shard_map/ppermute | solution.py:62
  8.2 13.1 %collective-permute-start.11 = (bf16[128,1024]{1,0:T(8,128)(2,1)}, bf16[128,1024]{1,0:T(8,128)(2,1)S(1)}, u32[]{:S(2)}, u32[]{:S(2)}) collective-permute-start(bf16[128,1024]{1,0:T(8,128)(2,1)} %refs_9_.1), channel_id=1, source_target_pairs={{0,128},{16,144},{32,160},{48,176},{64,192},{80,208},{96,224},{112... | collective-permute-start | bytes 786440 | tf_op jit(solution)/shard_map/ppermute | solution.py:62
  14.1 5.5 %collective-permute-start.3 = (bf16[128,512]{1,0:T(8,128)(2,1)S(1)}, bf16[128,512]{1,0:T(8,128)(2,1)S(1)}, u32[]{:S(2)}, u32[]{:S(2)}) collective-permute-start(bf16[128,512]{1,0:T(8,128)(2,1)S(1)} %slice.16), channel_id=1, source_target_pairs={{0,32},{16,48},{32,64},{48,80},{64,96},{80,112},{96,0},{112,16},{1... | collective-permute-start | bytes 393224 | tf_op jit(solution)/shard_map/ppermute | solution.py:63
  15.7 5.8 %collective-permute-start.12 = (bf16[128,512]{1,0:T(8,128)(2,1)S(1)}, bf16[128,512]{1,0:T(8,128)(2,1)S(1)}, u32[]{:S(2)}, u32[]{:S(2)}) collective-permute-start(bf16[128,512]{1,0:T(8,128)(2,1)S(1)} %slice.18), channel_id=1, source_target_pairs={{0,32},{16,48},{32,64},{48,80},{64,96},{80,112},{96,0},{112,16},{1... | collective-permute-start | bytes 393224 | tf_op jit(solution)/shard_map/ppermute | solution.py:63
  17.3 6.9 %collective-permute-start.4 = (bf16[128,512]{1,0:T(8,128)(2,1)S(1)}, bf16[128,512]{1,0:T(8,128)(2,1)S(1)}, u32[]{:S(2)}, u32[]{:S(2)}) collective-permute-start(bf16[128,512]{1,0:T(8,128)(2,1)S(1)} %slice.17), channel_id=1, source_target_pairs={{0,96},{16,112},{32,0},{48,16},{64,32},{80,48},{96,64},{112,80},{1... | collective-permute-start | bytes 393224 | tf_op jit(solution)/shard_map/ppermute | solution.py:64
  18.9 5.4 %collective-permute-start.13 = (bf16[128,512]{1,0:T(8,128)(2,1)S(1)}, bf16[128,512]{1,0:T(8,128)(2,1)S(1)}, u32[]{:S(2)}, u32[]{:S(2)}) collective-permute-start(bf16[128,512]{1,0:T(8,128)(2,1)S(1)} %slice.19), channel_id=1, source_target_pairs={{0,96},{16,112},{32,0},{48,16},{64,32},{80,48},{96,64},{112,80},{1... | collective-permute-start | bytes 393224 | tf_op jit(solution)/shard_map/ppermute | solution.py:64
  19.6 9.5 %collective-permute-start.6 = (bf16[128,1024]{1,0:T(8,128)(2,1)S(1)}, bf16[128,1024]{1,0:T(8,128)(2,1)S(1)}, u32[]{:S(2)}, u32[]{:S(2)}) collective-permute-start(bf16[128,1024]{1,0:T(8,128)(2,1)S(1)} %collective-permute-done.2.refs_3_), channel_id=1, source_target_pairs={{0,96},{16,112},{32,0},{48,16},{64,32},{80,48},{96,64},{112,80},{1... | collective-permute-start | bytes 786440 | tf_op jit(solution)/shard_map/ppermute | solution.py:66
  21.4 9.5 %collective-permute-start.5 = (bf16[128,1024]{1,0:T(8,128)(2,1)S(1)}, bf16[128,1024]{1,0:T(8,128)(2,1)S(1)}, u32[]{:S(2)}, u32[]{:S(2)}) collective-permute-start(bf16[128,1024]{1,0:T(8,128)(2,1)S(1)} %collective-permute-done.2.refs_3_), channel_id=1, source_target_pairs={{0,32},{16,48},{32,64},{48,80},{64,96},{80,112},{96,0},{112,16},{1... | collective-permute-start | bytes 786440 | tf_op jit(solution)/shard_map/ppermute | solution.py:65
  21.5 14.2 %collective-permute-start.15 = (bf16[128,1024]{1,0:T(8,128)(2,1)S(1)}, bf16[128,1024]{1,0:T(8,128)(2,1)S(1)}, u32[]{:S(2)}, u32[]{:S(2)}) collective-permute-start(bf16[128,1024]{1,0:T(8,128)(2,1)S(1)} %collective-permute-done.11.refs_11_.refs_12_), channel_id=1, source_target_pairs={{0,96},{16,112},{32,0},{48,16},{64,32},{80,48},{96,64},{112,80},{1... | collective-permute-start | bytes 786440 | tf_op jit(solution)/shard_map/ppermute | solution.py:66
  24.2 13.4 %collective-permute-start.14 = (bf16[128,1024]{1,0:T(8,128)(2,1)S(1)}, bf16[128,1024]{1,0:T(8,128)(2,1)S(1)}, u32[]{:S(2)}, u32[]{:S(2)}) collective-permute-start(bf16[128,1024]{1,0:T(8,128)(2,1)S(1)} %collective-permute-done.11.refs_11_.refs_12_), channel_id=1, source_target_pairs={{0,32},{16,48},{32,64},{48,80},{64,96},{80,112},{96,0},{112,16},{1... | collective-permute-start | bytes 786440 | tf_op jit(solution)/shard_map/ppermute | solution.py:65
  24.3 13.2 %collective-permute-start.7 = (bf16[128,1024]{1,0:T(8,128)(2,1)S(1)}, bf16[128,1024]{1,0:T(8,128)(2,1)S(1)}, u32[]{:S(2)}, u32[]{:S(2)}) collective-permute-start(bf16[128,1024]{1,0:T(8,128)(2,1)S(1)} %constant_dynamic-update-slice_fusion.refs_4_), channel_id=1, source_target_pairs={{0,128},{16,144},{32,160},{48,176},{64,192},{80,208},{96,224},{112... | collective-permute-start | bytes 786440 | tf_op jit(solution)/shard_map/ppermute | solution.py:68
  29.2 8.4 %collective-permute-start.16 = (bf16[128,1024]{1,0:T(8,128)(2,1)S(1)}, bf16[128,1024]{1,0:T(8,128)(2,1)S(1)}, u32[]{:S(2)}, u32[]{:S(2)}) collective-permute-start(bf16[128,1024]{1,0:T(8,128)(2,1)S(1)} %constant_dynamic-update-slice_fusion.2.refs_12_.refs_13_), channel_id=1, source_target_pairs={{0,128},{16,144},{32,160},{48,176},{64,192},{80,208},{96,224},{112... | collective-permute-start | bytes 786440 | tf_op jit(solution)/shard_map/ppermute | solution.py:68
  30.9 14.2 %collective-permute-start.8 = (bf16[128,1024]{1,0:T(8,128)(2,1)}, bf16[128,1024]{1,0:T(8,128)(2,1)S(1)}, u32[]{:S(2)}, u32[]{:S(2)}) collective-permute-start(bf16[128,1024]{1,0:T(8,128)(2,1)} %refs_0_.3), channel_id=1, source_target_pairs={{0,16},{16,0},{32,48},{48,32},{64,80},{80,64},{96,112},{112,96},{1... | collective-permute-start | bytes 786440 | tf_op jit(solution)/shard_map/ppermute | solution.py:175
  35.7 9.4 %collective-permute-start.17 = (bf16[128,1024]{1,0:T(8,128)(2,1)}, bf16[128,1024]{1,0:T(8,128)(2,1)S(1)}, u32[]{:S(2)}, u32[]{:S(2)}) collective-permute-start(bf16[128,1024]{1,0:T(8,128)(2,1)} %refs_9_.1), channel_id=1, source_target_pairs={{0,16},{16,0},{32,48},{48,32},{64,80},{80,64},{96,112},{112,96},{1... | collective-permute-start | bytes 786440 | tf_op jit(solution)/shard_map/ppermute | solution.py:176
  37.5 1.0 copy-start
  38.5 0.9 copy-start.1
  41.9 4.0 %collective-permute-start.18 = (f32[4,1024]{1,0:T(4,128)S(1)}, f32[4,1024]{1,0:T(4,128)S(1)}, u32[]{:S(2)}, u32[]{:S(2)}) collective-permute-start(f32[4,1024]{1,0:T(4,128)S(1)} %shard_map.41.refs_18_), channel_id=1, source_target_pairs={{0,16},{16,0},{32,48},{48,32},{64,80},{80,64},{96,112},{112,96},{1... | collective-permute-start | bytes 49160 | tf_op jit(solution)/shard_map/ppermute | solution.py:178
  119.9 5.2 %collective-permute-start.19 = (f32[2,128,1024]{2,1,0:T(8,128)S(1)}, f32[2,128,1024]{2,1,0:T(8,128)S(1)}, u32[]{:S(2)}, u32[]{:S(2)}) collective-permute-start(f32[2,128,1024]{2,1,0:T(8,128)S(1)} %get-tuple-element.15), channel_id=1, source_target_pairs={{0,16},{16,0},{32,48},{48,32},{64,80},{80,64},{96,112},{112,96},{1... | collective-permute-start | bytes 3145736 | tf_op jit(solution)/shard_map/ppermute | solution.py:208
  122.9 2.3 %collective-permute-start.20 = (f32[1,1024]{1,0:T(1,128)S(1)}, f32[1,1024]{1,0:T(1,128)S(1)}, u32[]{:S(2)}, u32[]{:S(2)}) collective-permute-start(f32[1,1024]{1,0:T(1,128)S(1)} %get-tuple-element.16.diag_own), channel_id=1, source_target_pairs={{0,16},{16,0},{32,48},{48,32},{64,80},{80,64},{96,112},{112,96},{1... | collective-permute-start | bytes 12296 | tf_op jit(solution)/shard_map/ppermute | solution.py:196

commit v3 on v2

v3 whole, which is shorter than its diff:
```python
import functools

import jax
import jax.numpy as jnp
from jax import lax
from jax.experimental import pallas as pl
from jax.experimental.pallas import tpu as pltpu
from jax.sharding import PartitionSpec as P

off_weight = 0.0051
epsilon = 1e-05
f32 = jnp.float32
bf16 = jnp.bfloat16

X_LO, Y, CORES = 2, 4, 2


def dp_perm(move):
    def index(x, y, c):
        return (x * Y + y) * CORES + c

    return [
        (index(x, y, c), index(*move(x, y, c)))
        for x in range(X_LO)
        for y in range(Y)
        for c in range(CORES)
    ]


TO_CORE = dp_perm(lambda x, y, c: (x, y, 1 - c))
TO_X = dp_perm(lambda x, y, c: (1 - x, y, c))
TO_UP = dp_perm(lambda x, y, c: (x, (y + 1) % Y, c))
TO_DOWN = dp_perm(lambda x, y, c: (x, (y - 1) % Y, c))


X_HI, Z = 2, 8
TO_X_HI = [(q, (q + Z) % (X_HI * Z)) for q in range(X_HI * Z)]


def z_shift(step):
    return [(h * Z + z, h * Z + (z + step) % Z) for h in range(X_HI) for z in range(Z)]


def send(x, to, axis="dp"):
    return lax.ppermute(x, axis, to)


def call(body, outs, *args, flops=0, scratch=()):
    def size(s):
        return s.size * s.dtype.itemsize

    return pl.pallas_call(
        body,
        out_shape=outs,
        in_specs=[pl.BlockSpec(memory_space=pltpu.VMEM)] * len(args),
        scratch_shapes=scratch,
        out_specs=jax.tree.map(lambda _: pl.BlockSpec(memory_space=pltpu.VMEM), outs),
        compiler_params=pltpu.CompilerParams(vmem_limit_bytes=16 * 2**20),
        cost_estimate=pl.CostEstimate(
            flops=flops,
            bytes_accessed=sum(size(a) for a in args) + sum(size(o) for o in jax.tree.leaves(outs)),
            transcendentals=0,
        ),
    )(*args)


def shape(*dims, dtype=f32):
    return jax.ShapeDtypeStruct(dims, dtype)


def moments_of(pieces):
    count = sum(p.shape[0] for p in pieces)
    total = sum(jnp.sum(p[...].astype(f32), 0, keepdims=True) for p in pieces)
    mean = total / count
    square = 0.0
    for p in pieces:
        centered = p[...].astype(f32) - mean
        square = square + jnp.sum(centered * centered, 0, keepdims=True)
    return count, mean, square


def early_moments_body(*refs):
    *pairs, far_a, far_b, out = refs
    for v, far in enumerate((far_a, far_b)):
        _, mean, square = moments_of([p.at[v] for p in pairs] + [far])
        out[2 * v : 2 * v + 1, :] = mean
        out[2 * v + 1 : 2 * v + 2, :] = square


def late_moments_body(early_count, early, far, out):
    for v in range(2):
        late_count, late_mean, late_square = moments_of([far.at[v]])
        mean = early[2 * v : 2 * v + 1, :]
        gap = late_mean - mean
        count = early_count + late_count
        out[2 * v : 2 * v + 1, :] = mean + gap * (late_count / count)
        out[2 * v + 1 : 2 * v + 2, :] = (
            early[2 * v + 1 : 2 * v + 2, :]
            + late_square
            + gap * gap * (early_count * late_count / count)
        )


def gram_body(batch, own_m, sib_m, sib, *refs):
    pairs, fars, outs = refs[:6], refs[6:9], refs[9:]
    lead, normed, spread_out, diag, mine, up_2, down_2, up_1, down_1, far_a, far_b, gram = outs
    rows, part = sib.shape[1], mine.shape[2]
    for v in range(2):
        m, q = slice(2 * v, 2 * v + 1), slice(2 * v + 1, 2 * v + 2)
        mean = 0.5 * (own_m[m, :] + sib_m[m, :])
        gap = own_m[m, :] - sib_m[m, :]
        square = own_m[q, :] + sib_m[q, :] + gap * gap * (batch / 4)
        spread = jnp.sqrt(square / batch + epsilon)
        spread_out[v : v + 1, :] = spread
        pieces = [p.at[v] for p in pairs] + [fars[v], fars[2].at[v]]
        for i, p in enumerate((pieces[0], sib.at[v])):
            r = slice(i * rows, (i + 1) * rows)
            lead[v, r, :] = ((p[...].astype(f32) - mean) / spread).astype(bf16)
        for i, p in enumerate(pieces):
            r = slice(i * rows, (i + 1) * rows)
            normed[v, r, :] = ((p[...].astype(f32) - mean) / spread).astype(bf16)
            block = lax.dot_general(
                lead[v], normed[v, r, :], (((1,), (1,)), ((), ())), preferred_element_type=f32
            )
            gram[v, :, r] = block.astype(bf16)
    z = lax.rem(lax.axis_index("feat"), Z)

    def store(ahead, v, out):
        start = lax.rem(z + ahead, Z) * part
        for h in range(X_HI):
            out[h] = gram[v, pl.ds(pl.multiple_of(start + h * rows, part), part), :]

    for v in range(2):
        store(0, v, mine.at[v])
        store(2, v, up_2.at[v])
        store(6, v, down_2.at[v])
        for i, (up, down) in enumerate(((3, 5), (1, 7))):
            store(up, v, up_1.at[i, v])
            store(down, v, down_1.at[i, v])
        store(4, v, (far_a, far_b)[v])
    total = 0.0
    for i in range(normed.shape[1] // rows):
        r = slice(i * rows, (i + 1) * rows)
        total = total + jnp.sum(
            normed[0, r, :].astype(f32) * normed[1, r, :].astype(f32), 0, keepdims=True
        )
    diag[...] = total


def fold_body(far_up, far_down, half_a, half_b, up_2, down_2, up_out, down_out):
    def plus(x, y, *z):
        total = x.astype(f32) + y.astype(f32)
        return (total + z[0].astype(f32) if z else total).astype(bf16)

    up_out[0] = plus(up_2[0], far_up[0, 0], half_a[...])
    up_out[1] = plus(up_2[1], far_up[0, 1])
    down_out[0] = plus(down_2[0], far_down[0, 0])
    down_out[1] = plus(down_2[1], far_down[0, 1], half_b[...])


def total_body(mine, near_up, near_down, far_up, far_down, out):
    total = mine[...].astype(f32) + near_up[1].astype(f32) + near_down[1].astype(f32)
    out[...] = (total + far_up[...].astype(f32) + far_down[...].astype(f32)).astype(bf16)


def add_body(a, b, out):
    out[...] = (a[...].astype(f32) + b[...].astype(f32)).astype(bf16)


def reduce_rows(mine, up_2, down_2, up_1, down_1, far_a, far_b):
    z = "feat"
    half_a = send(far_a, z_shift(2), z)
    half_b = send(far_b, z_shift(-2), z)
    from_down, from_up = send(up_1, z_shift(1), z), send(down_1, z_shift(-1), z)
    block = jax.ShapeDtypeStruct(mine.shape, bf16)
    up_2, down_2 = call(
        fold_body, (block, block), from_down, from_up, half_a, half_b, up_2, down_2
    )
    far_down, far_up = send(up_2, z_shift(2), z), send(down_2, z_shift(-2), z)
    total = call(total_body, block, mine, from_down, from_up, far_down, far_up)
    return call(add_body, block, total, send(total, TO_X_HI, z))


def spread_rows(block):
    z = "feat"
    from_1 = send(block, z_shift(1), z)
    from_7 = send(block, z_shift(-1), z)
    from_2 = send(block, z_shift(2), z)
    from_6 = send(block, z_shift(-2), z)
    from_3 = send(from_2, z_shift(1), z)
    from_5 = send(from_6, z_shift(-1), z)
    from_4a = send(from_2[0], z_shift(2), z)
    from_4b = send(from_6[1], z_shift(-2), z)
    return [block, from_1, from_2, from_3, from_5, from_6, from_7, from_4a, from_4b]


def apply_body(batch, scale, *refs):
    *blocks, from_4a, from_4b, normed, lead, diag_own, diag_sib, own, other, sums, gram = refs
    rows, part = own.shape[1], blocks[0].shape[2]
    z = lax.rem(lax.axis_index("feat"), Z)

    def load(back, v, block):
        start = lax.rem(z + Z - back, Z) * part
        for h in range(X_HI):
            gram[v, pl.ds(pl.multiple_of(start + h * rows, part), part), :] = block[h]

    for v in range(2):
        for back, block in zip((0, 1, 2, 3, 5, 6, 7), blocks):
            load(back, v, block.at[v])
        load(4, v, (from_4a, from_4b)[v])
    corr = (diag_own[...] + diag_sib[...]) / batch
    diag = 2.0 * (corr - 1.0) - 2.0 * off_weight * corr
    for v in range(2):
        first = second = 0.0
        for h, out in enumerate((own, other)):
            r = slice(h * rows, (h + 1) * rows)
            up = scale * jnp.dot(gram[1 - v, r, :], normed[v], preferred_element_type=f32)
            if h == 0:
                up = up + lead[1 - v, r, :].astype(f32) * diag
            out[v] = up
            first = first + jnp.sum(up, 0, keepdims=True)
            second = second + jnp.sum(up * lead[v, r, :].astype(f32), 0, keepdims=True)
        for i in range(sums.shape[0]):
            sums[i, 2 * v : 2 * v + 1, :] = first
            sums[i, 2 * v + 1 : 2 * v + 2, :] = second


def final_body(batch, own, recv, lead, sums, spread, grad_a, grad_b):
    rows = own.shape[1]
    total = sums[0]
    for i in range(1, sums.shape[0]):
        total = total + sums[i]
    total = total / batch
    for v, out in enumerate((grad_a, grad_b)):
        normal = lead[v, 0:rows, :].astype(f32)
        first, second = total[2 * v : 2 * v + 1, :], total[2 * v + 1 : 2 * v + 2, :]
        up = own[v] + recv[v]
        out[...] = ((up - first - normal * second) / spread[v : v + 1, :]).astype(bf16)


def on_device(view_a, view_b):
    rows, cols = view_a.shape
    dp_count = lax.axis_size("dp")
    feat_count = lax.axis_size("feat")
    batch = rows * dp_count
    half = batch // CORES
    part = CORES * rows // feat_count
    scale = 2.0 * off_weight / batch
    work = 2 * 2 * CORES * rows * half * cols

    views = jnp.stack([view_a, view_b])
    from_down, from_up, from_x = send(views, TO_UP), send(views, TO_DOWN), send(views, TO_X)
    sib = send(views, TO_CORE)
    far_a, far_b = send(from_down[0], TO_UP), send(from_up[1], TO_DOWN)
    x_down, x_up = send(from_x, TO_UP), send(from_x, TO_DOWN)
    x_far = send(jnp.stack([far_a, far_b]), TO_X)
    pairs = [views, from_down, from_up, from_x, x_down, x_up]
    early = call(early_moments_body, shape(4, cols), *pairs, far_a, far_b)
    moments = call(
        functools.partial(late_moments_body, half - rows), shape(4, cols), early, x_far
    )
    one = shape(X_HI, part, half, dtype=bf16)
    both = shape(2, *one.shape, dtype=bf16)
    four = shape(2, *both.shape, dtype=bf16)
    lead, normed, spread, diag, *chunks = call(
        functools.partial(gram_body, batch),
        (
            shape(2, CORES * rows, cols, dtype=bf16),
            shape(2, half, cols, dtype=bf16),
            shape(2, cols),
            shape(1, cols),
            both,
            both,
            both,
            four,
            four,
            one,
            one,
        ),
        moments,
        send(moments, TO_CORE),
        sib,
        *pairs,
        far_a,
        far_b,
        x_far,
        flops=work,
        scratch=[pltpu.VMEM((2, CORES * rows, half), bf16)],
    )
    diag_sib = send(diag, TO_CORE)
    blocks = spread_rows(reduce_rows(*chunks))
    own, other, sums = call(
        functools.partial(apply_body, batch, scale),
        (shape(2, rows, cols), shape(2, rows, cols), shape(dp_count, 4, cols)),
        *blocks,
        normed,
        lead,
        diag,
        diag_sib,
        flops=work,
        scratch=[pltpu.VMEM((2, CORES * rows, half), bf16)],
    )
    sums = lax.all_to_all(sums, "dp", 0, 0)
    return call(
        functools.partial(final_body, batch),
        (shape(rows, cols, dtype=bf16), shape(rows, cols, dtype=bf16)),
        own,
        send(other, TO_CORE),
        lead,
        sums,
        spread,
    )


def solution(mesh):
    spec = P("dp", "feat")
    return jax.shard_map(
        on_device, mesh=mesh, in_specs=(spec, spec), out_specs=(spec, spec), check_vma=False
    )
```

time: 139 us -> 117 us (0.84)
  blocking collectives: 81.9 us -> 9.82 us
  waiting for transfers between devices: 10.3 us -> 43.7 us
  starting transfers between devices: 35.7 us -> 53.7 us
  local copies, waits for them, and re-layouts: 1.97 us -> 0.05 us
    all_to_all x2 -> x0, blocking collectives: 70 us -> none  [the longest x1 37 us: on_device(): parts = lax.all_to_all(gram, 'feat', 0, 0)]
    ppermute x21 -> x27, waiting for transfers between devices: 10.3 us -> 43.7 us  [send(): return lax.ppermute(x, axis, to)]
    ppermute x21 -> x27, starting transfers between devices: 35.7 us -> 53.7 us  [send(): return lax.ppermute(x, axis, to)]
    all_to_all x1, blocking collectives: 11.9 us -> 9.82 us  [on_device(): sums = lax.all_to_all(sums, 'dp', 0, 0)]
    unnamed x6 -> x0, local copies, waits for them, and re-layouts: 1.91 us -> none
    pallas_call x6 -> x8, Pallas kernels: 7.8 us -> 7.95 us  [call(): pl.pallas_call(body, out_shape=outs, in_specs=[pl.BlockSpec(memory_space=...]
  transfers between devices with their start and end apart: 21 -> 27, of which waited for: 6 -> 12; matrix products, arithmetic and copies ran while one was open for 0% -> 0% of each run, Pallas kernels for 2% -> 2%
where the time goes in v3:
time: 117 us
  starting transfers between devices  53.7 us (46%)
  waiting for transfers between devices  43.7 us (37%)
  blocking collectives  9.82 us (8%)
  Pallas kernels  7.95 us (7%)
    ppermute x27, starting transfers between devices, send(): return lax.ppermute(x, axis, to)  53.7 us
    ppermute x27, waiting for transfers between devices, send(): return lax.ppermute(x, axis, to)  43.7 us
    all_to_all x1, blocking collectives, on_device(): sums = lax.all_to_all(sums, 'dp', 0, 0)  9.82 us
    pallas_call x8, Pallas kernels, call(): pl.pallas_call(body, out_shape=outs, in_specs=[pl.BlockSpec(memory_space=...  7.95 us
  transfers between devices with their start and end apart: 27, of which 12 were waited for; matrix products, arithmetic and copies ran while one was open for 0% of the time, Pallas kernels for 2%

profile of v3, /device:TPU:1, one launch (start us, length us, event | category | flops | bytes accessed | tf_op | source)
XLA Modules:
  0.0 117.0 jit_solution(16646361302690388454)
XLA Ops:
  0.6 1.1 pad_maximum_fusion.refs_0_
  1.7 3.6 %collective-permute-start.1 = (bf16[2,128,1024]{2,1,0:T(8,128)(2,1)S(1)}, bf16[2,128,1024]{2,1,0:T(8,128)(2,1)S(1)}, u32[]{:S(2)}, u32[]{:S(2)}) collective-permute-start(bf16[2,128,1024]{2,1,0:T(8,128)(2,1)S(1)} %pad_maximum_fusion.refs_0_), channel_id=1, source_target_pairs={{0,96},{16,112},{32,0},{48,16},{64,32},{80,48},{96,64},{112,80},{1... | collective-permute-start | bytes 1572872 | tf_op jit(solution)/shard_map/ppermute | solution.py:45
  5.4 1.2 %collective-permute-start.2 = (bf16[2,128,1024]{2,1,0:T(8,128)(2,1)S(1)}, bf16[2,128,1024]{2,1,0:T(8,128)(2,1)S(1)}, u32[]{:S(2)}, u32[]{:S(2)}) collective-permute-start(bf16[2,128,1024]{2,1,0:T(8,128)(2,1)S(1)} %pad_maximum_fusion.refs_0_), channel_id=1, source_target_pairs={{0,128},{16,144},{32,160},{48,176},{64,192},{80,208},{96,224},{112... | collective-permute-start | bytes 1572872 | tf_op jit(solution)/shard_map/ppermute | solution.py:45
  6.6 9.4 %collective-permute-done.1.refs_2_ = bf16[2,128,1024]{2,1,0:T(8,128)(2,1)S(1)} collective-permute-done((bf16[2,128,1024]{2,1,0:T(8,128)(2,1)S(1)}, bf16[2,128,1024]{2,1,0:T(8,128)(2,1)S(1)}, u32[]{:S(2)}, u32[]{:S(2)}) %collective-permute-start.1) | collective-permute-done | bytes 524320 | tf_op jit(solution)/shard_map/ppermute | solution.py:45
  16.0 3.5 %collective-permute-start.6 = (bf16[128,1024]{1,0:T(8,128)(2,1)S(1)}, bf16[128,1024]{1,0:T(8,128)(2,1)S(1)}, u32[]{:S(2)}, u32[]{:S(2)}) collective-permute-start(bf16[128,1024]{1,0:T(8,128)(2,1)S(1)} %slice_bitcast_fusion), channel_id=1, source_target_pairs={{0,96},{16,112},{32,0},{48,16},{64,32},{80,48},{96,64},{112,80},{1... | collective-permute-start | bytes 786440 | tf_op jit(solution)/shard_map/ppermute | solution.py:45
  19.5 0.0 collective-permute-done.refs_1_
  19.5 0.1 collective-permute-start.5
  19.6 0.0 collective-permute-done.2.refs_3_
  19.6 2.7 %collective-permute-start.4 = (bf16[2,128,1024]{2,1,0:T(8,128)(2,1)S(1)}, bf16[2,128,1024]{2,1,0:T(8,128)(2,1)S(1)}, u32[]{:S(2)}, u32[]{:S(2)}) collective-permute-start(bf16[2,128,1024]{2,1,0:T(8,128)(2,1)S(1)} %collective-permute-done.2.refs_3_), channel_id=1, source_target_pairs={{0,96},{16,112},{32,0},{48,16},{64,32},{80,48},{96,64},{112,80},{1... | collective-permute-start | bytes 1572872 | tf_op jit(solution)/shard_map/ppermute | solution.py:45
  22.2 0.0 collective-permute-start.3
  22.2 1.3 %collective-permute-done.6.refs_7_ = bf16[128,1024]{1,0:T(8,128)(2,1)S(1)} collective-permute-done((bf16[128,1024]{1,0:T(8,128)(2,1)S(1)}, bf16[128,1024]{1,0:T(8,128)(2,1)S(1)}, u32[]{:S(2)}, u32[]{:S(2)}) %collective-permute-start.6) | collective-permute-done | bytes 262176 | tf_op jit(solution)/shard_map/ppermute | solution.py:45
  23.5 3.2 %collective-permute-done.5.refs_6_ = bf16[128,1024]{1,0:T(8,128)(2,1)S(1)} collective-permute-done((bf16[128,1024]{1,0:T(8,128)(2,1)S(1)}, bf16[128,1024]{1,0:T(8,128)(2,1)S(1)}, u32[]{:S(2)}, u32[]{:S(2)}) %collective-permute-start.5) | collective-permute-done | bytes 262176 | tf_op jit(solution)/shard_map/ppermute | solution.py:45
  26.7 0.1 pad_maximum_fusion.1
  26.8 1.3 %collective-permute-start.7 = (bf16[2,128,1024]{2,1,0:T(8,128)(2,1)S(1)}, bf16[2,128,1024]{2,1,0:T(8,128)(2,1)S(1)}, u32[]{:S(2)}, u32[]{:S(2)}) collective-permute-start(bf16[2,128,1024]{2,1,0:T(8,128)(2,1)S(1)} %pad_maximum_fusion.1), channel_id=1, source_target_pairs={{0,128},{16,144},{32,160},{48,176},{64,192},{80,208},{96,224},{112... | collective-permute-start | bytes 1572872 | tf_op jit(solution)/shard_map/ppermute | solution.py:45
  28.1 5.4 %collective-permute-start.9 = (bf16[2,128,1024]{2,1,0:T(8,128)(2,1)S(1)}, bf16[2,128,1024]{2,1,0:T(8,128)(2,1)S(1)}, u32[]{:S(2)}, u32[]{:S(2)}) collective-permute-start(bf16[2,128,1024]{2,1,0:T(8,128)(2,1)S(1)} %pad_maximum_fusion.refs_0_), channel_id=1, source_target_pairs={{0,16},{16,0},{32,48},{48,32},{64,80},{80,64},{96,112},{112,96},{1... | collective-permute-start | bytes 1572872 | tf_op jit(solution)/shard_map/ppermute | solution.py:45
  33.5 1.3 %collective-permute-done.4.refs_5_ = bf16[2,128,1024]{2,1,0:T(8,128)(2,1)S(1)} collective-permute-done((bf16[2,128,1024]{2,1,0:T(8,128)(2,1)S(1)}, bf16[2,128,1024]{2,1,0:T(8,128)(2,1)S(1)}, u32[]{:S(2)}, u32[]{:S(2)}) %collective-permute-start.4) | collective-permute-done | bytes 524320 | tf_op jit(solution)/shard_map/ppermute | solution.py:45
  34.7 3.2 %collective-permute-done.3.refs_4_ = bf16[2,128,1024]{2,1,0:T(8,128)(2,1)S(1)} collective-permute-done((bf16[2,128,1024]{2,1,0:T(8,128)(2,1)S(1)}, bf16[2,128,1024]{2,1,0:T(8,128)(2,1)S(1)}, u32[]{:S(2)}, u32[]{:S(2)}) %collective-permute-start.3) | collective-permute-done | bytes 524320 | tf_op jit(solution)/shard_map/ppermute | solution.py:45
  38.0 2.2 %shard_map.41.early = f32[4,1024]{1,0:T(4,128)S(1)} custom-call(bf16[2,128,1024]{2,1,0:T(8,128)(2,1)S(1)} %pad_maximum_fusion.refs_0_, bf16[2,128,1024]{2,1,0:T(8,128)(2,1)S(1)} %collective-permute-done.refs_1_, bf16[2,128,1024]{2,1,0:T(8,128)(2,1)S(1)} %collective-permute-done.1.refs_2_, bf16[2,128,1024]{2,1,0:T(8,128)(2,1)S(1)} %collective-permute-done.2.refs_3_, ...), custom_call_target="tpu_custom_call" | custom-call | bytes 3686400 | tf_op jit(solution)/shard_map/pallas_call | solution.py:52
  40.2 0.3 shard_map.42.own_m
  40.5 3.0 %collective-permute-start.8 = (f32[4,1024]{1,0:T(4,128)S(1)}, f32[4,1024]{1,0:T(4,128)S(1)}, u32[]{:S(2)}, u32[]{:S(2)}) collective-permute-start(f32[4,1024]{1,0:T(4,128)S(1)} %shard_map.42.own_m), channel_id=1, source_target_pairs={{0,16},{16,0},{32,48},{48,32},{64,80},{80,64},{96,112},{112,96},{1... | collective-permute-start | bytes 49160 | tf_op jit(solution)/shard_map/ppermute | solution.py:45
  43.5 0.8 collective-permute-done.8.sib_m
  44.4 2.6 %shard_map.43 = (bf16[2,256,1024]{2,1,0:T(8,128)(2,1)S(1)}, bf16[2,1024,1024]{2,1,0:T(8,128)(2,1)S(1)}, f32[2,1024]{1,0:T(2,128)S(1)}, f32[1,1024]{1,0:T(1,128)S...) custom-call(f32[4,1024]{1,0:T(4,128)S(1)} %shard_map.42.own_m, ...), custom_call_target="tpu_custom_call" | custom-call | flops 1073741824 | bytes 11055104 | tf_op jit(solution)/shard_map/pallas_call | solution.py:52
  46.9 1.7 %collective-permute-start.10 = (bf16[2,2,2,16,1024]{4,3,2,1,0:T(8,128)(2,1)S(1)}, bf16[2,2,2,16,1024]{4,3,2,1,0:T(8,128)(2,1)S(1)}, u32[]{:S(2)}, u32[]{:S(2)}) collective-permute-start(bf16[2,2,2,16,1024]{4,3,2,1,0:T(8,128)(2,1)S(1)} %get-tuple-element.19), channel_id=1, source_target_pairs={{0,1},{1,2},{2,3},{3,4},{4,5},{5,6},{6,7},{7,0},{8,9},{9,10},{10,1... | collective-permute-start | bytes 786440 | tf_op jit(solution)/shard_map/ppermute | solution.py:45
  48.7 4.0 %collective-permute-start.11 = (bf16[2,2,2,16,1024]{4,3,2,1,0:T(8,128)(2,1)S(1)}, bf16[2,2,2,16,1024]{4,3,2,1,0:T(8,128)(2,1)S(1)}, u32[]{:S(2)}, u32[]{:S(2)}) collective-permute-start(bf16[2,2,2,16,1024]{4,3,2,1,0:T(8,128)(2,1)S(1)} %get-tuple-element.20), channel_id=1, source_target_pairs={{0,7},{1,0},{2,1},{3,2},{4,3},{5,4},{6,5},{7,6},{8,15},{9,8},{10,9... | collective-permute-start | bytes 786440 | tf_op jit(solution)/shard_map/ppermute | solution.py:45
  52.7 3.6 %collective-permute-start.13 = (bf16[2,16,1024]{2,1,0:T(8,128)(2,1)S(1)}, bf16[2,16,1024]{2,1,0:T(8,128)(2,1)S(1)}, u32[]{:S(2)}, u32[]{:S(2)}) collective-permute-start(bf16[2,16,1024]{2,1,0:T(8,128)(2,1)S(1)} %get-tuple-element.22), channel_id=1, source_target_pairs={{0,6},{1,7},{2,0},{3,1},{4,2},{5,3},{6,4},{7,5},{8,14},{9,15},{10,... | collective-permute-start | bytes 196616 | tf_op jit(solution)/shard_map/ppermute | solution.py:45
  56.3 5.2 %collective-permute-done.12.half_a = bf16[2,16,1024]{2,1,0:T(8,128)(2,1)S(1)} collective-permute-done((bf16[2,16,1024]{2,1,0:T(8,128)(2,1)S(1)}, bf16[2,16,1024]{2,1,0:T(8,128)(2,1)S(1)}, u32[]{:S(2)}, u32[]{:S(2)}) %collective-permute-start.12) | collective-permute-done | bytes 65568 | tf_op jit(solution)/shard_map/ppermute | solution.py:45
  61.4 0.1 shard_map.44
  61.5 3.8 %collective-permute-start.14 = (bf16[2,2,16,1024]{3,2,1,0:T(8,128)(2,1)S(1)}, bf16[2,2,16,1024]{3,2,1,0:T(8,128)(2,1)S(1)}, u32[]{:S(2)}, u32[]{:S(2)}) collective-permute-start(bf16[2,2,16,1024]{3,2,1,0:T(8,128)(2,1)S(1)} %get-tuple-element.25), channel_id=1, source_target_pairs={{0,2},{1,3},{2,4},{3,5},{4,6},{5,7},{6,0},{7,1},{8,10},{9,11},{10,... | collective-permute-start | bytes 393224 | tf_op jit(solution)/shard_map/ppermute | solution.py:45
  65.3 5.4 %collective-permute-done.14.far_up = bf16[2,2,16,1024]{3,2,1,0:T(8,128)(2,1)S(1)} collective-permute-done((bf16[2,2,16,1024]{3,2,1,0:T(8,128)(2,1)S(1)}, bf16[2,2,16,1024]{3,2,1,0:T(8,128)(2,1)S(1)}, u32[]{:S(2)}, u32[]{:S(2)}) %collective-permute-start.14) | collective-permute-done | bytes 131104 | tf_op jit(solution)/shard_map/ppermute | solution.py:45
  70.7 0.1 shard_map.45.a
  70.8 2.9 %collective-permute-start.16 = (bf16[2,2,16,1024]{3,2,1,0:T(8,128)(2,1)S(1)}, bf16[2,2,16,1024]{3,2,1,0:T(8,128)(2,1)S(1)}, u32[]{:S(2)}, u32[]{:S(2)}) collective-permute-start(bf16[2,2,16,1024]{3,2,1,0:T(8,128)(2,1)S(1)} %shard_map.45.a), channel_id=1, source_target_pairs={{0,8},{1,9},{2,10},{3,11},{4,12},{5,13},{6,14},{7,15},{8,0},{9,1},... | collective-permute-start | bytes 393224 | tf_op jit(solution)/shard_map/ppermute | solution.py:45
  73.7 2.5 %collective-permute-done.16.b = bf16[2,2,16,1024]{3,2,1,0:T(8,128)(2,1)S(1)} collective-permute-done((bf16[2,2,16,1024]{3,2,1,0:T(8,128)(2,1)S(1)}, bf16[2,2,16,1024]{3,2,1,0:T(8,128)(2,1)S(1)}, u32[]{:S(2)}, u32[]{:S(2)}) %collective-permute-start.16) | collective-permute-done | bytes 131104 | tf_op jit(solution)/shard_map/ppermute | solution.py:45
  76.3 3.5 %collective-permute-start.20 = (bf16[2,2,16,1024]{3,2,1,0:T(8,128)(2,1)S(1)}, bf16[2,2,16,1024]{3,2,1,0:T(8,128)(2,1)S(1)}, u32[]{:S(2)}, u32[]{:S(2)}) collective-permute-start(bf16[2,2,16,1024]{3,2,1,0:T(8,128)(2,1)S(1)} %shard_map.46.refs_0_), channel_id=1, source_target_pairs={{0,6},{1,7},{2,0},{3,1},{4,2},{5,3},{6,4},{7,5},{8,14},{9,15},{10,... | collective-permute-start | bytes 393224 | tf_op jit(solution)/shard_map/ppermute | solution.py:45
  79.7 3.5 %collective-permute-start.25 = (f32[1,1024]{1,0:T(1,128)S(1)}, f32[1,1024]{1,0:T(1,128)S(1)}, u32[]{:S(2)}, u32[]{:S(2)}) collective-permute-start(f32[1,1024]{1,0:T(1,128)S(1)} %get-tuple-element.29.refs_11_), channel_id=1, source_target_pairs={{0,16},{16,0},{32,48},{48,32},{64,80},{80,64},{96,112},{112,96},{1... | collective-permute-start | bytes 12296 | tf_op jit(solution)/shard_map/ppermute | solution.py:45
  83.2 0.3 collective-permute-start.22
  83.5 0.5 collective-permute-start.18
  84.1 1.2 %collective-permute-start.17 = (bf16[2,2,16,1024]{3,2,1,0:T(8,128)(2,1)S(1)}, bf16[2,2,16,1024]{3,2,1,0:T(8,128)(2,1)S(1)}, u32[]{:S(2)}, u32[]{:S(2)}) collective-permute-start(bf16[2,2,16,1024]{3,2,1,0:T(8,128)(2,1)S(1)} %shard_map.46.refs_0_), channel_id=1, source_target_pairs={{0,1},{1,2},{2,3},{3,4},{4,5},{5,6},{6,7},{7,0},{8,9},{9,10},{10,1... | collective-permute-start | bytes 393224 | tf_op jit(solution)/shard_map/ppermute | solution.py:45
  85.3 1.8 %collective-permute-start.21 = (bf16[2,2,16,1024]{3,2,1,0:T(8,128)(2,1)S(1)}, bf16[2,2,16,1024]{3,2,1,0:T(8,128)(2,1)S(1)}, u32[]{:S(2)}, u32[]{:S(2)}) collective-permute-start(bf16[2,2,16,1024]{3,2,1,0:T(8,128)(2,1)S(1)} %collective-permute-done.20.refs_5_), channel_id=1, source_target_pairs={{0,7},{1,0},{2,1},{3,2},{4,3},{5,4},{6,5},{7,6},{8,15},{9,8},{10,9... | collective-permute-start | bytes 393224 | tf_op jit(solution)/shard_map/ppermute | solution.py:45
  87.1 6.7 %collective-permute-done.18.refs_2_ = bf16[2,2,16,1024]{3,2,1,0:T(8,128)(2,1)S(1)} collective-permute-done((bf16[2,2,16,1024]{3,2,1,0:T(8,128)(2,1)S(1)}, bf16[2,2,16,1024]{3,2,1,0:T(8,128)(2,1)S(1)}, u32[]{:S(2)}, u32[]{:S(2)}) %collective-permute-start.18) | collective-permute-done | bytes 131104 | tf_op jit(solution)/shard_map/ppermute | solution.py:45
  93.8 0.0 collective-permute-start.19
  93.8 0.8 collective-permute-start.24
  94.6 1.7 %collective-permute-start.23 = (bf16[2,16,1024]{2,1,0:T(8,128)(2,1)S(1)}, bf16[2,16,1024]{2,1,0:T(8,128)(2,1)S(1)}, u32[]{:S(2)}, u32[]{:S(2)}) collective-permute-start(bf16[2,16,1024]{2,1,0:T(8,128)(2,1)S(1)} %slice_bitcast_fusion.3), channel_id=1, source_target_pairs={{0,2},{1,3},{2,4},{3,5},{4,6},{5,7},{6,0},{7,1},{8,10},{9,11},{10,... | collective-permute-start | bytes 196616 | tf_op jit(solution)/shard_map/ppermute | solution.py:45
  96.2 2.6 %collective-permute-done.24.refs_8_ = bf16[2,16,1024]{2,1,0:T(8,128)(2,1)S(1)} collective-permute-done((bf16[2,16,1024]{2,1,0:T(8,128)(2,1)S(1)}, bf16[2,16,1024]{2,1,0:T(8,128)(2,1)S(1)}, u32[]{:S(2)}, u32[]{:S(2)}) %collective-permute-start.24) | collective-permute-done | bytes 65568 | tf_op jit(solution)/shard_map/ppermute | solution.py:45
  98.9 2.0 %collective-permute-done.23.refs_7_ = bf16[2,16,1024]{2,1,0:T(8,128)(2,1)S(1)} collective-permute-done((bf16[2,16,1024]{2,1,0:T(8,128)(2,1)S(1)}, bf16[2,16,1024]{2,1,0:T(8,128)(2,1)S(1)}, u32[]{:S(2)}, u32[]{:S(2)}) %collective-permute-start.23) | collective-permute-done | bytes 65568 | tf_op jit(solution)/shard_map/ppermute | solution.py:45
  100.9 1.7 %shard_map.47 = (f32[2,128,1024]{2,1,0:T(8,128)S(1)}, f32[2,128,1024]{2,1,0:T(8,128)S(1)}, f32[16,4,1024]{2,1,0:T(4,128)S(1)}) custom-call(bf16[2,2,16,1024]{3,2,1,0:T(8,128)(2,1)S(1)} %shard_map.46.refs_0_, bf16[2,2,16,1024]{3,2,1,0:T(8,128)(2,1)S(1)} %collective-permute-done.17.refs_1_, bf16[2,2,16,1024]{3,2,1,0:T(8,128)(2,1)S(1)} %collective-permute-done.18.refs_2_, ...), custom_call_target="tpu_custom_call" | custom-call | flops 1073741824 | bytes 8658944 | tf_op jit(solution)/shard_map/pallas_call | solution.py:52
  102.6 3.6 %collective-permute-start.26 = (f32[2,128,1024]{2,1,0:T(8,128)S(1)}, f32[2,128,1024]{2,1,0:T(8,128)S(1)}, u32[]{:S(2)}, u32[]{:S(2)}) collective-permute-start(f32[2,128,1024]{2,1,0:T(8,128)S(1)} %get-tuple-element.31), channel_id=1, source_target_pairs={{0,16},{16,0},{32,48},{48,32},{64,80},{80,64},{96,112},{112,96},{1... | collective-permute-start | bytes 3145736 | tf_op jit(solution)/shard_map/ppermute | solution.py:45
  106.2 9.8 %all_to_all.5.sums = f32[16,4,1024]{2,1,0:T(4,128)S(1)} all-to-all(f32[16,4,1024]{2,1,0:T(4,128)S(1)} %get-tuple-element.32), channel_id=1, replica_groups=mesh['dp'=16,'feat'=16] {'dp'}, dimensions={0} | all-to-all | bytes 524288 | tf_op jit(solution)/shard_map/all_to_all | solution.py:303
  116.0 1.0 shard_map.48
  (21 shorter events, 0.1 us)
Async XLA Ops:
  1.7 14.2 %collective-permute-start.1 = (bf16[2,128,1024]{2,1,0:T(8,128)(2,1)S(1)}, bf16[2,128,1024]{2,1,0:T(8,128)(2,1)S(1)}, u32[]{:S(2)}, u32[]{:S(2)}) collective-permute-start(bf16[2,128,1024]{2,1,0:T(8,128)(2,1)S(1)} %pad_maximum_fusion.refs_0_), channel_id=1, source_target_pairs={{0,96},{16,112},{32,0},{48,16},{64,32},{80,48},{96,64},{112,80},{1... | collective-permute-start | bytes 1572872 | tf_op jit(solution)/shard_map/ppermute | solution.py:45
  5.4 14.1 %collective-permute-start = (bf16[2,128,1024]{2,1,0:T(8,128)(2,1)S(1)}, bf16[2,128,1024]{2,1,0:T(8,128)(2,1)S(1)}, u32[]{:S(2)}, u32[]{:S(2)}) collective-permute-start(bf16[2,128,1024]{2,1,0:T(8,128)(2,1)S(1)} %pad_maximum_fusion.refs_0_), channel_id=1, source_target_pairs={{0,32},{16,48},{32,64},{48,80},{64,96},{80,112},{96,0},{112,16},{1... | collective-permute-start | bytes 1572872 | tf_op jit(solution)/shard_map/ppermute | solution.py:45
  5.4 14.2 %collective-permute-start.2 = (bf16[2,128,1024]{2,1,0:T(8,128)(2,1)S(1)}, bf16[2,128,1024]{2,1,0:T(8,128)(2,1)S(1)}, u32[]{:S(2)}, u32[]{:S(2)}) collective-permute-start(bf16[2,128,1024]{2,1,0:T(8,128)(2,1)S(1)} %pad_maximum_fusion.refs_0_), channel_id=1, source_target_pairs={{0,128},{16,144},{32,160},{48,176},{64,192},{80,208},{96,224},{112... | collective-permute-start | bytes 1572872 | tf_op jit(solution)/shard_map/ppermute | solution.py:45
  16.0 7.5 %collective-permute-start.6 = (bf16[128,1024]{1,0:T(8,128)(2,1)S(1)}, bf16[128,1024]{1,0:T(8,128)(2,1)S(1)}, u32[]{:S(2)}, u32[]{:S(2)}) collective-permute-start(bf16[128,1024]{1,0:T(8,128)(2,1)S(1)} %slice_bitcast_fusion), channel_id=1, source_target_pairs={{0,96},{16,112},{32,0},{48,16},{64,32},{80,48},{96,64},{112,80},{1... | collective-permute-start | bytes 786440 | tf_op jit(solution)/shard_map/ppermute | solution.py:45
  19.5 7.3 %collective-permute-start.5 = (bf16[128,1024]{1,0:T(8,128)(2,1)S(1)}, bf16[128,1024]{1,0:T(8,128)(2,1)S(1)}, u32[]{:S(2)}, u32[]{:S(2)}) collective-permute-start(bf16[128,1024]{1,0:T(8,128)(2,1)S(1)} %slice_bitcast_fusion.1), channel_id=1, source_target_pairs={{0,32},{16,48},{32,64},{48,80},{64,96},{80,112},{96,0},{112,16},{1... | collective-permute-start | bytes 786440 | tf_op jit(solution)/shard_map/ppermute | solution.py:45
  19.6 15.2 %collective-permute-start.4 = (bf16[2,128,1024]{2,1,0:T(8,128)(2,1)S(1)}, bf16[2,128,1024]{2,1,0:T(8,128)(2,1)S(1)}, u32[]{:S(2)}, u32[]{:S(2)}) collective-permute-start(bf16[2,128,1024]{2,1,0:T(8,128)(2,1)S(1)} %collective-permute-done.2.refs_3_), channel_id=1, source_target_pairs={{0,96},{16,112},{32,0},{48,16},{64,32},{80,48},{96,64},{112,80},{1... | collective-permute-start | bytes 1572872 | tf_op jit(solution)/shard_map/ppermute | solution.py:45
  22.2 15.7 %collective-permute-start.3 = (bf16[2,128,1024]{2,1,0:T(8,128)(2,1)S(1)}, bf16[2,128,1024]{2,1,0:T(8,128)(2,1)S(1)}, u32[]{:S(2)}, u32[]{:S(2)}) collective-permute-start(bf16[2,128,1024]{2,1,0:T(8,128)(2,1)S(1)} %collective-permute-done.2.refs_3_), channel_id=1, source_target_pairs={{0,32},{16,48},{32,64},{48,80},{64,96},{80,112},{96,0},{112,16},{1... | collective-permute-start | bytes 1572872 | tf_op jit(solution)/shard_map/ppermute | solution.py:45
  26.8 13.4 %collective-permute-start.7 = (bf16[2,128,1024]{2,1,0:T(8,128)(2,1)S(1)}, bf16[2,128,1024]{2,1,0:T(8,128)(2,1)S(1)}, u32[]{:S(2)}, u32[]{:S(2)}) collective-permute-start(bf16[2,128,1024]{2,1,0:T(8,128)(2,1)S(1)} %pad_maximum_fusion.1), channel_id=1, source_target_pairs={{0,128},{16,144},{32,160},{48,176},{64,192},{80,208},{96,224},{112... | collective-permute-start | bytes 1572872 | tf_op jit(solution)/shard_map/ppermute | solution.py:45
  28.1 15.4 %collective-permute-start.9 = (bf16[2,128,1024]{2,1,0:T(8,128)(2,1)S(1)}, bf16[2,128,1024]{2,1,0:T(8,128)(2,1)S(1)}, u32[]{:S(2)}, u32[]{:S(2)}) collective-permute-start(bf16[2,128,1024]{2,1,0:T(8,128)(2,1)S(1)} %pad_maximum_fusion.refs_0_), channel_id=1, source_target_pairs={{0,16},{16,0},{32,48},{48,32},{64,80},{80,64},{96,112},{112,96},{1... | collective-permute-start | bytes 1572872 | tf_op jit(solution)/shard_map/ppermute | solution.py:45
  40.5 3.9 %collective-permute-start.8 = (f32[4,1024]{1,0:T(4,128)S(1)}, f32[4,1024]{1,0:T(4,128)S(1)}, u32[]{:S(2)}, u32[]{:S(2)}) collective-permute-start(f32[4,1024]{1,0:T(4,128)S(1)} %shard_map.42.own_m), channel_id=1, source_target_pairs={{0,16},{16,0},{32,48},{48,32},{64,80},{80,64},{96,112},{112,96},{1... | collective-permute-start | bytes 49160 | tf_op jit(solution)/shard_map/ppermute | solution.py:45
  46.9 14.5 %collective-permute-start.10 = (bf16[2,2,2,16,1024]{4,3,2,1,0:T(8,128)(2,1)S(1)}, bf16[2,2,2,16,1024]{4,3,2,1,0:T(8,128)(2,1)S(1)}, u32[]{:S(2)}, u32[]{:S(2)}) collective-permute-start(bf16[2,2,2,16,1024]{4,3,2,1,0:T(8,128)(2,1)S(1)} %get-tuple-element.19), channel_id=1, source_target_pairs={{0,1},{1,2},{2,3},{3,4},{4,5},{5,6},{6,7},{7,0},{8,9},{9,10},{10,1... | collective-permute-start | bytes 786440 | tf_op jit(solution)/shard_map/ppermute | solution.py:45
  48.7 12.8 %collective-permute-start.11 = (bf16[2,2,2,16,1024]{4,3,2,1,0:T(8,128)(2,1)S(1)}, bf16[2,2,2,16,1024]{4,3,2,1,0:T(8,128)(2,1)S(1)}, u32[]{:S(2)}, u32[]{:S(2)}) collective-permute-start(bf16[2,2,2,16,1024]{4,3,2,1,0:T(8,128)(2,1)S(1)} %get-tuple-element.20), channel_id=1, source_target_pairs={{0,7},{1,0},{2,1},{3,2},{4,3},{5,4},{6,5},{7,6},{8,15},{9,8},{10,9... | collective-permute-start | bytes 786440 | tf_op jit(solution)/shard_map/ppermute | solution.py:45
  52.7 8.7 %collective-permute-start.12 = (bf16[2,16,1024]{2,1,0:T(8,128)(2,1)S(1)}, bf16[2,16,1024]{2,1,0:T(8,128)(2,1)S(1)}, u32[]{:S(2)}, u32[]{:S(2)}) collective-permute-start(bf16[2,16,1024]{2,1,0:T(8,128)(2,1)S(1)} %get-tuple-element.21), channel_id=1, source_target_pairs={{0,2},{1,3},{2,4},{3,5},{4,6},{5,7},{6,0},{7,1},{8,10},{9,11},{10,... | collective-permute-start | bytes 196616 | tf_op jit(solution)/shard_map/ppermute | solution.py:45
  52.7 8.7 %collective-permute-start.13 = (bf16[2,16,1024]{2,1,0:T(8,128)(2,1)S(1)}, bf16[2,16,1024]{2,1,0:T(8,128)(2,1)S(1)}, u32[]{:S(2)}, u32[]{:S(2)}) collective-permute-start(bf16[2,16,1024]{2,1,0:T(8,128)(2,1)S(1)} %get-tuple-element.22), channel_id=1, source_target_pairs={{0,6},{1,7},{2,0},{3,1},{4,2},{5,3},{6,4},{7,5},{8,14},{9,15},{10,... | collective-permute-start | bytes 196616 | tf_op jit(solution)/shard_map/ppermute | solution.py:45
  61.5 9.2 %collective-permute-start.14 = (bf16[2,2,16,1024]{3,2,1,0:T(8,128)(2,1)S(1)}, bf16[2,2,16,1024]{3,2,1,0:T(8,128)(2,1)S(1)}, u32[]{:S(2)}, u32[]{:S(2)}) collective-permute-start(bf16[2,2,16,1024]{3,2,1,0:T(8,128)(2,1)S(1)} %get-tuple-element.25), channel_id=1, source_target_pairs={{0,2},{1,3},{2,4},{3,5},{4,6},{5,7},{6,0},{7,1},{8,10},{9,11},{10,... | collective-permute-start | bytes 393224 | tf_op jit(solution)/shard_map/ppermute | solution.py:45
  65.3 5.4 %collective-permute-start.15 = (bf16[2,2,16,1024]{3,2,1,0:T(8,128)(2,1)S(1)}, bf16[2,2,16,1024]{3,2,1,0:T(8,128)(2,1)S(1)}, u32[]{:S(2)}, u32[]{:S(2)}) collective-permute-start(bf16[2,2,16,1024]{3,2,1,0:T(8,128)(2,1)S(1)} %get-tuple-element.26), channel_id=1, source_target_pairs={{0,6},{1,7},{2,0},{3,1},{4,2},{5,3},{6,4},{7,5},{8,14},{9,15},{10,... | collective-permute-start | bytes 393224 | tf_op jit(solution)/shard_map/ppermute | solution.py:45
  70.8 5.4 %collective-permute-start.16 = (bf16[2,2,16,1024]{3,2,1,0:T(8,128)(2,1)S(1)}, bf16[2,2,16,1024]{3,2,1,0:T(8,128)(2,1)S(1)}, u32[]{:S(2)}, u32[]{:S(2)}) collective-permute-start(bf16[2,2,16,1024]{3,2,1,0:T(8,128)(2,1)S(1)} %shard_map.45.a), channel_id=1, source_target_pairs={{0,8},{1,9},{2,10},{3,11},{4,12},{5,13},{6,14},{7,15},{8,0},{9,1},... | collective-permute-start | bytes 393224 | tf_op jit(solution)/shard_map/ppermute | solution.py:45
  76.3 9.0 %collective-permute-start.20 = (bf16[2,2,16,1024]{3,2,1,0:T(8,128)(2,1)S(1)}, bf16[2,2,16,1024]{3,2,1,0:T(8,128)(2,1)S(1)}, u32[]{:S(2)}, u32[]{:S(2)}) collective-permute-start(bf16[2,2,16,1024]{3,2,1,0:T(8,128)(2,1)S(1)} %shard_map.46.refs_0_), channel_id=1, source_target_pairs={{0,6},{1,7},{2,0},{3,1},{4,2},{5,3},{6,4},{7,5},{8,14},{9,15},{10,... | collective-permute-start | bytes 393224 | tf_op jit(solution)/shard_map/ppermute | solution.py:45
  79.7 14.0 %collective-permute-start.25 = (f32[1,1024]{1,0:T(1,128)S(1)}, f32[1,1024]{1,0:T(1,128)S(1)}, u32[]{:S(2)}, u32[]{:S(2)}) collective-permute-start(f32[1,1024]{1,0:T(1,128)S(1)} %get-tuple-element.29.refs_11_), channel_id=1, source_target_pairs={{0,16},{16,0},{32,48},{48,32},{64,80},{80,64},{96,112},{112,96},{1... | collective-permute-start | bytes 12296 | tf_op jit(solution)/shard_map/ppermute | solution.py:45
  83.2 11.4 %collective-permute-start.22 = (bf16[2,2,16,1024]{3,2,1,0:T(8,128)(2,1)S(1)}, bf16[2,2,16,1024]{3,2,1,0:T(8,128)(2,1)S(1)}, u32[]{:S(2)}, u32[]{:S(2)}) collective-permute-start(bf16[2,2,16,1024]{3,2,1,0:T(8,128)(2,1)S(1)} %shard_map.46.refs_0_), channel_id=1, source_target_pairs={{0,7},{1,0},{2,1},{3,2},{4,3},{5,4},{6,5},{7,6},{8,15},{9,8},{10,9... | collective-permute-start | bytes 393224 | tf_op jit(solution)/shard_map/ppermute | solution.py:45
  83.5 10.2 %collective-permute-start.18 = (bf16[2,2,16,1024]{3,2,1,0:T(8,128)(2,1)S(1)}, bf16[2,2,16,1024]{3,2,1,0:T(8,128)(2,1)S(1)}, u32[]{:S(2)}, u32[]{:S(2)}) collective-permute-start(bf16[2,2,16,1024]{3,2,1,0:T(8,128)(2,1)S(1)} %shard_map.46.refs_0_), channel_id=1, source_target_pairs={{0,2},{1,3},{2,4},{3,5},{4,6},{5,7},{6,0},{7,1},{8,10},{9,11},{10,... | collective-permute-start | bytes 393224 | tf_op jit(solution)/shard_map/ppermute | solution.py:45
  84.1 12.2 %collective-permute-start.17 = (bf16[2,2,16,1024]{3,2,1,0:T(8,128)(2,1)S(1)}, bf16[2,2,16,1024]{3,2,1,0:T(8,128)(2,1)S(1)}, u32[]{:S(2)}, u32[]{:S(2)}) collective-permute-start(bf16[2,2,16,1024]{3,2,1,0:T(8,128)(2,1)S(1)} %shard_map.46.refs_0_), channel_id=1, source_target_pairs={{0,1},{1,2},{2,3},{3,4},{4,5},{5,6},{6,7},{7,0},{8,9},{9,10},{10,1... | collective-permute-start | bytes 393224 | tf_op jit(solution)/shard_map/ppermute | solution.py:45
  85.3 15.6 %collective-permute-start.21 = (bf16[2,2,16,1024]{3,2,1,0:T(8,128)(2,1)S(1)}, bf16[2,2,16,1024]{3,2,1,0:T(8,128)(2,1)S(1)}, u32[]{:S(2)}, u32[]{:S(2)}) collective-permute-start(bf16[2,2,16,1024]{3,2,1,0:T(8,128)(2,1)S(1)} %collective-permute-done.20.refs_5_), channel_id=1, source_target_pairs={{0,7},{1,0},{2,1},{3,2},{4,3},{5,4},{6,5},{7,6},{8,15},{9,8},{10,9... | collective-permute-start | bytes 393224 | tf_op jit(solution)/shard_map/ppermute | solution.py:45
  93.8 7.1 %collective-permute-start.19 = (bf16[2,2,16,1024]{3,2,1,0:T(8,128)(2,1)S(1)}, bf16[2,2,16,1024]{3,2,1,0:T(8,128)(2,1)S(1)}, u32[]{:S(2)}, u32[]{:S(2)}) collective-permute-start(bf16[2,2,16,1024]{3,2,1,0:T(8,128)(2,1)S(1)} %collective-permute-done.18.refs_2_), channel_id=1, source_target_pairs={{0,1},{1,2},{2,3},{3,4},{4,5},{5,6},{6,7},{7,0},{8,9},{9,10},{10,1... | collective-permute-start | bytes 393224 | tf_op jit(solution)/shard_map/ppermute | solution.py:45
  93.8 5.1 %collective-permute-start.24 = (bf16[2,16,1024]{2,1,0:T(8,128)(2,1)S(1)}, bf16[2,16,1024]{2,1,0:T(8,128)(2,1)S(1)}, u32[]{:S(2)}, u32[]{:S(2)}) collective-permute-start(bf16[2,16,1024]{2,1,0:T(8,128)(2,1)S(1)} %slice_bitcast_fusion.2), channel_id=1, source_target_pairs={{0,6},{1,7},{2,0},{3,1},{4,2},{5,3},{6,4},{7,5},{8,14},{9,15},{10,... | collective-permute-start | bytes 196616 | tf_op jit(solution)/shard_map/ppermute | solution.py:45
  94.6 6.3 %collective-permute-start.23 = (bf16[2,16,1024]{2,1,0:T(8,128)(2,1)S(1)}, bf16[2,16,1024]{2,1,0:T(8,128)(2,1)S(1)}, u32[]{:S(2)}, u32[]{:S(2)}) collective-permute-start(bf16[2,16,1024]{2,1,0:T(8,128)(2,1)S(1)} %slice_bitcast_fusion.3), channel_id=1, source_target_pairs={{0,2},{1,3},{2,4},{3,5},{4,6},{5,7},{6,0},{7,1},{8,10},{9,11},{10,... | collective-permute-start | bytes 196616 | tf_op jit(solution)/shard_map/ppermute | solution.py:45
  102.6 13.5 %collective-permute-start.26 = (f32[2,128,1024]{2,1,0:T(8,128)S(1)}, f32[2,128,1024]{2,1,0:T(8,128)S(1)}, u32[]{:S(2)}, u32[]{:S(2)}) collective-permute-start(f32[2,128,1024]{2,1,0:T(8,128)S(1)} %get-tuple-element.31), channel_id=1, source_target_pairs={{0,16},{16,0},{32,48},{48,32},{64,80},{80,64},{96,112},{112,96},{1... | collective-permute-start | bytes 3145736 | tf_op jit(solution)/shard_map/ppermute | solution.py:45

commit v4 on v3

--- a/solution.py
+++ b/solution.py
@@ -68,55 +68,72 @@
     return jax.ShapeDtypeStruct(dims, dtype)
 
 
-def moments_of(pieces):
-    count = sum(p.shape[0] for p in pieces)
-    total = sum(jnp.sum(p[...].astype(f32), 0, keepdims=True) for p in pieces)
-    mean = total / count
-    square = 0.0
-    for p in pieces:
-        centered = p[...].astype(f32) - mean
-        square = square + jnp.sum(centered * centered, 0, keepdims=True)
-    return count, mean, square
+def moments_of(pieces_a, pieces_b):
+    count = sum(p.shape[0] for p in pieces_a)
+    mean_a = sum(jnp.sum(p[...].astype(f32), 0, keepdims=True) for p in pieces_a) / count
+    mean_b = sum(jnp.sum(p[...].astype(f32), 0, keepdims=True) for p in pieces_b) / count
+    square_a = square_b = product = 0.0
+    for p, q in zip(pieces_a, pieces_b):
+        a, b = p[...].astype(f32) - mean_a, q[...].astype(f32) - mean_b
+        square_a = square_a + jnp.sum(a * a, 0, keepdims=True)
+        square_b = square_b + jnp.sum(b * b, 0, keepdims=True)
+        product = product + jnp.sum(a * b, 0, keepdims=True)
+    return count, (mean_a, mean_b, square_a, square_b, product)
+
+
+def merge(count, one, other_count, other):
+    total = count + other_count
+    gap_a, gap_b = other[0] - one[0], other[1] - one[1]
+    weight = count * other_count / total
+    return (
+        one[0] + gap_a * (other_count / total),
+        one[1] + gap_b * (other_count / total),
+        one[2] + other[2] + gap_a * gap_a * weight,
+        one[3] + other[3] + gap_b * gap_b * weight,
+        one[4] + other[4] + gap_a * gap_b * weight,
+    )
+
+
+def put_rows(out, values):
+    for i, value in enumerate(values):
+        out[i : i + 1, :] = value
+
+
+def get_rows(ref):
+    return [ref[i : i + 1, :] for i in range(ref.shape[0])]
 
 
 def early_moments_body(*refs):
-    *pairs, far_a, far_b, out = refs
-    for v, far in enumerate((far_a, far_b)):
-        _, mean, square = moments_of([p.at[v] for p in pairs] + [far])
-        out[2 * v : 2 * v + 1, :] = mean
-        out[2 * v + 1 : 2 * v + 2, :] = square
-
-
-def late_moments_body(early_count, early, far, out):
-    for v in range(2):
-        late_count, late_mean, late_square = moments_of([far.at[v]])
-        mean = early[2 * v : 2 * v + 1, :]
-        gap = late_mean - mean
-        count = early_count + late_count
-        out[2 * v : 2 * v + 1, :] = mean + gap * (late_count / count)
-        out[2 * v + 1 : 2 * v + 2, :] = (
-            early[2 * v + 1 : 2 * v + 2, :]
-            + late_square
-            + gap * gap * (early_count * late_count / count)
-        )
+    *pieces, out = refs
+    single, stacked = pieces[:2], pieces[2:]
+    _, moments = moments_of(
+        [single[0], *(p.at[0] for p in stacked)], [single[1], *(p.at[1] for p in stacked)]
+    )
+    put_rows(out, moments)
+
+
+def late_moments_body(early_count, early, *refs):
+    *pairs, out = refs
+    count, late = moments_of([p.at[0] for p in pairs], [p.at[1] for p in pairs])
+    put_rows(out, merge(early_count, get_rows(early), count, late))
 
 
 def gram_body(batch, own_m, sib_m, sib, *refs):
-    pairs, fars, outs = refs[:6], refs[6:9], refs[9:]
-    lead, normed, spread_out, diag, mine, up_2, down_2, up_1, down_1, far_a, far_b, gram = outs
+    *refs, lead, normed, stats, mine, up_2, down_2, up_1, down_1, far_a, far_b, gram = refs
+    single, stacked = refs[:2], refs[2:]
     rows, part = sib.shape[1], mine.shape[2]
-    for v in range(2):
-        m, q = slice(2 * v, 2 * v + 1), slice(2 * v + 1, 2 * v + 2)
-        mean = 0.5 * (own_m[m, :] + sib_m[m, :])
-        gap = own_m[m, :] - sib_m[m, :]
-        square = own_m[q, :] + sib_m[q, :] + gap * gap * (batch / 4)
-        spread = jnp.sqrt(square / batch + epsilon)
-        spread_out[v : v + 1, :] = spread
-        pieces = [p.at[v] for p in pairs] + [fars[v], fars[2].at[v]]
-        for i, p in enumerate((pieces[0], sib.at[v])):
+    mean_a, mean_b, square_a, square_b, product = merge(
+        batch // 2, get_rows(own_m), batch // 2, get_rows(sib_m)
+    )
+    spreads = [jnp.sqrt(square / batch + epsilon) for square in (square_a, square_b)]
+    corr = product / (batch * spreads[0] * spreads[1])
+    put_rows(stats, (*spreads, 2.0 * (corr - 1.0) - 2.0 * off_weight * corr))
+    for v, (mean, spread) in enumerate(zip((mean_a, mean_b), spreads)):
+        view = [*(p.at[v] for p in stacked), single[v]]
+        for i, p in enumerate((view[0], sib.at[v])):
             r = slice(i * rows, (i + 1) * rows)
             lead[v, r, :] = ((p[...].astype(f32) - mean) / spread).astype(bf16)
-        for i, p in enumerate(pieces):
+        for i, p in enumerate(view):
             r = slice(i * rows, (i + 1) * rows)
             normed[v, r, :] = ((p[...].astype(f32) - mean) / spread).astype(bf16)
             block = lax.dot_general(
@@ -138,13 +155,6 @@
             store(up, v, up_1.at[i, v])
             store(down, v, down_1.at[i, v])
         store(4, v, (far_a, far_b)[v])
-    total = 0.0
-    for i in range(normed.shape[1] // rows):
-        r = slice(i * rows, (i + 1) * rows)
-        total = total + jnp.sum(
-            normed[0, r, :].astype(f32) * normed[1, r, :].astype(f32), 0, keepdims=True
-        )
-    diag[...] = total
 
 
 def fold_body(far_up, far_down, half_a, half_b, up_2, down_2, up_out, down_out):
@@ -194,8 +204,8 @@
     return [block, from_1, from_2, from_3, from_5, from_6, from_7, from_4a, from_4b]
 
 
-def apply_body(batch, scale, *refs):
-    *blocks, from_4a, from_4b, normed, lead, diag_own, diag_sib, own, other, sums, gram = refs
+def apply_body(scale, *refs):
+    *blocks, from_4a, from_4b, normed, lead, stats, own, other, sums, gram = refs
     rows, part = own.shape[1], blocks[0].shape[2]
     z = lax.rem(lax.axis_index("feat"), Z)
 
@@ -208,8 +218,7 @@
         for back, block in zip((0, 1, 2, 3, 5, 6, 7), blocks):
             load(back, v, block.at[v])
         load(4, v, (from_4a, from_4b)[v])
-    corr = (diag_own[...] + diag_sib[...]) / batch
-    diag = 2.0 * (corr - 1.0) - 2.0 * off_weight * corr
+    diag = stats[2:3, :]
     for v in range(2):
         first = second = 0.0
         for h, out in enumerate((own, other)):
@@ -225,7 +234,7 @@
             sums[i, 2 * v + 1 : 2 * v + 2, :] = second
 
 
-def final_body(batch, own, recv, lead, sums, spread, grad_a, grad_b):
+def final_body(batch, own, recv, lead, sums, stats, grad_a, grad_b):
     rows = own.shape[1]
     total = sums[0]
     for i in range(1, sums.shape[0]):
@@ -235,7 +244,7 @@
         normal = lead[v, 0:rows, :].astype(f32)
         first, second = total[2 * v : 2 * v + 1, :], total[2 * v + 1 : 2 * v + 2, :]
         up = own[v] + recv[v]
-        out[...] = ((up - first - normal * second) / spread[v : v + 1, :]).astype(bf16)
+        out[...] = ((up - first - normal * second) / stats[v : v + 1, :]).astype(bf16)
 
 
 def on_device(view_a, view_b):
@@ -254,21 +263,21 @@
     far_a, far_b = send(from_down[0], TO_UP), send(from_up[1], TO_DOWN)
     x_down, x_up = send(from_x, TO_UP), send(from_x, TO_DOWN)
     x_far = send(jnp.stack([far_a, far_b]), TO_X)
-    pairs = [views, from_down, from_up, from_x, x_down, x_up]
-    early = call(early_moments_body, shape(4, cols), *pairs, far_a, far_b)
+    single = [far_a, far_b]
+    stacked = [views, from_down, from_up, from_x, x_down, x_up, x_far]
+    early = call(early_moments_body, shape(5, cols), *single, *stacked[:4])
     moments = call(
-        functools.partial(late_moments_body, half - rows), shape(4, cols), early, x_far
+        functools.partial(late_moments_body, 5 * rows), shape(5, cols), early, *stacked[4:]
     )
     one = shape(X_HI, part, half, dtype=bf16)
     both = shape(2, *one.shape, dtype=bf16)
     four = shape(2, *both.shape, dtype=bf16)
-    lead, normed, spread, diag, *chunks = call(
+    lead, normed, stats, *chunks = call(
         functools.partial(gram_body, batch),
         (
             shape(2, CORES * rows, cols, dtype=bf16),
             shape(2, half, cols, dtype=bf16),
-            shape(2, cols),
-            shape(1, cols),
+            shape(3, cols),
             both,
             both,
             both,
@@ -280,23 +289,19 @@
         moments,
         send(moments, TO_CORE),
         sib,
-        *pairs,
-        far_a,
-        far_b,
-        x_far,
+        *single,
+        *stacked,
         flops=work,
         scratch=[pltpu.VMEM((2, CORES * rows, half), bf16)],
     )
-    diag_sib = send(diag, TO_CORE)
     blocks = spread_rows(reduce_rows(*chunks))
     own, other, sums = call(
-        functools.partial(apply_body, batch, scale),
+        functools.partial(apply_body, scale),
         (shape(2, rows, cols), shape(2, rows, cols), shape(dp_count, 4, cols)),
         *blocks,
         normed,
         lead,
-        diag,
-        diag_sib,
+        stats,
         flops=work,
         scratch=[pltpu.VMEM((2, CORES * rows, half), bf16)],
     )
@@ -308,7 +313,7 @@
         send(other, TO_CORE),
         lead,
         sums,
-        spread,
+        stats,
     )
 
 

time: 117 us -> 112 us (0.957)
  waiting for transfers between devices: 43.7 us -> 40.4 us
  starting transfers between devices: 53.7 us -> 51.7 us
    ppermute x27 -> x26, waiting for transfers between devices: 43.7 us -> 40.4 us  [send(): return lax.ppermute(x, axis, to)]
    ppermute x27 -> x26, starting transfers between devices: 53.7 us -> 51.7 us  [send(): return lax.ppermute(x, axis, to)]
  transfers between devices with their start and end apart: 27 -> 26, of which waited for: 12 -> 12; matrix products, arithmetic and copies ran while one was open for 0% -> 0% of each run, Pallas kernels for 2% -> 3%
where the time goes in v4:
time: 112 us
  starting transfers between devices  51.7 us (46%)
  waiting for transfers between devices  40.4 us (36%)
  blocking collectives  9.85 us (9%)
  Pallas kernels  8.24 us (7%)
  other arithmetic  1.13 us (1%)
    ppermute x26, starting transfers between devices, send(): return lax.ppermute(x, axis, to)  51.7 us
    ppermute x26, waiting for transfers between devices, send(): return lax.ppermute(x, axis, to)  40.4 us
    all_to_all x1, blocking collectives, on_device(): sums = lax.all_to_all(sums, 'dp', 0, 0)  9.85 us
    pallas_call x8, Pallas kernels, call(): pl.pallas_call(body, out_shape=outs, in_specs=[pl.BlockSpec(memory_space=...  8.24 us
  transfers between devices with their start and end apart: 26, of which 12 were waited for; matrix products, arithmetic and copies ran while one was open for 0% of the time, Pallas kernels for 3%

profile of v4, /device:TPU:1, one launch (start us, length us, event | category | flops | bytes accessed | tf_op | source)
XLA Modules:
  0.0 112.1 jit_solution(15403455492472055434)
XLA Ops:
  0.6 1.1 pad_maximum_fusion.refs_2_
  1.7 3.6 %collective-permute-start.2 = (bf16[2,128,1024]{2,1,0:T(8,128)(2,1)S(1)}, bf16[2,128,1024]{2,1,0:T(8,128)(2,1)S(1)}, u32[]{:S(2)}, u32[]{:S(2)}) collective-permute-start(bf16[2,128,1024]{2,1,0:T(8,128)(2,1)S(1)} %pad_maximum_fusion.refs_2_), channel_id=1, source_target_pairs={{0,96},{16,112},{32,0},{48,16},{64,32},{80,48},{96,64},{112,80},{1... | collective-permute-start | bytes 1572872 | tf_op jit(solution)/shard_map/ppermute | solution.py:45
  5.4 1.2 %collective-permute-start.4 = (bf16[2,128,1024]{2,1,0:T(8,128)(2,1)S(1)}, bf16[2,128,1024]{2,1,0:T(8,128)(2,1)S(1)}, u32[]{:S(2)}, u32[]{:S(2)}) collective-permute-start(bf16[2,128,1024]{2,1,0:T(8,128)(2,1)S(1)} %pad_maximum_fusion.refs_2_), channel_id=1, source_target_pairs={{0,128},{16,144},{32,160},{48,176},{64,192},{80,208},{96,224},{112... | collective-permute-start | bytes 1572872 | tf_op jit(solution)/shard_map/ppermute | solution.py:45
  6.6 9.4 %collective-permute-done.2.refs_4_ = bf16[2,128,1024]{2,1,0:T(8,128)(2,1)S(1)} collective-permute-done((bf16[2,128,1024]{2,1,0:T(8,128)(2,1)S(1)}, bf16[2,128,1024]{2,1,0:T(8,128)(2,1)S(1)}, u32[]{:S(2)}, u32[]{:S(2)}) %collective-permute-start.2) | collective-permute-done | bytes 524320 | tf_op jit(solution)/shard_map/ppermute | solution.py:45
  16.0 3.5 %collective-permute-start.3 = (bf16[128,1024]{1,0:T(8,128)(2,1)S(1)}, bf16[128,1024]{1,0:T(8,128)(2,1)S(1)}, u32[]{:S(2)}, u32[]{:S(2)}) collective-permute-start(bf16[128,1024]{1,0:T(8,128)(2,1)S(1)} %slice_bitcast_fusion), channel_id=1, source_target_pairs={{0,96},{16,112},{32,0},{48,16},{64,32},{80,48},{96,64},{112,80},{1... | collective-permute-start | bytes 786440 | tf_op jit(solution)/shard_map/ppermute | solution.py:45
  19.5 0.1 collective-permute-start.1
  19.6 2.7 %collective-permute-start.6 = (bf16[2,128,1024]{2,1,0:T(8,128)(2,1)S(1)}, bf16[2,128,1024]{2,1,0:T(8,128)(2,1)S(1)}, u32[]{:S(2)}, u32[]{:S(2)}) collective-permute-start(bf16[2,128,1024]{2,1,0:T(8,128)(2,1)S(1)} %collective-permute-done.4.refs_5_), channel_id=1, source_target_pairs={{0,96},{16,112},{32,0},{48,16},{64,32},{80,48},{96,64},{112,80},{1... | collective-permute-start | bytes 1572872 | tf_op jit(solution)/shard_map/ppermute | solution.py:45
  22.2 0.0 collective-permute-start.5
  22.2 1.3 %collective-permute-done.3.refs_1_ = bf16[128,1024]{1,0:T(8,128)(2,1)S(1)} collective-permute-done((bf16[128,1024]{1,0:T(8,128)(2,1)S(1)}, bf16[128,1024]{1,0:T(8,128)(2,1)S(1)}, u32[]{:S(2)}, u32[]{:S(2)}) %collective-permute-start.3) | collective-permute-done | bytes 262176 | tf_op jit(solution)/shard_map/ppermute | solution.py:45
  23.5 3.2 %collective-permute-done.1.refs_0_ = bf16[128,1024]{1,0:T(8,128)(2,1)S(1)} collective-permute-done((bf16[128,1024]{1,0:T(8,128)(2,1)S(1)}, bf16[128,1024]{1,0:T(8,128)(2,1)S(1)}, u32[]{:S(2)}, u32[]{:S(2)}) %collective-permute-start.1) | collective-permute-done | bytes 262176 | tf_op jit(solution)/shard_map/ppermute | solution.py:45
  26.7 0.1 pad_maximum_fusion.1
  26.8 1.3 %collective-permute-start.7 = (bf16[2,128,1024]{2,1,0:T(8,128)(2,1)S(1)}, bf16[2,128,1024]{2,1,0:T(8,128)(2,1)S(1)}, u32[]{:S(2)}, u32[]{:S(2)}) collective-permute-start(bf16[2,128,1024]{2,1,0:T(8,128)(2,1)S(1)} %pad_maximum_fusion.1), channel_id=1, source_target_pairs={{0,128},{16,144},{32,160},{48,176},{64,192},{80,208},{96,224},{112... | collective-permute-start | bytes 1572872 | tf_op jit(solution)/shard_map/ppermute | solution.py:45
  28.1 5.4 %collective-permute-start.9 = (bf16[2,128,1024]{2,1,0:T(8,128)(2,1)S(1)}, bf16[2,128,1024]{2,1,0:T(8,128)(2,1)S(1)}, u32[]{:S(2)}, u32[]{:S(2)}) collective-permute-start(bf16[2,128,1024]{2,1,0:T(8,128)(2,1)S(1)} %pad_maximum_fusion.refs_2_), channel_id=1, source_target_pairs={{0,16},{16,0},{32,48},{48,32},{64,80},{80,64},{96,112},{112,96},{1... | collective-permute-start | bytes 1572872 | tf_op jit(solution)/shard_map/ppermute | solution.py:45
  33.5 1.9 %shard_map.41.early = f32[5,1024]{1,0:T(8,128)S(1)} custom-call(bf16[128,1024]{1,0:T(8,128)(2,1)S(1)} %collective-permute-done.1.refs_0_, bf16[128,1024]{1,0:T(8,128)(2,1)S(1)} %collective-permute-done.3.refs_1_, bf16[2,128,1024]{2,1,0:T(8,128)(2,1)S(1)} %pad_maximum_fusion.refs_2_, bf16[2,128,1024]{2,1,0:T(8,128)(2,1)S(1)} %collective-permute-done.refs_3_, ...), custom_call_target="tpu_custom_call" | custom-call | bytes 2641920 | tf_op jit(solution)/shard_map/pallas_call | solution.py:52
  35.4 2.6 %collective-permute-done.5.refs_0_.refs_6_ = bf16[2,128,1024]{2,1,0:T(8,128)(2,1)S(1)} collective-permute-done((bf16[2,128,1024]{2,1,0:T(8,128)(2,1)S(1)}, bf16[2,128,1024]{2,1,0:T(8,128)(2,1)S(1)}, u32[]{:S(2)}, u32[]{:S(2)}) %collective-permute-start.5) | collective-permute-done | bytes 524320 | tf_op jit(solution)/shard_map/ppermute | solution.py:45
  38.0 0.0 collective-permute-done.7.refs_2_.refs_8_
  38.0 1.2 %shard_map.42.own_m = f32[5,1024]{1,0:T(8,128)S(1)} custom-call(f32[5,1024]{1,0:T(8,128)S(1)} %shard_map.41.early, bf16[2,128,1024]{2,1,0:T(8,128)(2,1)S(1)} %collective-permute-done.5.refs_0_.refs_6_, bf16[2,128,1024]{2,1,0:T(8,128)(2,1)S(1)} %collective-permute-done.6.refs_1_.refs_7_, bf16[2,128,1024]{2,1,0:T(8,128)(2,1)S(1)} %collective-permute-done.7.refs_2_.refs_8_), custom_call_target="tpu_custom_call" | custom-call | bytes 1613824 | tf_op jit(solution)/shard_map/pallas_call | solution.py:52
  39.1 3.5 %collective-permute-start.8 = (f32[5,1024]{1,0:T(8,128)S(1)}, f32[5,1024]{1,0:T(8,128)S(1)}, u32[]{:S(2)}, u32[]{:S(2)}) collective-permute-start(f32[5,1024]{1,0:T(8,128)S(1)} %shard_map.42.own_m), channel_id=1, source_target_pairs={{0,16},{16,0},{32,48},{48,32},{64,80},{80,64},{96,112},{112,96},{1... | collective-permute-start | bytes 61448 | tf_op jit(solution)/shard_map/ppermute | solution.py:45
  42.7 0.9 collective-permute-done.8.sib_m
  43.5 2.4 %shard_map.43 = (bf16[2,256,1024]{2,1,0:T(8,128)(2,1)S(1)}, bf16[2,1024,1024]{2,1,0:T(8,128)(2,1)S(1)}, f32[3,1024]{1,0:T(4,128)S(1)}, bf16[2,2,16,1024]{3,2,1,0...) custom-call(f32[5,1024]{1,0:T(8,128)S(1)} %shard_map.42.own_m, ...), custom_call_target="tpu_custom_call" | custom-call | flops 1073741824 | bytes 11063296 | tf_op jit(solution)/shard_map/pallas_call | solution.py:52
  46.0 1.7 %collective-permute-start.10 = (bf16[2,2,2,16,1024]{4,3,2,1,0:T(8,128)(2,1)S(1)}, bf16[2,2,2,16,1024]{4,3,2,1,0:T(8,128)(2,1)S(1)}, u32[]{:S(2)}, u32[]{:S(2)}) collective-permute-start(bf16[2,2,2,16,1024]{4,3,2,1,0:T(8,128)(2,1)S(1)} %get-tuple-element.18), channel_id=1, source_target_pairs={{0,1},{1,2},{2,3},{3,4},{4,5},{5,6},{6,7},{7,0},{8,9},{9,10},{10,1... | collective-permute-start | bytes 786440 | tf_op jit(solution)/shard_map/ppermute | solution.py:45
  47.7 4.0 %collective-permute-start.11 = (bf16[2,2,2,16,1024]{4,3,2,1,0:T(8,128)(2,1)S(1)}, bf16[2,2,2,16,1024]{4,3,2,1,0:T(8,128)(2,1)S(1)}, u32[]{:S(2)}, u32[]{:S(2)}) collective-permute-start(bf16[2,2,2,16,1024]{4,3,2,1,0:T(8,128)(2,1)S(1)} %get-tuple-element.19), channel_id=1, source_target_pairs={{0,7},{1,0},{2,1},{3,2},{4,3},{5,4},{6,5},{7,6},{8,15},{9,8},{10,9... | collective-permute-start | bytes 786440 | tf_op jit(solution)/shard_map/ppermute | solution.py:45
  51.7 0.0 collective-permute-start.12
  51.7 3.6 %collective-permute-start.13 = (bf16[2,16,1024]{2,1,0:T(8,128)(2,1)S(1)}, bf16[2,16,1024]{2,1,0:T(8,128)(2,1)S(1)}, u32[]{:S(2)}, u32[]{:S(2)}) collective-permute-start(bf16[2,16,1024]{2,1,0:T(8,128)(2,1)S(1)} %get-tuple-element.21), channel_id=1, source_target_pairs={{0,6},{1,7},{2,0},{3,1},{4,2},{5,3},{6,4},{7,5},{8,14},{9,15},{10,... | collective-permute-start | bytes 196616 | tf_op jit(solution)/shard_map/ppermute | solution.py:45
  55.3 5.2 %collective-permute-done.12.half_a = bf16[2,16,1024]{2,1,0:T(8,128)(2,1)S(1)} collective-permute-done((bf16[2,16,1024]{2,1,0:T(8,128)(2,1)S(1)}, bf16[2,16,1024]{2,1,0:T(8,128)(2,1)S(1)}, u32[]{:S(2)}, u32[]{:S(2)}) %collective-permute-start.12) | collective-permute-done | bytes 65568 | tf_op jit(solution)/shard_map/ppermute | solution.py:45
  60.5 0.0 collective-permute-done.13.half_b
  60.5 0.1 shard_map.44
  60.6 3.8 %collective-permute-start.14 = (bf16[2,2,16,1024]{3,2,1,0:T(8,128)(2,1)S(1)}, bf16[2,2,16,1024]{3,2,1,0:T(8,128)(2,1)S(1)}, u32[]{:S(2)}, u32[]{:S(2)}) collective-permute-start(bf16[2,2,16,1024]{3,2,1,0:T(8,128)(2,1)S(1)} %get-tuple-element.24), channel_id=1, source_target_pairs={{0,2},{1,3},{2,4},{3,5},{4,6},{5,7},{6,0},{7,1},{8,10},{9,11},{10,... | collective-permute-start | bytes 393224 | tf_op jit(solution)/shard_map/ppermute | solution.py:45
  64.4 5.4 %collective-permute-done.14.far_up = bf16[2,2,16,1024]{3,2,1,0:T(8,128)(2,1)S(1)} collective-permute-done((bf16[2,2,16,1024]{3,2,1,0:T(8,128)(2,1)S(1)}, bf16[2,2,16,1024]{3,2,1,0:T(8,128)(2,1)S(1)}, u32[]{:S(2)}, u32[]{:S(2)}) %collective-permute-start.14) | collective-permute-done | bytes 131104 | tf_op jit(solution)/shard_map/ppermute | solution.py:45
  69.7 0.1 shard_map.45.a
  69.8 2.9 %collective-permute-start.16 = (bf16[2,2,16,1024]{3,2,1,0:T(8,128)(2,1)S(1)}, bf16[2,2,16,1024]{3,2,1,0:T(8,128)(2,1)S(1)}, u32[]{:S(2)}, u32[]{:S(2)}) collective-permute-start(bf16[2,2,16,1024]{3,2,1,0:T(8,128)(2,1)S(1)} %shard_map.45.a), channel_id=1, source_target_pairs={{0,8},{1,9},{2,10},{3,11},{4,12},{5,13},{6,14},{7,15},{8,0},{9,1},... | collective-permute-start | bytes 393224 | tf_op jit(solution)/shard_map/ppermute | solution.py:45
  72.7 2.5 %collective-permute-done.16.b = bf16[2,2,16,1024]{3,2,1,0:T(8,128)(2,1)S(1)} collective-permute-done((bf16[2,2,16,1024]{3,2,1,0:T(8,128)(2,1)S(1)}, bf16[2,2,16,1024]{3,2,1,0:T(8,128)(2,1)S(1)}, u32[]{:S(2)}, u32[]{:S(2)}) %collective-permute-start.16) | collective-permute-done | bytes 131104 | tf_op jit(solution)/shard_map/ppermute | solution.py:45
  75.3 3.5 %collective-permute-start.20 = (bf16[2,2,16,1024]{3,2,1,0:T(8,128)(2,1)S(1)}, bf16[2,2,16,1024]{3,2,1,0:T(8,128)(2,1)S(1)}, u32[]{:S(2)}, u32[]{:S(2)}) collective-permute-start(bf16[2,2,16,1024]{3,2,1,0:T(8,128)(2,1)S(1)} %shard_map.46.refs_0_), channel_id=1, source_target_pairs={{0,6},{1,7},{2,0},{3,1},{4,2},{5,3},{6,4},{7,5},{8,14},{9,15},{10,... | collective-permute-start | bytes 393224 | tf_op jit(solution)/shard_map/ppermute | solution.py:45
  78.8 1.2 %collective-permute-start.22 = (bf16[2,2,16,1024]{3,2,1,0:T(8,128)(2,1)S(1)}, bf16[2,2,16,1024]{3,2,1,0:T(8,128)(2,1)S(1)}, u32[]{:S(2)}, u32[]{:S(2)}) collective-permute-start(bf16[2,2,16,1024]{3,2,1,0:T(8,128)(2,1)S(1)} %shard_map.46.refs_0_), channel_id=1, source_target_pairs={{0,7},{1,0},{2,1},{3,2},{4,3},{5,4},{6,5},{7,6},{8,15},{9,8},{10,9... | collective-permute-start | bytes 393224 | tf_op jit(solution)/shard_map/ppermute | solution.py:45
  80.0 0.0 collective-permute-start.18
  80.0 0.2 collective-permute-start.17
  80.2 1.3 %collective-permute-done.20.refs_5_ = bf16[2,2,16,1024]{3,2,1,0:T(8,128)(2,1)S(1)} collective-permute-done((bf16[2,2,16,1024]{3,2,1,0:T(8,128)(2,1)S(1)}, bf16[2,2,16,1024]{3,2,1,0:T(8,128)(2,1)S(1)}, u32[]{:S(2)}, u32[]{:S(2)}) %collective-permute-start.20) | collective-permute-done | bytes 131104 | tf_op jit(solution)/shard_map/ppermute | solution.py:45
  81.5 3.3 %collective-permute-start.24 = (bf16[2,16,1024]{2,1,0:T(8,128)(2,1)S(1)}, bf16[2,16,1024]{2,1,0:T(8,128)(2,1)S(1)}, u32[]{:S(2)}, u32[]{:S(2)}) collective-permute-start(bf16[2,16,1024]{2,1,0:T(8,128)(2,1)S(1)} %slice_bitcast_fusion.2), channel_id=1, source_target_pairs={{0,6},{1,7},{2,0},{3,1},{4,2},{5,3},{6,4},{7,5},{8,14},{9,15},{10,... | collective-permute-start | bytes 196616 | tf_op jit(solution)/shard_map/ppermute | solution.py:45
  84.8 1.7 %collective-permute-start.21 = (bf16[2,2,16,1024]{3,2,1,0:T(8,128)(2,1)S(1)}, bf16[2,2,16,1024]{3,2,1,0:T(8,128)(2,1)S(1)}, u32[]{:S(2)}, u32[]{:S(2)}) collective-permute-start(bf16[2,2,16,1024]{3,2,1,0:T(8,128)(2,1)S(1)} %collective-permute-done.20.refs_5_), channel_id=1, source_target_pairs={{0,7},{1,0},{2,1},{3,2},{4,3},{5,4},{6,5},{7,6},{8,15},{9,8},{10,9... | collective-permute-start | bytes 393224 | tf_op jit(solution)/shard_map/ppermute | solution.py:45
  86.5 0.5 collective-permute-done.18.refs_2_
  87.1 0.1 collective-permute-start.23
  87.2 0.8 collective-permute-done.17.refs_1_
  87.9 0.0 collective-permute-done.24.refs_8_
  88.0 7.5 %collective-permute-done.23.refs_7_ = bf16[2,16,1024]{2,1,0:T(8,128)(2,1)S(1)} collective-permute-done((bf16[2,16,1024]{2,1,0:T(8,128)(2,1)S(1)}, bf16[2,16,1024]{2,1,0:T(8,128)(2,1)S(1)}, u32[]{:S(2)}, u32[]{:S(2)}) %collective-permute-start.23) | collective-permute-done | bytes 65568 | tf_op jit(solution)/shard_map/ppermute | solution.py:45
  95.4 1.6 %shard_map.47 = (f32[2,128,1024]{2,1,0:T(8,128)S(1)}, f32[2,128,1024]{2,1,0:T(8,128)S(1)}, f32[16,4,1024]{2,1,0:T(4,128)S(1)}) custom-call(bf16[2,2,16,1024]{3,2,1,0:T(8,128)(2,1)S(1)} %shard_map.46.refs_0_, bf16[2,2,16,1024]{3,2,1,0:T(8,128)(2,1)S(1)} %collective-permute-done.17.refs_1_, bf16[2,2,16,1024]{3,2,1,0:T(8,128)(2,1)S(1)} %collective-permute-done.18.refs_2_, ...), custom_call_target="tpu_custom_call" | custom-call | flops 1073741824 | bytes 8663040 | tf_op jit(solution)/shard_map/pallas_call | solution.py:52
  97.0 4.3 %collective-permute-start.25 = (f32[2,128,1024]{2,1,0:T(8,128)S(1)}, f32[2,128,1024]{2,1,0:T(8,128)S(1)}, u32[]{:S(2)}, u32[]{:S(2)}) collective-permute-start(f32[2,128,1024]{2,1,0:T(8,128)S(1)} %get-tuple-element.30), channel_id=1, source_target_pairs={{0,16},{16,0},{32,48},{48,32},{64,80},{80,64},{96,112},{112,96},{1... | collective-permute-start | bytes 3145736 | tf_op jit(solution)/shard_map/ppermute | solution.py:45
  101.3 9.8 %all_to_all.5.sums = f32[16,4,1024]{2,1,0:T(4,128)S(1)} all-to-all(f32[16,4,1024]{2,1,0:T(4,128)S(1)} %get-tuple-element.31), channel_id=1, replica_groups=mesh['dp'=16,'feat'=16] {'dp'}, dimensions={0} | all-to-all | bytes 524288 | tf_op jit(solution)/shard_map/all_to_all | solution.py:308
  111.2 1.0 shard_map.48
  (19 shorter events, 0.1 us)
Async XLA Ops:
  1.7 14.2 %collective-permute-start.2 = (bf16[2,128,1024]{2,1,0:T(8,128)(2,1)S(1)}, bf16[2,128,1024]{2,1,0:T(8,128)(2,1)S(1)}, u32[]{:S(2)}, u32[]{:S(2)}) collective-permute-start(bf16[2,128,1024]{2,1,0:T(8,128)(2,1)S(1)} %pad_maximum_fusion.refs_2_), channel_id=1, source_target_pairs={{0,96},{16,112},{32,0},{48,16},{64,32},{80,48},{96,64},{112,80},{1... | collective-permute-start | bytes 1572872 | tf_op jit(solution)/shard_map/ppermute | solution.py:45
  5.4 14.1 %collective-permute-start = (bf16[2,128,1024]{2,1,0:T(8,128)(2,1)S(1)}, bf16[2,128,1024]{2,1,0:T(8,128)(2,1)S(1)}, u32[]{:S(2)}, u32[]{:S(2)}) collective-permute-start(bf16[2,128,1024]{2,1,0:T(8,128)(2,1)S(1)} %pad_maximum_fusion.refs_2_), channel_id=1, source_target_pairs={{0,32},{16,48},{32,64},{48,80},{64,96},{80,112},{96,0},{112,16},{1... | collective-permute-start | bytes 1572872 | tf_op jit(solution)/shard_map/ppermute | solution.py:45
  5.4 14.2 %collective-permute-start.4 = (bf16[2,128,1024]{2,1,0:T(8,128)(2,1)S(1)}, bf16[2,128,1024]{2,1,0:T(8,128)(2,1)S(1)}, u32[]{:S(2)}, u32[]{:S(2)}) collective-permute-start(bf16[2,128,1024]{2,1,0:T(8,128)(2,1)S(1)} %pad_maximum_fusion.refs_2_), channel_id=1, source_target_pairs={{0,128},{16,144},{32,160},{48,176},{64,192},{80,208},{96,224},{112... | collective-permute-start | bytes 1572872 | tf_op jit(solution)/shard_map/ppermute | solution.py:45
  16.0 7.5 %collective-permute-start.3 = (bf16[128,1024]{1,0:T(8,128)(2,1)S(1)}, bf16[128,1024]{1,0:T(8,128)(2,1)S(1)}, u32[]{:S(2)}, u32[]{:S(2)}) collective-permute-start(bf16[128,1024]{1,0:T(8,128)(2,1)S(1)} %slice_bitcast_fusion), channel_id=1, source_target_pairs={{0,96},{16,112},{32,0},{48,16},{64,32},{80,48},{96,64},{112,80},{1... | collective-permute-start | bytes 786440 | tf_op jit(solution)/shard_map/ppermute | solution.py:45
  19.5 7.3 %collective-permute-start.1 = (bf16[128,1024]{1,0:T(8,128)(2,1)S(1)}, bf16[128,1024]{1,0:T(8,128)(2,1)S(1)}, u32[]{:S(2)}, u32[]{:S(2)}) collective-permute-start(bf16[128,1024]{1,0:T(8,128)(2,1)S(1)} %slice_bitcast_fusion.1), channel_id=1, source_target_pairs={{0,32},{16,48},{32,64},{48,80},{64,96},{80,112},{96,0},{112,16},{1... | collective-permute-start | bytes 786440 | tf_op jit(solution)/shard_map/ppermute | solution.py:45
  19.6 15.8 %collective-permute-start.6 = (bf16[2,128,1024]{2,1,0:T(8,128)(2,1)S(1)}, bf16[2,128,1024]{2,1,0:T(8,128)(2,1)S(1)}, u32[]{:S(2)}, u32[]{:S(2)}) collective-permute-start(bf16[2,128,1024]{2,1,0:T(8,128)(2,1)S(1)} %collective-permute-done.4.refs_5_), channel_id=1, source_target_pairs={{0,96},{16,112},{32,0},{48,16},{64,32},{80,48},{96,64},{112,80},{1... | collective-permute-start | bytes 1572872 | tf_op jit(solution)/shard_map/ppermute | solution.py:45
  22.2 15.7 %collective-permute-start.5 = (bf16[2,128,1024]{2,1,0:T(8,128)(2,1)S(1)}, bf16[2,128,1024]{2,1,0:T(8,128)(2,1)S(1)}, u32[]{:S(2)}, u32[]{:S(2)}) collective-permute-start(bf16[2,128,1024]{2,1,0:T(8,128)(2,1)S(1)} %collective-permute-done.4.refs_5_), channel_id=1, source_target_pairs={{0,32},{16,48},{32,64},{48,80},{64,96},{80,112},{96,0},{112,16},{1... | collective-permute-start | bytes 1572872 | tf_op jit(solution)/shard_map/ppermute | solution.py:45
  26.8 11.2 %collective-permute-start.7 = (bf16[2,128,1024]{2,1,0:T(8,128)(2,1)S(1)}, bf16[2,128,1024]{2,1,0:T(8,128)(2,1)S(1)}, u32[]{:S(2)}, u32[]{:S(2)}) collective-permute-start(bf16[2,128,1024]{2,1,0:T(8,128)(2,1)S(1)} %pad_maximum_fusion.1), channel_id=1, source_target_pairs={{0,128},{16,144},{32,160},{48,176},{64,192},{80,208},{96,224},{112... | collective-permute-start | bytes 1572872 | tf_op jit(solution)/shard_map/ppermute | solution.py:45
  28.1 14.6 %collective-permute-start.9 = (bf16[2,128,1024]{2,1,0:T(8,128)(2,1)S(1)}, bf16[2,128,1024]{2,1,0:T(8,128)(2,1)S(1)}, u32[]{:S(2)}, u32[]{:S(2)}) collective-permute-start(bf16[2,128,1024]{2,1,0:T(8,128)(2,1)S(1)} %pad_maximum_fusion.refs_2_), channel_id=1, source_target_pairs={{0,16},{16,0},{32,48},{48,32},{64,80},{80,64},{96,112},{112,96},{1... | collective-permute-start | bytes 1572872 | tf_op jit(solution)/shard_map/ppermute | solution.py:45
  39.1 4.4 %collective-permute-start.8 = (f32[5,1024]{1,0:T(8,128)S(1)}, f32[5,1024]{1,0:T(8,128)S(1)}, u32[]{:S(2)}, u32[]{:S(2)}) collective-permute-start(f32[5,1024]{1,0:T(8,128)S(1)} %shard_map.42.own_m), channel_id=1, source_target_pairs={{0,16},{16,0},{32,48},{48,32},{64,80},{80,64},{96,112},{112,96},{1... | collective-permute-start | bytes 61448 | tf_op jit(solution)/shard_map/ppermute | solution.py:45
  46.0 14.5 %collective-permute-start.10 = (bf16[2,2,2,16,1024]{4,3,2,1,0:T(8,128)(2,1)S(1)}, bf16[2,2,2,16,1024]{4,3,2,1,0:T(8,128)(2,1)S(1)}, u32[]{:S(2)}, u32[]{:S(2)}) collective-permute-start(bf16[2,2,2,16,1024]{4,3,2,1,0:T(8,128)(2,1)S(1)} %get-tuple-element.18), channel_id=1, source_target_pairs={{0,1},{1,2},{2,3},{3,4},{4,5},{5,6},{6,7},{7,0},{8,9},{9,10},{10,1... | collective-permute-start | bytes 786440 | tf_op jit(solution)/shard_map/ppermute | solution.py:45
  47.7 12.8 %collective-permute-start.11 = (bf16[2,2,2,16,1024]{4,3,2,1,0:T(8,128)(2,1)S(1)}, bf16[2,2,2,16,1024]{4,3,2,1,0:T(8,128)(2,1)S(1)}, u32[]{:S(2)}, u32[]{:S(2)}) collective-permute-start(bf16[2,2,2,16,1024]{4,3,2,1,0:T(8,128)(2,1)S(1)} %get-tuple-element.19), channel_id=1, source_target_pairs={{0,7},{1,0},{2,1},{3,2},{4,3},{5,4},{6,5},{7,6},{8,15},{9,8},{10,9... | collective-permute-start | bytes 786440 | tf_op jit(solution)/shard_map/ppermute | solution.py:45
  51.7 8.7 %collective-permute-start.12 = (bf16[2,16,1024]{2,1,0:T(8,128)(2,1)S(1)}, bf16[2,16,1024]{2,1,0:T(8,128)(2,1)S(1)}, u32[]{:S(2)}, u32[]{:S(2)}) collective-permute-start(bf16[2,16,1024]{2,1,0:T(8,128)(2,1)S(1)} %get-tuple-element.20), channel_id=1, source_target_pairs={{0,2},{1,3},{2,4},{3,5},{4,6},{5,7},{6,0},{7,1},{8,10},{9,11},{10,... | collective-permute-start | bytes 196616 | tf_op jit(solution)/shard_map/ppermute | solution.py:45
  51.7 8.7 %collective-permute-start.13 = (bf16[2,16,1024]{2,1,0:T(8,128)(2,1)S(1)}, bf16[2,16,1024]{2,1,0:T(8,128)(2,1)S(1)}, u32[]{:S(2)}, u32[]{:S(2)}) collective-permute-start(bf16[2,16,1024]{2,1,0:T(8,128)(2,1)S(1)} %get-tuple-element.21), channel_id=1, source_target_pairs={{0,6},{1,7},{2,0},{3,1},{4,2},{5,3},{6,4},{7,5},{8,14},{9,15},{10,... | collective-permute-start | bytes 196616 | tf_op jit(solution)/shard_map/ppermute | solution.py:45
  60.6 9.2 %collective-permute-start.14 = (bf16[2,2,16,1024]{3,2,1,0:T(8,128)(2,1)S(1)}, bf16[2,2,16,1024]{3,2,1,0:T(8,128)(2,1)S(1)}, u32[]{:S(2)}, u32[]{:S(2)}) collective-permute-start(bf16[2,2,16,1024]{3,2,1,0:T(8,128)(2,1)S(1)} %get-tuple-element.24), channel_id=1, source_target_pairs={{0,2},{1,3},{2,4},{3,5},{4,6},{5,7},{6,0},{7,1},{8,10},{9,11},{10,... | collective-permute-start | bytes 393224 | tf_op jit(solution)/shard_map/ppermute | solution.py:45
  64.4 5.4 %collective-permute-start.15 = (bf16[2,2,16,1024]{3,2,1,0:T(8,128)(2,1)S(1)}, bf16[2,2,16,1024]{3,2,1,0:T(8,128)(2,1)S(1)}, u32[]{:S(2)}, u32[]{:S(2)}) collective-permute-start(bf16[2,2,16,1024]{3,2,1,0:T(8,128)(2,1)S(1)} %get-tuple-element.25), channel_id=1, source_target_pairs={{0,6},{1,7},{2,0},{3,1},{4,2},{5,3},{6,4},{7,5},{8,14},{9,15},{10,... | collective-permute-start | bytes 393224 | tf_op jit(solution)/shard_map/ppermute | solution.py:45
  69.8 5.4 %collective-permute-start.16 = (bf16[2,2,16,1024]{3,2,1,0:T(8,128)(2,1)S(1)}, bf16[2,2,16,1024]{3,2,1,0:T(8,128)(2,1)S(1)}, u32[]{:S(2)}, u32[]{:S(2)}) collective-permute-start(bf16[2,2,16,1024]{3,2,1,0:T(8,128)(2,1)S(1)} %shard_map.45.a), channel_id=1, source_target_pairs={{0,8},{1,9},{2,10},{3,11},{4,12},{5,13},{6,14},{7,15},{8,0},{9,1},... | collective-permute-start | bytes 393224 | tf_op jit(solution)/shard_map/ppermute | solution.py:45
  75.3 6.2 %collective-permute-start.20 = (bf16[2,2,16,1024]{3,2,1,0:T(8,128)(2,1)S(1)}, bf16[2,2,16,1024]{3,2,1,0:T(8,128)(2,1)S(1)}, u32[]{:S(2)}, u32[]{:S(2)}) collective-permute-start(bf16[2,2,16,1024]{3,2,1,0:T(8,128)(2,1)S(1)} %shard_map.46.refs_0_), channel_id=1, source_target_pairs={{0,6},{1,7},{2,0},{3,1},{4,2},{5,3},{6,4},{7,5},{8,14},{9,15},{10,... | collective-permute-start | bytes 393224 | tf_op jit(solution)/shard_map/ppermute | solution.py:45
  78.8 8.3 %collective-permute-start.22 = (bf16[2,2,16,1024]{3,2,1,0:T(8,128)(2,1)S(1)}, bf16[2,2,16,1024]{3,2,1,0:T(8,128)(2,1)S(1)}, u32[]{:S(2)}, u32[]{:S(2)}) collective-permute-start(bf16[2,2,16,1024]{3,2,1,0:T(8,128)(2,1)S(1)} %shard_map.46.refs_0_), channel_id=1, source_target_pairs={{0,7},{1,0},{2,1},{3,2},{4,3},{5,4},{6,5},{7,6},{8,15},{9,8},{10,9... | collective-permute-start | bytes 393224 | tf_op jit(solution)/shard_map/ppermute | solution.py:45
  80.0 7.0 %collective-permute-start.18 = (bf16[2,2,16,1024]{3,2,1,0:T(8,128)(2,1)S(1)}, bf16[2,2,16,1024]{3,2,1,0:T(8,128)(2,1)S(1)}, u32[]{:S(2)}, u32[]{:S(2)}) collective-permute-start(bf16[2,2,16,1024]{3,2,1,0:T(8,128)(2,1)S(1)} %shard_map.46.refs_0_), channel_id=1, source_target_pairs={{0,2},{1,3},{2,4},{3,5},{4,6},{5,7},{6,0},{7,1},{8,10},{9,11},{10,... | collective-permute-start | bytes 393224 | tf_op jit(solution)/shard_map/ppermute | solution.py:45
  80.0 7.9 %collective-permute-start.17 = (bf16[2,2,16,1024]{3,2,1,0:T(8,128)(2,1)S(1)}, bf16[2,2,16,1024]{3,2,1,0:T(8,128)(2,1)S(1)}, u32[]{:S(2)}, u32[]{:S(2)}) collective-permute-start(bf16[2,2,16,1024]{3,2,1,0:T(8,128)(2,1)S(1)} %shard_map.46.refs_0_), channel_id=1, source_target_pairs={{0,1},{1,2},{2,3},{3,4},{4,5},{5,6},{6,7},{7,0},{8,9},{9,10},{10,1... | collective-permute-start | bytes 393224 | tf_op jit(solution)/shard_map/ppermute | solution.py:45
  81.5 6.4 %collective-permute-start.24 = (bf16[2,16,1024]{2,1,0:T(8,128)(2,1)S(1)}, bf16[2,16,1024]{2,1,0:T(8,128)(2,1)S(1)}, u32[]{:S(2)}, u32[]{:S(2)}) collective-permute-start(bf16[2,16,1024]{2,1,0:T(8,128)(2,1)S(1)} %slice_bitcast_fusion.2), channel_id=1, source_target_pairs={{0,6},{1,7},{2,0},{3,1},{4,2},{5,3},{6,4},{7,5},{8,14},{9,15},{10,... | collective-permute-start | bytes 196616 | tf_op jit(solution)/shard_map/ppermute | solution.py:45
  84.8 10.6 %collective-permute-start.21 = (bf16[2,2,16,1024]{3,2,1,0:T(8,128)(2,1)S(1)}, bf16[2,2,16,1024]{3,2,1,0:T(8,128)(2,1)S(1)}, u32[]{:S(2)}, u32[]{:S(2)}) collective-permute-start(bf16[2,2,16,1024]{3,2,1,0:T(8,128)(2,1)S(1)} %collective-permute-done.20.refs_5_), channel_id=1, source_target_pairs={{0,7},{1,0},{2,1},{3,2},{4,3},{5,4},{6,5},{7,6},{8,15},{9,8},{10,9... | collective-permute-start | bytes 393224 | tf_op jit(solution)/shard_map/ppermute | solution.py:45
  87.0 8.4 %collective-permute-start.19 = (bf16[2,2,16,1024]{3,2,1,0:T(8,128)(2,1)S(1)}, bf16[2,2,16,1024]{3,2,1,0:T(8,128)(2,1)S(1)}, u32[]{:S(2)}, u32[]{:S(2)}) collective-permute-start(bf16[2,2,16,1024]{3,2,1,0:T(8,128)(2,1)S(1)} %collective-permute-done.18.refs_2_), channel_id=1, source_target_pairs={{0,1},{1,2},{2,3},{3,4},{4,5},{5,6},{6,7},{7,0},{8,9},{9,10},{10,1... | collective-permute-start | bytes 393224 | tf_op jit(solution)/shard_map/ppermute | solution.py:45
  87.1 8.3 %collective-permute-start.23 = (bf16[2,16,1024]{2,1,0:T(8,128)(2,1)S(1)}, bf16[2,16,1024]{2,1,0:T(8,128)(2,1)S(1)}, u32[]{:S(2)}, u32[]{:S(2)}) collective-permute-start(bf16[2,16,1024]{2,1,0:T(8,128)(2,1)S(1)} %slice_bitcast_fusion.3), channel_id=1, source_target_pairs={{0,2},{1,3},{2,4},{3,5},{4,6},{5,7},{6,0},{7,1},{8,10},{9,11},{10,... | collective-permute-start | bytes 196616 | tf_op jit(solution)/shard_map/ppermute | solution.py:45
  97.0 14.2 %collective-permute-start.25 = (f32[2,128,1024]{2,1,0:T(8,128)S(1)}, f32[2,128,1024]{2,1,0:T(8,128)S(1)}, u32[]{:S(2)}, u32[]{:S(2)}) collective-permute-start(f32[2,128,1024]{2,1,0:T(8,128)S(1)} %get-tuple-element.30), channel_id=1, source_target_pairs={{0,16},{16,0},{32,48},{48,32},{64,80},{80,64},{96,112},{112,96},{1... | collective-permute-start | bytes 3145736 | tf_op jit(solution)/shard_map/ppermute | solution.py:45

commit v5 on v4

--- a/solution.py
+++ b/solution.py
@@ -31,6 +31,7 @@
 TO_X = dp_perm(lambda x, y, c: (1 - x, y, c))
 TO_UP = dp_perm(lambda x, y, c: (x, (y + 1) % Y, c))
 TO_DOWN = dp_perm(lambda x, y, c: (x, (y - 1) % Y, c))
+TO_UP_2 = dp_perm(lambda x, y, c: (x, (y + 2) % Y, c))
 
 
 X_HI, Z = 2, 8
@@ -68,84 +69,107 @@
     return jax.ShapeDtypeStruct(dims, dtype)
 
 
-def moments_of(pieces_a, pieces_b):
-    count = sum(p.shape[0] for p in pieces_a)
-    mean_a = sum(jnp.sum(p[...].astype(f32), 0, keepdims=True) for p in pieces_a) / count
-    mean_b = sum(jnp.sum(p[...].astype(f32), 0, keepdims=True) for p in pieces_b) / count
-    square_a = square_b = product = 0.0
-    for p, q in zip(pieces_a, pieces_b):
-        a, b = p[...].astype(f32) - mean_a, q[...].astype(f32) - mean_b
-        square_a = square_a + jnp.sum(a * a, 0, keepdims=True)
-        square_b = square_b + jnp.sum(b * b, 0, keepdims=True)
-        product = product + jnp.sum(a * b, 0, keepdims=True)
-    return count, (mean_a, mean_b, square_a, square_b, product)
-
-
-def merge(count, one, other_count, other):
-    total = count + other_count
-    gap_a, gap_b = other[0] - one[0], other[1] - one[1]
-    weight = count * other_count / total
-    return (
-        one[0] + gap_a * (other_count / total),
-        one[1] + gap_b * (other_count / total),
-        one[2] + other[2] + gap_a * gap_a * weight,
-        one[3] + other[3] + gap_b * gap_b * weight,
-        one[4] + other[4] + gap_a * gap_b * weight,
-    )
-
-
-def put_rows(out, values):
-    for i, value in enumerate(values):
-        out[i : i + 1, :] = value
-
-
-def get_rows(ref):
-    return [ref[i : i + 1, :] for i in range(ref.shape[0])]
-
-
-def early_moments_body(*refs):
-    *pieces, out = refs
-    single, stacked = pieces[:2], pieces[2:]
-    _, moments = moments_of(
-        [single[0], *(p.at[0] for p in stacked)], [single[1], *(p.at[1] for p in stacked)]
-    )
-    put_rows(out, moments)
-
-
-def late_moments_body(early_count, early, *refs):
-    *pairs, out = refs
-    count, late = moments_of([p.at[0] for p in pairs], [p.at[1] for p in pairs])
-    put_rows(out, merge(early_count, get_rows(early), count, late))
-
-
-def gram_body(batch, own_m, sib_m, sib, *refs):
-    *refs, lead, normed, stats, mine, up_2, down_2, up_1, down_1, far_a, far_b, gram = refs
-    single, stacked = refs[:2], refs[2:]
-    rows, part = sib.shape[1], mine.shape[2]
-    mean_a, mean_b, square_a, square_b, product = merge(
-        batch // 2, get_rows(own_m), batch // 2, get_rows(sib_m)
-    )
-    spreads = [jnp.sqrt(square / batch + epsilon) for square in (square_a, square_b)]
-    corr = product / (batch * spreads[0] * spreads[1])
-    put_rows(stats, (*spreads, 2.0 * (corr - 1.0) - 2.0 * off_weight * corr))
-    for v, (mean, spread) in enumerate(zip((mean_a, mean_b), spreads)):
-        view = [*(p.at[v] for p in stacked), single[v]]
-        for i, p in enumerate((view[0], sib.at[v])):
+SUB, LANE = 8, 128
+
+
+def moments_body(views, out):
+    rows = views.shape[1]
+    a, b = views[0].astype(f32), views[1].astype(f32)
+    mean_a = jnp.sum(a, 0, keepdims=True) / rows
+    mean_b = jnp.sum(b, 0, keepdims=True) / rows
+    a, b = a - mean_a, b - mean_b
+    moments = (mean_a, mean_b, *(jnp.sum(x, 0, keepdims=True) for x in (a * a, b * b, a * b)))
+    for i, value in enumerate(moments):
+        for k in range(SUB):
+            out[i * SUB + k : i * SUB + k + 1, :] = value[:, k * LANE : (k + 1) * LANE]
+
+
+def merge(rows, *parts):
+    parts = [[p[k * SUB : (k + 1) * SUB, :] for k in range(5)] for p in parts]
+    mean_a, mean_b = (sum(p[k] for p in parts) / len(parts) for k in range(2))
+    square_a, square_b, product = (sum(p[k] for p in parts) for k in range(2, 5))
+    for p in parts:
+        gap_a, gap_b = p[0] - mean_a, p[1] - mean_b
+        square_a = square_a + rows * gap_a * gap_a
+        square_b = square_b + rows * gap_b * gap_b
+        product = product + rows * gap_a * gap_b
+    return mean_a, mean_b, square_a, square_b, product
+
+
+def merge_body(rows, one, other, out):
+    for k, value in enumerate(merge(rows, one, other)):
+        out[k * SUB : (k + 1) * SUB, :] = value
+
+
+def stats_of(batch, moments, stats):
+    mean_a, mean_b, square_a, square_b, product = merge(batch // len(moments), *moments)
+    spread_a, spread_b = jnp.sqrt(square_a / batch + epsilon), jnp.sqrt(square_b / batch + epsilon)
+    corr = product / (batch * spread_a * spread_b)
+    diag = 2.0 * (corr - 1.0) - 2.0 * off_weight * corr
+    for i, value in enumerate((mean_a, mean_b, spread_a, spread_b, diag)):
+        for k in range(SUB):
+            stats[i : i + 1, k * LANE : (k + 1) * LANE] = value[k : k + 1, :]
+
+
+def normal(piece, stats, v):
+    return ((piece.astype(f32) - stats[v : v + 1, :]) / stats[2 + v : 3 + v, :]).astype(bf16)
+
+
+def multiply(lead, pieces, stats, normed, gram):
+    rows = pieces[0][0].shape[0]
+    for v in range(2):
+        for i, piece in enumerate(pieces[v]):
             r = slice(i * rows, (i + 1) * rows)
-            lead[v, r, :] = ((p[...].astype(f32) - mean) / spread).astype(bf16)
-        for i, p in enumerate(view):
-            r = slice(i * rows, (i + 1) * rows)
-            normed[v, r, :] = ((p[...].astype(f32) - mean) / spread).astype(bf16)
+            normed[v, r, :] = normal(piece[...], stats, v)
             block = lax.dot_general(
                 lead[v], normed[v, r, :], (((1,), (1,)), ((), ())), preferred_element_type=f32
             )
             gram[v, :, r] = block.astype(bf16)
+
+
+def split_views(pairs):
+    return [[p.at[v] for p in pairs] for v in range(2)]
+
+
+def stack_body(a, b, out):
+    out[0] = a[...]
+    out[1] = b[...]
+
+
+def copy_body(x, out):
+    out[...] = x[...]
+
+
+def near_body(batch, *refs):
+    *moments, sib, views, from_down, from_up, from_x, stats, lead, normed, gram = refs
+    pairs = [views, from_down, from_up, from_x]
+    rows = sib.shape[1]
+    stats_of(batch, moments, stats)
+    for v in range(2):
+        lead[v, 0:rows, :] = normal(pairs[0][v], stats, v)
+        lead[v, rows:, :] = normal(sib[v], stats, v)
+    multiply(lead, split_views(pairs), stats, normed, gram)
+
+
+def far_body(lead, stats, far_a, far_b, x_down, x_up, normed, gram):
+    pieces = split_views([x_down, x_up])
+    multiply(lead, [[far_a, *pieces[0]], [far_b, *pieces[1]]], stats, normed, gram)
+
+
+def last_body(lead, stats, x_far, gram_near, gram_far, *outs):
+    normed, mine, up_2, down_2, up_1, down_1, far_a, far_b, gram = outs
+    rows, part = x_far.shape[1], mine.shape[2]
+    near, far = gram_near.shape[2], gram_near.shape[2] + gram_far.shape[2]
+    multiply(lead, split_views([x_far]), stats, normed, gram)
     z = lax.rem(lax.axis_index("feat"), Z)
 
     def store(ahead, v, out):
         start = lax.rem(z + ahead, Z) * part
         for h in range(X_HI):
-            out[h] = gram[v, pl.ds(pl.multiple_of(start + h * rows, part), part), :]
+            r = pl.ds(pl.multiple_of(start + h * rows, part), part)
+            out[h, :, 0:near] = gram_near[v, r, :]
+            out[h, :, near:far] = gram_far[v, r, :]
+            out[h, :, far:] = gram[v, r, :]
 
     for v in range(2):
         store(0, v, mine.at[v])
@@ -205,7 +229,7 @@
 
 
 def apply_body(scale, *refs):
-    *blocks, from_4a, from_4b, normed, lead, stats, own, other, sums, gram = refs
+    *blocks, from_4a, from_4b, near, far, last, lead, stats, own, other, sums, gram = refs
     rows, part = own.shape[1], blocks[0].shape[2]
     z = lax.rem(lax.axis_index("feat"), Z)
 
@@ -218,12 +242,17 @@
         for back, block in zip((0, 1, 2, 3, 5, 6, 7), blocks):
             load(back, v, block.at[v])
         load(4, v, (from_4a, from_4b)[v])
-    diag = stats[2:3, :]
+    diag = stats[4:5, :]
+    ends = (0, near.shape[1], near.shape[1] + far.shape[1], gram.shape[2])
     for v in range(2):
         first = second = 0.0
         for h, out in enumerate((own, other)):
             r = slice(h * rows, (h + 1) * rows)
-            up = scale * jnp.dot(gram[1 - v, r, :], normed[v], preferred_element_type=f32)
+            up = 0.0
+            for i, normed in enumerate((near, far, last)):
+                left = gram[1 - v, r, ends[i] : ends[i + 1]]
+                up = up + jnp.dot(left, normed[v], preferred_element_type=f32)
+            up = scale * up
             if h == 0:
                 up = up + lead[1 - v, r, :].astype(f32) * diag
             out[v] = up
@@ -241,10 +270,10 @@
         total = total + sums[i]
     total = total / batch
     for v, out in enumerate((grad_a, grad_b)):
-        normal = lead[v, 0:rows, :].astype(f32)
+        own_normed = lead[v, 0:rows, :].astype(f32)
         first, second = total[2 * v : 2 * v + 1, :], total[2 * v + 1 : 2 * v + 2, :]
         up = own[v] + recv[v]
-        out[...] = ((up - first - normal * second) / stats[v : v + 1, :]).astype(bf16)
+        out[...] = ((up - first - own_normed * second) / stats[2 + v : 3 + v, :]).astype(bf16)
 
 
 def on_device(view_a, view_b):
@@ -258,48 +287,65 @@
     work = 2 * 2 * CORES * rows * half * cols
 
     views = jnp.stack([view_a, view_b])
-    from_down, from_up, from_x = send(views, TO_UP), send(views, TO_DOWN), send(views, TO_X)
+    from_down, from_up = send(views, TO_UP), send(views, TO_DOWN)
     sib = send(views, TO_CORE)
+    moments = call(moments_body, shape(5 * SUB, LANE), views)
+    for rank, to in enumerate((TO_CORE, TO_X)):
+        body = functools.partial(merge_body, rows * 2**rank)
+        moments = call(body, shape(5 * SUB, LANE), moments, send(moments, to))
+    late_views, moments = lax.optimization_barrier((views, moments))
+    from_x = send(late_views, TO_X)
+    moments = [moments, *(send(moments, to) for to in (TO_UP, TO_DOWN, TO_UP_2))]
+    from_down, from_up, moments[2] = lax.optimization_barrier((from_down, from_up, moments[2]))
+    from_x, moments[3] = lax.optimization_barrier((from_x, moments[3]))
     far_a, far_b = send(from_down[0], TO_UP), send(from_up[1], TO_DOWN)
+    from_x = call(copy_body, jax.ShapeDtypeStruct(from_x.shape, bf16), from_x, flops=10**10)
     x_down, x_up = send(from_x, TO_UP), send(from_x, TO_DOWN)
-    x_far = send(jnp.stack([far_a, far_b]), TO_X)
-    single = [far_a, far_b]
-    stacked = [views, from_down, from_up, from_x, x_down, x_up, x_far]
-    early = call(early_moments_body, shape(5, cols), *single, *stacked[:4])
-    moments = call(
-        functools.partial(late_moments_body, 5 * rows), shape(5, cols), early, *stacked[4:]
+    far = call(stack_body, jax.ShapeDtypeStruct(views.shape, bf16), far_a, far_b, flops=10**10)
+    x_far = send(far, TO_X)
+
+    def results(pieces):
+        return (
+            shape(2, pieces * rows, cols, dtype=bf16),
+            shape(2, CORES * rows, pieces * rows, dtype=bf16),
+        )
+
+    stats, lead, near, gram_near = call(
+        functools.partial(near_body, batch),
+        (shape(5, cols), shape(2, CORES * rows, cols, dtype=bf16), *results(4)),
+        *moments,
+        sib,
+        views,
+        from_down,
+        from_up,
+        from_x,
+        flops=work // 2,
+    )
+    far, gram_far = call(
+        far_body, results(3), lead, stats, far_a, far_b, x_down, x_up, flops=work * 3 // 8
     )
     one = shape(X_HI, part, half, dtype=bf16)
     both = shape(2, *one.shape, dtype=bf16)
     four = shape(2, *both.shape, dtype=bf16)
-    lead, normed, stats, *chunks = call(
-        functools.partial(gram_body, batch),
-        (
-            shape(2, CORES * rows, cols, dtype=bf16),
-            shape(2, half, cols, dtype=bf16),
-            shape(3, cols),
-            both,
-            both,
-            both,
-            four,
-            four,
-            one,
-            one,
-        ),
-        moments,
-        send(moments, TO_CORE),
-        sib,
-        *single,
-        *stacked,
-        flops=work,
-        scratch=[pltpu.VMEM((2, CORES * rows, half), bf16)],
+    last, *chunks = call(
+        last_body,
+        (results(1)[0], both, both, both, four, four, one, one),
+        lead,
+        stats,
+        x_far,
+        gram_near,
+        gram_far,
+        flops=work // 8,
+        scratch=[pltpu.VMEM(results(1)[1].shape, bf16)],
     )
     blocks = spread_rows(reduce_rows(*chunks))
     own, other, sums = call(
         functools.partial(apply_body, scale),
         (shape(2, rows, cols), shape(2, rows, cols), shape(dp_count, 4, cols)),
         *blocks,
-        normed,
+        near,
+        far,
+        last,
         lead,
         stats,
         flops=work,

time: 112 us -> 110 us (0.982)
  waiting for transfers between devices: 40.4 us -> 38 us
  Pallas kernels: 8.24 us -> 6.32 us
  starting transfers between devices: 51.7 us -> 53 us
    ppermute x26 -> x30, waiting for transfers between devices: 40.4 us -> 38 us  [send(): return lax.ppermute(x, axis, to)]
    pallas_call x8 -> x13, Pallas kernels: 8.24 us -> 6.32 us  [call(): pl.pallas_call(body, out_shape=outs, in_specs=[pl.BlockSpec(memory_space=...]
    ppermute x26 -> x30, starting transfers between devices: 51.7 us -> 53 us  [send(): return lax.ppermute(x, axis, to)]
  transfers between devices with their start and end apart: 26 -> 30, of which waited for: 12 -> 16; matrix products, arithmetic and copies ran while one was open for 0% -> 0% of each run, Pallas kernels for 3% -> 3%
where the time goes in v5:
time: 110 us
  starting transfers between devices  53 us (48%)
  waiting for transfers between devices  38 us (35%)
  blocking collectives  10.3 us (9%)
  Pallas kernels  6.32 us (6%)
    ppermute x30, starting transfers between devices, send(): return lax.ppermute(x, axis, to)  53 us
    ppermute x30, waiting for transfers between devices, send(): return lax.ppermute(x, axis, to)  38 us
    all_to_all x1, blocking collectives, on_device(): sums = lax.all_to_all(sums, 'dp', 0, 0)  10.3 us
    pallas_call x13, Pallas kernels, call(): pl.pallas_call(body, out_shape=outs, in_specs=[pl.BlockSpec(memory_space=...  6.32 us
  transfers between devices with their start and end apart: 30, of which 16 were waited for; matrix products, arithmetic and copies ran while one was open for 0% of the time, Pallas kernels for 3%

profile of v5, /device:TPU:1, one launch (start us, length us, event | category | flops | bytes accessed | tf_op | source)
XLA Modules:
  0.0 109.6 jit_solution(2635533902976333742)
XLA Ops:
  0.6 1.1 pad_maximum_fusion.views.refs_5_
  1.7 3.6 %collective-permute-start.4 = (bf16[2,128,1024]{2,1,0:T(8,128)(2,1)S(1)}, bf16[2,128,1024]{2,1,0:T(8,128)(2,1)S(1)}, u32[]{:S(2)}, u32[]{:S(2)}) collective-permute-start(bf16[2,128,1024]{2,1,0:T(8,128)(2,1)S(1)} %pad_maximum_fusion.views.refs_5_), channel_id=1, source_target_pairs={{0,96},{16,112},{32,0},{48,16},{64,32},{80,48},{96,64},{112,80},{1... | collective-permute-start | bytes 1572872 | tf_op jit(solution)/shard_map/ppermute | solution.py:46
  5.4 0.3 shard_map.41.one
  5.7 1.8 %collective-permute-start = (f32[40,128]{1,0:T(8,128)S(1)}, f32[40,128]{1,0:T(8,128)S(1)}, u32[]{:S(2)}, u32[]{:S(2)}) collective-permute-start(f32[40,128]{1,0:T(8,128)S(1)} %shard_map.41.one), channel_id=1, source_target_pairs={{0,16},{16,0},{32,48},{48,32},{64,80},{80,64},{96,112},{112,96},{1... | collective-permute-start | bytes 61448 | tf_op jit(solution)/shard_map/ppermute | solution.py:46
  7.5 0.8 collective-permute-done.other
  8.3 0.6 collective-permute-start.1
  8.9 2.5 %collective-permute-done.1.other = f32[40,128]{1,0:T(8,128)S(1)} collective-permute-done((f32[40,128]{1,0:T(8,128)S(1)}, f32[40,128]{1,0:T(8,128)S(1)}, u32[]{:S(2)}, u32[]{:S(2)}) %collective-permute-start.1) | collective-permute-done | bytes 20512 | tf_op jit(solution)/shard_map/ppermute | solution.py:46
  11.3 0.6 collective-permute-start.6
  11.9 3.0 %collective-permute-start.5 = (f32[40,128]{1,0:T(8,128)S(1)}, f32[40,128]{1,0:T(8,128)S(1)}, u32[]{:S(2)}, u32[]{:S(2)}) collective-permute-start(f32[40,128]{1,0:T(8,128)S(1)} %shard_map.43.refs_0_), channel_id=1, source_target_pairs={{0,96},{16,112},{32,0},{48,16},{64,32},{80,48},{96,64},{112,80},{1... | collective-permute-start | bytes 61448 | tf_op jit(solution)/shard_map/ppermute | solution.py:46
  14.9 1.8 %collective-permute-start.8 = (bf16[2,128,1024]{2,1,0:T(8,128)(2,1)S(1)}, bf16[2,128,1024]{2,1,0:T(8,128)(2,1)S(1)}, u32[]{:S(2)}, u32[]{:S(2)}) collective-permute-start(bf16[2,128,1024]{2,1,0:T(8,128)(2,1)S(1)} %pad_maximum_fusion.views.refs_5_), channel_id=1, source_target_pairs={{0,16},{16,0},{32,48},{48,32},{64,80},{80,64},{96,112},{112,96},{1... | collective-permute-start | bytes 1572872 | tf_op jit(solution)/shard_map/ppermute | solution.py:46
  16.6 2.1 %collective-permute-start.7 = (f32[40,128]{1,0:T(8,128)S(1)}, f32[40,128]{1,0:T(8,128)S(1)}, u32[]{:S(2)}, u32[]{:S(2)}) collective-permute-start(f32[40,128]{1,0:T(8,128)S(1)} %shard_map.43.refs_0_), channel_id=1, source_target_pairs={{0,64},{16,80},{32,96},{48,112},{64,0},{80,16},{96,32},{112,48},{1... | collective-permute-start | bytes 61448 | tf_op jit(solution)/shard_map/ppermute | solution.py:46
  18.8 0.3 collective-permute-done.3.refs_6_
  19.1 0.9 collective-permute-start.10
  19.9 0.7 collective-permute-start.9
  20.6 0.1 collective-permute-done.7.refs_3_
  20.8 2.9 %collective-permute-done.6.x = bf16[2,128,1024]{2,1,0:T(8,128)(2,1)S(1)} collective-permute-done((bf16[2,128,1024]{2,1,0:T(8,128)(2,1)S(1)}, bf16[2,128,1024]{2,1,0:T(8,128)(2,1)S(1)}, u32[]{:S(2)}, u32[]{:S(2)}) %collective-permute-start.6) | collective-permute-done | bytes 524320 | tf_op jit(solution)/shard_map/ppermute | solution.py:46
  23.7 2.3 %collective-permute-start.13 = (bf16[2,128,1024]{2,1,0:T(8,128)(2,1)S(1)}, bf16[2,128,1024]{2,1,0:T(8,128)(2,1)S(1)}, u32[]{:S(2)}, u32[]{:S(2)}) collective-permute-start(bf16[2,128,1024]{2,1,0:T(8,128)(2,1)S(1)} %shard_map.44.refs_8_), channel_id=1, source_target_pairs={{0,96},{16,112},{32,0},{48,16},{64,32},{80,48},{96,64},{112,80},{1... | collective-permute-start | bytes 1572872 | tf_op jit(solution)/shard_map/ppermute | solution.py:46
  26.0 1.1 %collective-permute-done.9.a.far_a = bf16[128,1024]{1,0:T(8,128)(2,1)S(1)} collective-permute-done((bf16[128,1024]{1,0:T(8,128)(2,1)S(1)}, bf16[128,1024]{1,0:T(8,128)(2,1)S(1)}, u32[]{:S(2)}, u32[]{:S(2)}) %collective-permute-start.9) | collective-permute-done | bytes 262176 | tf_op jit(solution)/shard_map/ppermute | solution.py:46
  27.1 1.3 %collective-permute-start.11 = (bf16[2,128,1024]{2,1,0:T(8,128)(2,1)S(1)}, bf16[2,128,1024]{2,1,0:T(8,128)(2,1)S(1)}, u32[]{:S(2)}, u32[]{:S(2)}) collective-permute-start(bf16[2,128,1024]{2,1,0:T(8,128)(2,1)S(1)} %shard_map.46), channel_id=1, source_target_pairs={{0,128},{16,144},{32,160},{48,176},{64,192},{80,208},{96,224},{112... | collective-permute-start | bytes 1572872 | tf_op jit(solution)/shard_map/ppermute | solution.py:46
  28.4 10.2 %collective-permute-done.2.refs_1_ = f32[40,128]{1,0:T(8,128)S(1)} collective-permute-done((f32[40,128]{1,0:T(8,128)S(1)}, f32[40,128]{1,0:T(8,128)S(1)}, u32[]{:S(2)}, u32[]{:S(2)}) %collective-permute-start.2) | collective-permute-done | bytes 20512 | tf_op jit(solution)/shard_map/ppermute | solution.py:46
  38.6 1.3 %shard_map.45 = (f32[5,1024]{1,0:T(8,128)S(1)}, bf16[2,256,1024]{2,1,0:T(8,128)(2,1)S(1)}, bf16[2,512,1024]{2,1,0:T(8,128)(2,1)S(1)}, bf16[2,256,512]{2,1,0:T(8,128)(2,1)S(1)}) custom-call(f32[40,128]{1,0:T(8,128)S(1)} %shard_map.43.refs_0_, f32[40,128]{1,0:T(8,128)S(1)} %collective-permute-done.2.refs_1_, f32[40,128]{1,0:T(8,128)S(1)} %collective-permute-done.5.refs_2_, ...), custom_call_target="tpu_custom_call" | custom-call | flops 536870912 | bytes 6393856 | tf_op jit(solution)/shard_map/pallas_call | solution.py:53
  40.0 1.0 shard_map.47
  41.0 0.5 shard_map.48
  41.5 1.7 %collective-permute-start.14 = (bf16[2,2,2,16,1024]{4,3,2,1,0:T(8,128)(2,1)S(1)}, bf16[2,2,2,16,1024]{4,3,2,1,0:T(8,128)(2,1)S(1)}, u32[]{:S(2)}, u32[]{:S(2)}) collective-permute-start(bf16[2,2,2,16,1024]{4,3,2,1,0:T(8,128)(2,1)S(1)} %get-tuple-element.40), channel_id=1, source_target_pairs={{0,1},{1,2},{2,3},{3,4},{4,5},{5,6},{6,7},{7,0},{8,9},{9,10},{10,1... | collective-permute-start | bytes 786440 | tf_op jit(solution)/shard_map/ppermute | solution.py:46
  43.2 4.0 %collective-permute-start.15 = (bf16[2,2,2,16,1024]{4,3,2,1,0:T(8,128)(2,1)S(1)}, bf16[2,2,2,16,1024]{4,3,2,1,0:T(8,128)(2,1)S(1)}, u32[]{:S(2)}, u32[]{:S(2)}) collective-permute-start(bf16[2,2,2,16,1024]{4,3,2,1,0:T(8,128)(2,1)S(1)} %get-tuple-element.41), channel_id=1, source_target_pairs={{0,7},{1,0},{2,1},{3,2},{4,3},{5,4},{6,5},{7,6},{8,15},{9,8},{10,9... | collective-permute-start | bytes 786440 | tf_op jit(solution)/shard_map/ppermute | solution.py:46
  47.3 3.6 %collective-permute-start.17 = (bf16[2,16,1024]{2,1,0:T(8,128)(2,1)S(1)}, bf16[2,16,1024]{2,1,0:T(8,128)(2,1)S(1)}, u32[]{:S(2)}, u32[]{:S(2)}) collective-permute-start(bf16[2,16,1024]{2,1,0:T(8,128)(2,1)S(1)} %get-tuple-element.43), channel_id=1, source_target_pairs={{0,6},{1,7},{2,0},{3,1},{4,2},{5,3},{6,4},{7,5},{8,14},{9,15},{10,... | collective-permute-start | bytes 196616 | tf_op jit(solution)/shard_map/ppermute | solution.py:46
  50.9 2.6 %collective-permute-done.16.half_a = bf16[2,16,1024]{2,1,0:T(8,128)(2,1)S(1)} collective-permute-done((bf16[2,16,1024]{2,1,0:T(8,128)(2,1)S(1)}, bf16[2,16,1024]{2,1,0:T(8,128)(2,1)S(1)}, u32[]{:S(2)}, u32[]{:S(2)}) %collective-permute-start.16) | collective-permute-done | bytes 65568 | tf_op jit(solution)/shard_map/ppermute | solution.py:46
  53.5 1.4 %collective-permute-done.17.half_b = bf16[2,16,1024]{2,1,0:T(8,128)(2,1)S(1)} collective-permute-done((bf16[2,16,1024]{2,1,0:T(8,128)(2,1)S(1)}, bf16[2,16,1024]{2,1,0:T(8,128)(2,1)S(1)}, u32[]{:S(2)}, u32[]{:S(2)}) %collective-permute-start.17) | collective-permute-done | bytes 65568 | tf_op jit(solution)/shard_map/ppermute | solution.py:46
  55.0 2.6 %collective-permute-start.18 = (bf16[2,2,16,1024]{3,2,1,0:T(8,128)(2,1)S(1)}, bf16[2,2,16,1024]{3,2,1,0:T(8,128)(2,1)S(1)}, u32[]{:S(2)}, u32[]{:S(2)}) collective-permute-start(bf16[2,2,16,1024]{3,2,1,0:T(8,128)(2,1)S(1)} %get-tuple-element.46), channel_id=1, source_target_pairs={{0,2},{1,3},{2,4},{3,5},{4,6},{5,7},{6,0},{7,1},{8,10},{9,11},{10,... | collective-permute-start | bytes 393224 | tf_op jit(solution)/shard_map/ppermute | solution.py:46
  57.6 1.0 collective-permute-start.19
  58.6 2.4 %collective-permute-done.18.far_up = bf16[2,2,16,1024]{3,2,1,0:T(8,128)(2,1)S(1)} collective-permute-done((bf16[2,2,16,1024]{3,2,1,0:T(8,128)(2,1)S(1)}, bf16[2,2,16,1024]{3,2,1,0:T(8,128)(2,1)S(1)}, u32[]{:S(2)}, u32[]{:S(2)}) %collective-permute-start.18) | collective-permute-done | bytes 131104 | tf_op jit(solution)/shard_map/ppermute | solution.py:46
  61.0 2.5 %collective-permute-done.19.far_down = bf16[2,2,16,1024]{3,2,1,0:T(8,128)(2,1)S(1)} collective-permute-done((bf16[2,2,16,1024]{3,2,1,0:T(8,128)(2,1)S(1)}, bf16[2,2,16,1024]{3,2,1,0:T(8,128)(2,1)S(1)}, u32[]{:S(2)}, u32[]{:S(2)}) %collective-permute-start.19) | collective-permute-done | bytes 131104 | tf_op jit(solution)/shard_map/ppermute | solution.py:46
  63.5 0.1 shard_map.50.a
  63.6 2.8 %collective-permute-start.20 = (bf16[2,2,16,1024]{3,2,1,0:T(8,128)(2,1)S(1)}, bf16[2,2,16,1024]{3,2,1,0:T(8,128)(2,1)S(1)}, u32[]{:S(2)}, u32[]{:S(2)}) collective-permute-start(bf16[2,2,16,1024]{3,2,1,0:T(8,128)(2,1)S(1)} %shard_map.50.a), channel_id=1, source_target_pairs={{0,8},{1,9},{2,10},{3,11},{4,12},{5,13},{6,14},{7,15},{8,0},{9,1},... | collective-permute-start | bytes 393224 | tf_op jit(solution)/shard_map/ppermute | solution.py:46
  66.4 2.6 %collective-permute-done.20.b = bf16[2,2,16,1024]{3,2,1,0:T(8,128)(2,1)S(1)} collective-permute-done((bf16[2,2,16,1024]{3,2,1,0:T(8,128)(2,1)S(1)}, bf16[2,2,16,1024]{3,2,1,0:T(8,128)(2,1)S(1)}, u32[]{:S(2)}, u32[]{:S(2)}) %collective-permute-start.20) | collective-permute-done | bytes 131104 | tf_op jit(solution)/shard_map/ppermute | solution.py:46
  69.1 1.4 %collective-permute-start.24 = (bf16[2,2,16,1024]{3,2,1,0:T(8,128)(2,1)S(1)}, bf16[2,2,16,1024]{3,2,1,0:T(8,128)(2,1)S(1)}, u32[]{:S(2)}, u32[]{:S(2)}) collective-permute-start(bf16[2,2,16,1024]{3,2,1,0:T(8,128)(2,1)S(1)} %shard_map.51.refs_0_), channel_id=1, source_target_pairs={{0,6},{1,7},{2,0},{3,1},{4,2},{5,3},{6,4},{7,5},{8,14},{9,15},{10,... | collective-permute-start | bytes 393224 | tf_op jit(solution)/shard_map/ppermute | solution.py:46
  70.5 1.1 collective-permute-start.22
  71.5 1.5 %collective-permute-start.21 = (bf16[2,2,16,1024]{3,2,1,0:T(8,128)(2,1)S(1)}, bf16[2,2,16,1024]{3,2,1,0:T(8,128)(2,1)S(1)}, u32[]{:S(2)}, u32[]{:S(2)}) collective-permute-start(bf16[2,2,16,1024]{3,2,1,0:T(8,128)(2,1)S(1)} %shard_map.51.refs_0_), channel_id=1, source_target_pairs={{0,1},{1,2},{2,3},{3,4},{4,5},{5,6},{6,7},{7,0},{8,9},{9,10},{10,1... | collective-permute-start | bytes 393224 | tf_op jit(solution)/shard_map/ppermute | solution.py:46
  73.0 1.7 %collective-permute-done.24.refs_5_ = bf16[2,2,16,1024]{3,2,1,0:T(8,128)(2,1)S(1)} collective-permute-done((bf16[2,2,16,1024]{3,2,1,0:T(8,128)(2,1)S(1)}, bf16[2,2,16,1024]{3,2,1,0:T(8,128)(2,1)S(1)}, u32[]{:S(2)}, u32[]{:S(2)}) %collective-permute-start.24) | collective-permute-done | bytes 131104 | tf_op jit(solution)/shard_map/ppermute | solution.py:46
  74.7 2.0 %collective-permute-start.28 = (bf16[2,16,1024]{2,1,0:T(8,128)(2,1)S(1)}, bf16[2,16,1024]{2,1,0:T(8,128)(2,1)S(1)}, u32[]{:S(2)}, u32[]{:S(2)}) collective-permute-start(bf16[2,16,1024]{2,1,0:T(8,128)(2,1)S(1)} %slice_bitcast_fusion.2), channel_id=1, source_target_pairs={{0,6},{1,7},{2,0},{3,1},{4,2},{5,3},{6,4},{7,5},{8,14},{9,15},{10,... | collective-permute-start | bytes 196616 | tf_op jit(solution)/shard_map/ppermute | solution.py:46
  76.7 2.3 %collective-permute-start.23 = (bf16[2,2,16,1024]{3,2,1,0:T(8,128)(2,1)S(1)}, bf16[2,2,16,1024]{3,2,1,0:T(8,128)(2,1)S(1)}, u32[]{:S(2)}, u32[]{:S(2)}) collective-permute-start(bf16[2,2,16,1024]{3,2,1,0:T(8,128)(2,1)S(1)} %collective-permute-done.22.refs_2_), channel_id=1, source_target_pairs={{0,1},{1,2},{2,3},{3,4},{4,5},{5,6},{6,7},{7,0},{8,9},{9,10},{10,1... | collective-permute-start | bytes 393224 | tf_op jit(solution)/shard_map/ppermute | solution.py:46
  79.1 0.1 collective-permute-done.21.refs_1_
  79.2 1.1 %collective-permute-done.28.refs_8_ = bf16[2,16,1024]{2,1,0:T(8,128)(2,1)S(1)} collective-permute-done((bf16[2,16,1024]{2,1,0:T(8,128)(2,1)S(1)}, bf16[2,16,1024]{2,1,0:T(8,128)(2,1)S(1)}, u32[]{:S(2)}, u32[]{:S(2)}) %collective-permute-start.28) | collective-permute-done | bytes 65568 | tf_op jit(solution)/shard_map/ppermute | solution.py:46
  80.3 5.6 %collective-permute-done.27.refs_7_ = bf16[2,16,1024]{2,1,0:T(8,128)(2,1)S(1)} collective-permute-done((bf16[2,16,1024]{2,1,0:T(8,128)(2,1)S(1)}, bf16[2,16,1024]{2,1,0:T(8,128)(2,1)S(1)}, u32[]{:S(2)}, u32[]{:S(2)}) %collective-permute-start.27) | collective-permute-done | bytes 65568 | tf_op jit(solution)/shard_map/ppermute | solution.py:46
  86.0 1.9 %shard_map.52 = (f32[2,128,1024]{2,1,0:T(8,128)S(1)}, f32[2,128,1024]{2,1,0:T(8,128)S(1)}, f32[16,4,1024]{2,1,0:T(4,128)S(1)}) custom-call(bf16[2,2,16,1024]{3,2,1,0:T(8,128)(2,1)S(1)} %shard_map.51.refs_0_, bf16[2,2,16,1024]{3,2,1,0:T(8,128)(2,1)S(1)} %collective-permute-done.21.refs_1_, bf16[2,2,16,1024]{3,2,1,0:T(8,128)(2,1)S(1)} %collective-permute-done.22.refs_2_, ...), custom_call_target="tpu_custom_call" | custom-call | flops 1073741824 | bytes 8671232 | tf_op jit(solution)/shard_map/pallas_call | solution.py:53
  87.9 10.4 %collective-permute-start.29 = (f32[2,128,1024]{2,1,0:T(8,128)S(1)}, f32[2,128,1024]{2,1,0:T(8,128)S(1)}, u32[]{:S(2)}, u32[]{:S(2)}) collective-permute-start(f32[2,128,1024]{2,1,0:T(8,128)S(1)} %get-tuple-element.52), channel_id=1, source_target_pairs={{0,16},{16,0},{32,48},{48,32},{64,80},{80,64},{96,112},{112,96},{1... | collective-permute-start | bytes 3145736 | tf_op jit(solution)/shard_map/ppermute | solution.py:46
  98.3 10.3 %all_to_all.5.sums = f32[16,4,1024]{2,1,0:T(4,128)S(1)} all-to-all(f32[16,4,1024]{2,1,0:T(4,128)S(1)} %get-tuple-element.53), channel_id=1, replica_groups=mesh['dp'=16,'feat'=16] {'dp'}, dimensions={0} | all-to-all | bytes 524288 | tf_op jit(solution)/shard_map/all_to_all | solution.py:354
  108.7 1.0 shard_map.53
  (31 shorter events, 0.4 us)
Async XLA Ops:
  1.7 17.1 %collective-permute-start.4 = (bf16[2,128,1024]{2,1,0:T(8,128)(2,1)S(1)}, bf16[2,128,1024]{2,1,0:T(8,128)(2,1)S(1)}, u32[]{:S(2)}, u32[]{:S(2)}) collective-permute-start(bf16[2,128,1024]{2,1,0:T(8,128)(2,1)S(1)} %pad_maximum_fusion.views.refs_5_), channel_id=1, source_target_pairs={{0,96},{16,112},{32,0},{48,16},{64,32},{80,48},{96,64},{112,80},{1... | collective-permute-start | bytes 1572872 | tf_op jit(solution)/shard_map/ppermute | solution.py:46
  5.4 13.7 %collective-permute-start.3 = (bf16[2,128,1024]{2,1,0:T(8,128)(2,1)S(1)}, bf16[2,128,1024]{2,1,0:T(8,128)(2,1)S(1)}, u32[]{:S(2)}, u32[]{:S(2)}) collective-permute-start(bf16[2,128,1024]{2,1,0:T(8,128)(2,1)S(1)} %pad_maximum_fusion.views.refs_5_), channel_id=1, source_target_pairs={{0,32},{16,48},{32,64},{48,80},{64,96},{80,112},{96,0},{112,16},{1... | collective-permute-start | bytes 1572872 | tf_op jit(solution)/shard_map/ppermute | solution.py:46
  5.7 2.6 %collective-permute-start = (f32[40,128]{1,0:T(8,128)S(1)}, f32[40,128]{1,0:T(8,128)S(1)}, u32[]{:S(2)}, u32[]{:S(2)}) collective-permute-start(f32[40,128]{1,0:T(8,128)S(1)} %shard_map.41.one), channel_id=1, source_target_pairs={{0,16},{16,0},{32,48},{48,32},{64,80},{80,64},{96,112},{112,96},{1... | collective-permute-start | bytes 61448 | tf_op jit(solution)/shard_map/ppermute | solution.py:46
  8.3 3.0 %collective-permute-start.1 = (f32[40,128]{1,0:T(8,128)S(1)}, f32[40,128]{1,0:T(8,128)S(1)}, u32[]{:S(2)}, u32[]{:S(2)}) collective-permute-start(f32[40,128]{1,0:T(8,128)S(1)} %shard_map.42.one), channel_id=1, source_target_pairs={{0,128},{16,144},{32,160},{48,176},{64,192},{80,208},{96,224},{112... | collective-permute-start | bytes 61448 | tf_op jit(solution)/shard_map/ppermute | solution.py:46
  11.3 12.3 %collective-permute-start.6 = (bf16[2,128,1024]{2,1,0:T(8,128)(2,1)S(1)}, bf16[2,128,1024]{2,1,0:T(8,128)(2,1)S(1)}, u32[]{:S(2)}, u32[]{:S(2)}) collective-permute-start(bf16[2,128,1024]{2,1,0:T(8,128)(2,1)S(1)} %pad_maximum_fusion.views.refs_5_), channel_id=1, source_target_pairs={{0,128},{16,144},{32,160},{48,176},{64,192},{80,208},{96,224},{112... | collective-permute-start | bytes 1572872 | tf_op jit(solution)/shard_map/ppermute | solution.py:46
  11.9 4.7 %collective-permute-start.5 = (f32[40,128]{1,0:T(8,128)S(1)}, f32[40,128]{1,0:T(8,128)S(1)}, u32[]{:S(2)}, u32[]{:S(2)}) collective-permute-start(f32[40,128]{1,0:T(8,128)S(1)} %shard_map.43.refs_0_), channel_id=1, source_target_pairs={{0,96},{16,112},{32,0},{48,16},{64,32},{80,48},{96,64},{112,80},{1... | collective-permute-start | bytes 61448 | tf_op jit(solution)/shard_map/ppermute | solution.py:46
  14.9 23.8 %collective-permute-start.8 = (bf16[2,128,1024]{2,1,0:T(8,128)(2,1)S(1)}, bf16[2,128,1024]{2,1,0:T(8,128)(2,1)S(1)}, u32[]{:S(2)}, u32[]{:S(2)}) collective-permute-start(bf16[2,128,1024]{2,1,0:T(8,128)(2,1)S(1)} %pad_maximum_fusion.views.refs_5_), channel_id=1, source_target_pairs={{0,16},{16,0},{32,48},{48,32},{64,80},{80,64},{96,112},{112,96},{1... | collective-permute-start | bytes 1572872 | tf_op jit(solution)/shard_map/ppermute | solution.py:46
  16.6 4.1 %collective-permute-start.7 = (f32[40,128]{1,0:T(8,128)S(1)}, f32[40,128]{1,0:T(8,128)S(1)}, u32[]{:S(2)}, u32[]{:S(2)}) collective-permute-start(f32[40,128]{1,0:T(8,128)S(1)} %shard_map.43.refs_0_), channel_id=1, source_target_pairs={{0,64},{16,80},{32,96},{48,112},{64,0},{80,16},{96,32},{112,48},{1... | collective-permute-start | bytes 61448 | tf_op jit(solution)/shard_map/ppermute | solution.py:46
  19.1 6.9 %collective-permute-start.10 = (bf16[128,1024]{1,0:T(8,128)(2,1)S(1)}, bf16[128,1024]{1,0:T(8,128)(2,1)S(1)}, u32[]{:S(2)}, u32[]{:S(2)}) collective-permute-start(bf16[128,1024]{1,0:T(8,128)(2,1)S(1)} %slice_bitcast_fusion), channel_id=1, source_target_pairs={{0,96},{16,112},{32,0},{48,16},{64,32},{80,48},{96,64},{112,80},{1... | collective-permute-start | bytes 786440 | tf_op jit(solution)/shard_map/ppermute | solution.py:46
  19.9 7.2 %collective-permute-start.9 = (bf16[128,1024]{1,0:T(8,128)(2,1)S(1)}, bf16[128,1024]{1,0:T(8,128)(2,1)S(1)}, u32[]{:S(2)}, u32[]{:S(2)}) collective-permute-start(bf16[128,1024]{1,0:T(8,128)(2,1)S(1)} %slice_bitcast_fusion.1), channel_id=1, source_target_pairs={{0,32},{16,48},{32,64},{48,80},{64,96},{80,112},{96,0},{112,16},{1... | collective-permute-start | bytes 786440 | tf_op jit(solution)/shard_map/ppermute | solution.py:46
  23.7 16.3 %collective-permute-start.13 = (bf16[2,128,1024]{2,1,0:T(8,128)(2,1)S(1)}, bf16[2,128,1024]{2,1,0:T(8,128)(2,1)S(1)}, u32[]{:S(2)}, u32[]{:S(2)}) collective-permute-start(bf16[2,128,1024]{2,1,0:T(8,128)(2,1)S(1)} %shard_map.44.refs_8_), channel_id=1, source_target_pairs={{0,96},{16,112},{32,0},{48,16},{64,32},{80,48},{96,64},{112,80},{1... | collective-permute-start | bytes 1572872 | tf_op jit(solution)/shard_map/ppermute | solution.py:46
  26.0 14.0 %collective-permute-start.12 = (bf16[2,128,1024]{2,1,0:T(8,128)(2,1)S(1)}, bf16[2,128,1024]{2,1,0:T(8,128)(2,1)S(1)}, u32[]{:S(2)}, u32[]{:S(2)}) collective-permute-start(bf16[2,128,1024]{2,1,0:T(8,128)(2,1)S(1)} %shard_map.44.refs_8_), channel_id=1, source_target_pairs={{0,32},{16,48},{32,64},{48,80},{64,96},{80,112},{96,0},{112,16},{1... | collective-permute-start | bytes 1572872 | tf_op jit(solution)/shard_map/ppermute | solution.py:46
  27.1 13.9 %collective-permute-start.11 = (bf16[2,128,1024]{2,1,0:T(8,128)(2,1)S(1)}, bf16[2,128,1024]{2,1,0:T(8,128)(2,1)S(1)}, u32[]{:S(2)}, u32[]{:S(2)}) collective-permute-start(bf16[2,128,1024]{2,1,0:T(8,128)(2,1)S(1)} %shard_map.46), channel_id=1, source_target_pairs={{0,128},{16,144},{32,160},{48,176},{64,192},{80,208},{96,224},{112... | collective-permute-start | bytes 1572872 | tf_op jit(solution)/shard_map/ppermute | solution.py:46
  28.4 10.2 %collective-permute-start.2 = (f32[40,128]{1,0:T(8,128)S(1)}, f32[40,128]{1,0:T(8,128)S(1)}, u32[]{:S(2)}, u32[]{:S(2)}) collective-permute-start(f32[40,128]{1,0:T(8,128)S(1)} %shard_map.43.refs_0_), channel_id=1, source_target_pairs={{0,32},{16,48},{32,64},{48,80},{64,96},{80,112},{96,0},{112,16},{1... | collective-permute-start | bytes 61448 | tf_op jit(solution)/shard_map/ppermute | solution.py:46
  41.5 13.4 %collective-permute-start.14 = (bf16[2,2,2,16,1024]{4,3,2,1,0:T(8,128)(2,1)S(1)}, bf16[2,2,2,16,1024]{4,3,2,1,0:T(8,128)(2,1)S(1)}, u32[]{:S(2)}, u32[]{:S(2)}) collective-permute-start(bf16[2,2,2,16,1024]{4,3,2,1,0:T(8,128)(2,1)S(1)} %get-tuple-element.40), channel_id=1, source_target_pairs={{0,1},{1,2},{2,3},{3,4},{4,5},{5,6},{6,7},{7,0},{8,9},{9,10},{10,1... | collective-permute-start | bytes 786440 | tf_op jit(solution)/shard_map/ppermute | solution.py:46
  43.2 11.7 %collective-permute-start.15 = (bf16[2,2,2,16,1024]{4,3,2,1,0:T(8,128)(2,1)S(1)}, bf16[2,2,2,16,1024]{4,3,2,1,0:T(8,128)(2,1)S(1)}, u32[]{:S(2)}, u32[]{:S(2)}) collective-permute-start(bf16[2,2,2,16,1024]{4,3,2,1,0:T(8,128)(2,1)S(1)} %get-tuple-element.41), channel_id=1, source_target_pairs={{0,7},{1,0},{2,1},{3,2},{4,3},{5,4},{6,5},{7,6},{8,15},{9,8},{10,9... | collective-permute-start | bytes 786440 | tf_op jit(solution)/shard_map/ppermute | solution.py:46
  47.3 6.2 %collective-permute-start.16 = (bf16[2,16,1024]{2,1,0:T(8,128)(2,1)S(1)}, bf16[2,16,1024]{2,1,0:T(8,128)(2,1)S(1)}, u32[]{:S(2)}, u32[]{:S(2)}) collective-permute-start(bf16[2,16,1024]{2,1,0:T(8,128)(2,1)S(1)} %get-tuple-element.42), channel_id=1, source_target_pairs={{0,2},{1,3},{2,4},{3,5},{4,6},{5,7},{6,0},{7,1},{8,10},{9,11},{10,... | collective-permute-start | bytes 196616 | tf_op jit(solution)/shard_map/ppermute | solution.py:46
  47.3 7.6 %collective-permute-start.17 = (bf16[2,16,1024]{2,1,0:T(8,128)(2,1)S(1)}, bf16[2,16,1024]{2,1,0:T(8,128)(2,1)S(1)}, u32[]{:S(2)}, u32[]{:S(2)}) collective-permute-start(bf16[2,16,1024]{2,1,0:T(8,128)(2,1)S(1)} %get-tuple-element.43), channel_id=1, source_target_pairs={{0,6},{1,7},{2,0},{3,1},{4,2},{5,3},{6,4},{7,5},{8,14},{9,15},{10,... | collective-permute-start | bytes 196616 | tf_op jit(solution)/shard_map/ppermute | solution.py:46
  55.0 6.0 %collective-permute-start.18 = (bf16[2,2,16,1024]{3,2,1,0:T(8,128)(2,1)S(1)}, bf16[2,2,16,1024]{3,2,1,0:T(8,128)(2,1)S(1)}, u32[]{:S(2)}, u32[]{:S(2)}) collective-permute-start(bf16[2,2,16,1024]{3,2,1,0:T(8,128)(2,1)S(1)} %get-tuple-element.46), channel_id=1, source_target_pairs={{0,2},{1,3},{2,4},{3,5},{4,6},{5,7},{6,0},{7,1},{8,10},{9,11},{10,... | collective-permute-start | bytes 393224 | tf_op jit(solution)/shard_map/ppermute | solution.py:46
  57.6 6.0 %collective-permute-start.19 = (bf16[2,2,16,1024]{3,2,1,0:T(8,128)(2,1)S(1)}, bf16[2,2,16,1024]{3,2,1,0:T(8,128)(2,1)S(1)}, u32[]{:S(2)}, u32[]{:S(2)}) collective-permute-start(bf16[2,2,16,1024]{3,2,1,0:T(8,128)(2,1)S(1)} %get-tuple-element.47), channel_id=1, source_target_pairs={{0,6},{1,7},{2,0},{3,1},{4,2},{5,3},{6,4},{7,5},{8,14},{9,15},{10,... | collective-permute-start | bytes 393224 | tf_op jit(solution)/shard_map/ppermute | solution.py:46
  63.6 5.4 %collective-permute-start.20 = (bf16[2,2,16,1024]{3,2,1,0:T(8,128)(2,1)S(1)}, bf16[2,2,16,1024]{3,2,1,0:T(8,128)(2,1)S(1)}, u32[]{:S(2)}, u32[]{:S(2)}) collective-permute-start(bf16[2,2,16,1024]{3,2,1,0:T(8,128)(2,1)S(1)} %shard_map.50.a), channel_id=1, source_target_pairs={{0,8},{1,9},{2,10},{3,11},{4,12},{5,13},{6,14},{7,15},{8,0},{9,1},... | collective-permute-start | bytes 393224 | tf_op jit(solution)/shard_map/ppermute | solution.py:46
  69.1 5.6 %collective-permute-start.24 = (bf16[2,2,16,1024]{3,2,1,0:T(8,128)(2,1)S(1)}, bf16[2,2,16,1024]{3,2,1,0:T(8,128)(2,1)S(1)}, u32[]{:S(2)}, u32[]{:S(2)}) collective-permute-start(bf16[2,2,16,1024]{3,2,1,0:T(8,128)(2,1)S(1)} %shard_map.51.refs_0_), channel_id=1, source_target_pairs={{0,6},{1,7},{2,0},{3,1},{4,2},{5,3},{6,4},{7,5},{8,14},{9,15},{10,... | collective-permute-start | bytes 393224 | tf_op jit(solution)/shard_map/ppermute | solution.py:46
  70.5 8.5 %collective-permute-start.26 = (bf16[2,2,16,1024]{3,2,1,0:T(8,128)(2,1)S(1)}, bf16[2,2,16,1024]{3,2,1,0:T(8,128)(2,1)S(1)}, u32[]{:S(2)}, u32[]{:S(2)}) collective-permute-start(bf16[2,2,16,1024]{3,2,1,0:T(8,128)(2,1)S(1)} %shard_map.51.refs_0_), channel_id=1, source_target_pairs={{0,7},{1,0},{2,1},{3,2},{4,3},{5,4},{6,5},{7,6},{8,15},{9,8},{10,9... | collective-permute-start | bytes 393224 | tf_op jit(solution)/shard_map/ppermute | solution.py:46
  70.5 6.2 %collective-permute-start.22 = (bf16[2,2,16,1024]{3,2,1,0:T(8,128)(2,1)S(1)}, bf16[2,2,16,1024]{3,2,1,0:T(8,128)(2,1)S(1)}, u32[]{:S(2)}, u32[]{:S(2)}) collective-permute-start(bf16[2,2,16,1024]{3,2,1,0:T(8,128)(2,1)S(1)} %shard_map.51.refs_0_), channel_id=1, source_target_pairs={{0,2},{1,3},{2,4},{3,5},{4,6},{5,7},{6,0},{7,1},{8,10},{9,11},{10,... | collective-permute-start | bytes 393224 | tf_op jit(solution)/shard_map/ppermute | solution.py:46
  71.5 7.7 %collective-permute-start.21 = (bf16[2,2,16,1024]{3,2,1,0:T(8,128)(2,1)S(1)}, bf16[2,2,16,1024]{3,2,1,0:T(8,128)(2,1)S(1)}, u32[]{:S(2)}, u32[]{:S(2)}) collective-permute-start(bf16[2,2,16,1024]{3,2,1,0:T(8,128)(2,1)S(1)} %shard_map.51.refs_0_), channel_id=1, source_target_pairs={{0,1},{1,2},{2,3},{3,4},{4,5},{5,6},{6,7},{7,0},{8,9},{9,10},{10,1... | collective-permute-start | bytes 393224 | tf_op jit(solution)/shard_map/ppermute | solution.py:46
  74.7 5.7 %collective-permute-start.28 = (bf16[2,16,1024]{2,1,0:T(8,128)(2,1)S(1)}, bf16[2,16,1024]{2,1,0:T(8,128)(2,1)S(1)}, u32[]{:S(2)}, u32[]{:S(2)}) collective-permute-start(bf16[2,16,1024]{2,1,0:T(8,128)(2,1)S(1)} %slice_bitcast_fusion.2), channel_id=1, source_target_pairs={{0,6},{1,7},{2,0},{3,1},{4,2},{5,3},{6,4},{7,5},{8,14},{9,15},{10,... | collective-permute-start | bytes 196616 | tf_op jit(solution)/shard_map/ppermute | solution.py:46
  76.7 9.3 %collective-permute-start.25 = (bf16[2,2,16,1024]{3,2,1,0:T(8,128)(2,1)S(1)}, bf16[2,2,16,1024]{3,2,1,0:T(8,128)(2,1)S(1)}, u32[]{:S(2)}, u32[]{:S(2)}) collective-permute-start(bf16[2,2,16,1024]{3,2,1,0:T(8,128)(2,1)S(1)} %collective-permute-done.24.refs_5_), channel_id=1, source_target_pairs={{0,7},{1,0},{2,1},{3,2},{4,3},{5,4},{6,5},{7,6},{8,15},{9,8},{10,9... | collective-permute-start | bytes 393224 | tf_op jit(solution)/shard_map/ppermute | solution.py:46
  76.7 9.3 %collective-permute-start.23 = (bf16[2,2,16,1024]{3,2,1,0:T(8,128)(2,1)S(1)}, bf16[2,2,16,1024]{3,2,1,0:T(8,128)(2,1)S(1)}, u32[]{:S(2)}, u32[]{:S(2)}) collective-permute-start(bf16[2,2,16,1024]{3,2,1,0:T(8,128)(2,1)S(1)} %collective-permute-done.22.refs_2_), channel_id=1, source_target_pairs={{0,1},{1,2},{2,3},{3,4},{4,5},{5,6},{6,7},{7,0},{8,9},{9,10},{10,1... | collective-permute-start | bytes 393224 | tf_op jit(solution)/shard_map/ppermute | solution.py:46
  79.0 7.0 %collective-permute-start.27 = (bf16[2,16,1024]{2,1,0:T(8,128)(2,1)S(1)}, bf16[2,16,1024]{2,1,0:T(8,128)(2,1)S(1)}, u32[]{:S(2)}, u32[]{:S(2)}) collective-permute-start(bf16[2,16,1024]{2,1,0:T(8,128)(2,1)S(1)} %slice_bitcast_fusion.3), channel_id=1, source_target_pairs={{0,2},{1,3},{2,4},{3,5},{4,6},{5,7},{6,0},{7,1},{8,10},{9,11},{10,... | collective-permute-start | bytes 196616 | tf_op jit(solution)/shard_map/ppermute | solution.py:46
  87.9 20.8 %collective-permute-start.29 = (f32[2,128,1024]{2,1,0:T(8,128)S(1)}, f32[2,128,1024]{2,1,0:T(8,128)S(1)}, u32[]{:S(2)}, u32[]{:S(2)}) collective-permute-start(f32[2,128,1024]{2,1,0:T(8,128)S(1)} %get-tuple-element.52), channel_id=1, source_target_pairs={{0,16},{16,0},{32,48},{48,32},{64,80},{80,64},{96,112},{112,96},{1... | collective-permute-start | bytes 3145736 | tf_op jit(solution)/shard_map/ppermute | solution.py:46

commit v6 on v5

--- a/solution.py
+++ b/solution.py
@@ -31,7 +31,6 @@
 TO_X = dp_perm(lambda x, y, c: (1 - x, y, c))
 TO_UP = dp_perm(lambda x, y, c: (x, (y + 1) % Y, c))
 TO_DOWN = dp_perm(lambda x, y, c: (x, (y - 1) % Y, c))
-TO_UP_2 = dp_perm(lambda x, y, c: (x, (y + 2) % Y, c))
 
 
 X_HI, Z = 2, 8
@@ -96,8 +95,9 @@
     return mean_a, mean_b, square_a, square_b, product
 
 
-def merge_body(rows, one, other, out):
-    for k, value in enumerate(merge(rows, one, other)):
+def merge_body(rows, *refs):
+    *parts, out = refs
+    for k, value in enumerate(merge(rows, *parts)):
         out[k * SUB : (k + 1) * SUB, :] = value
 
 
@@ -287,20 +287,25 @@
     work = 2 * 2 * CORES * rows * half * cols
 
     views = jnp.stack([view_a, view_b])
-    from_down, from_up = send(views, TO_UP), send(views, TO_DOWN)
+    from_down, from_up, from_x = send(views, TO_UP), send(views, TO_DOWN), send(views, TO_X)
     sib = send(views, TO_CORE)
-    moments = call(moments_body, shape(5 * SUB, LANE), views)
-    for rank, to in enumerate((TO_CORE, TO_X)):
-        body = functools.partial(merge_body, rows * 2**rank)
-        moments = call(body, shape(5 * SUB, LANE), moments, send(moments, to))
-    late_views, moments = lax.optimization_barrier((views, moments))
-    from_x = send(late_views, TO_X)
-    moments = [moments, *(send(moments, to) for to in (TO_UP, TO_DOWN, TO_UP_2))]
-    from_down, from_up, moments[2] = lax.optimization_barrier((from_down, from_up, moments[2]))
-    from_x, moments[3] = lax.optimization_barrier((from_x, moments[3]))
+    tile = shape(5 * SUB, LANE)
+    moments = call(moments_body, tile, views)
+    moments = call(
+        functools.partial(merge_body, rows), tile, moments, send(moments, TO_CORE)
+    )
+    below, above = send(moments, TO_UP), send(moments, TO_DOWN)
+    from_down, from_up, below, above = lax.optimization_barrier((from_down, from_up, below, above))
+    opposite = send(below, TO_UP)
+    from_x, opposite = lax.optimization_barrier((from_x, opposite))
+    moments = call(
+        functools.partial(merge_body, CORES * rows), tile, moments, below, above, opposite
+    )
+    moments_x = send(moments, TO_X)
     far_a, far_b = send(from_down[0], TO_UP), send(from_up[1], TO_DOWN)
     from_x = call(copy_body, jax.ShapeDtypeStruct(from_x.shape, bf16), from_x, flops=10**10)
     x_down, x_up = send(from_x, TO_UP), send(from_x, TO_DOWN)
+    far_b, moments_x = lax.optimization_barrier((far_b, moments_x))
     far = call(stack_body, jax.ShapeDtypeStruct(views.shape, bf16), far_a, far_b, flops=10**10)
     x_far = send(far, TO_X)
 
@@ -313,7 +318,8 @@
     stats, lead, near, gram_near = call(
         functools.partial(near_body, batch),
         (shape(5, cols), shape(2, CORES * rows, cols, dtype=bf16), *results(4)),
-        *moments,
+        moments,
+        moments_x,
         sib,
         views,
         from_down,

time: 110 us -> 110 us (level)
  blocking collectives: 10.3 us -> 11.8 us
  starting transfers between devices: 53 us -> 51.9 us
    all_to_all x1, blocking collectives: 10.3 us -> 11.8 us  [on_device(): sums = lax.all_to_all(sums, 'dp', 0, 0)]
    ppermute x30, starting transfers between devices: 53 us -> 51.9 us  [send(): return lax.ppermute(x, axis, to)]
where the time goes in v6:
time: 110 us; the launch traced here: 109 us
  starting transfers between devices  51.9 us (47%)
  waiting for transfers between devices  37.4 us (34%)
  blocking collectives  11.8 us (11%)
  Pallas kernels  6.42 us (6%)
    ppermute x30, starting transfers between devices, send(): return lax.ppermute(x, axis, to)  51.9 us
    ppermute x30, waiting for transfers between devices, send(): return lax.ppermute(x, axis, to)  37.4 us
    all_to_all x1, blocking collectives, on_device(): sums = lax.all_to_all(sums, 'dp', 0, 0)  11.8 us
    pallas_call x13, Pallas kernels, call(): pl.pallas_call(body, out_shape=outs, in_specs=[pl.BlockSpec(memory_space=...  6.42 us
  transfers between devices with their start and end apart: 30, of which 16 were waited for; matrix products, arithmetic and copies ran while one was open for 0% of the time, Pallas kernels for 3%

profile of v6, /device:TPU:1, one launch (start us, length us, event | category | flops | bytes accessed | tf_op | source)
XLA Modules:
  0.0 109.4 jit_solution(14200137731484969378)
XLA Ops:
  0.6 1.1 pad_maximum_fusion.views.refs_3_
  1.7 3.6 %collective-permute-start.2 = (bf16[2,128,1024]{2,1,0:T(8,128)(2,1)S(1)}, bf16[2,128,1024]{2,1,0:T(8,128)(2,1)S(1)}, u32[]{:S(2)}, u32[]{:S(2)}) collective-permute-start(bf16[2,128,1024]{2,1,0:T(8,128)(2,1)S(1)} %pad_maximum_fusion.views.refs_3_), channel_id=1, source_target_pairs={{0,96},{16,112},{32,0},{48,16},{64,32},{80,48},{96,64},{112,80},{1... | collective-permute-start | bytes 1572872 | tf_op jit(solution)/shard_map/ppermute | solution.py:45
  5.4 1.2 %collective-permute-start.5 = (bf16[2,128,1024]{2,1,0:T(8,128)(2,1)S(1)}, bf16[2,128,1024]{2,1,0:T(8,128)(2,1)S(1)}, u32[]{:S(2)}, u32[]{:S(2)}) collective-permute-start(bf16[2,128,1024]{2,1,0:T(8,128)(2,1)S(1)} %pad_maximum_fusion.views.refs_3_), channel_id=1, source_target_pairs={{0,128},{16,144},{32,160},{48,176},{64,192},{80,208},{96,224},{112... | collective-permute-start | bytes 1572872 | tf_op jit(solution)/shard_map/ppermute | solution.py:45
  6.6 0.3 shard_map.41.refs_0_
  6.9 1.3 %collective-permute-start = (f32[40,128]{1,0:T(8,128)S(1)}, f32[40,128]{1,0:T(8,128)S(1)}, u32[]{:S(2)}, u32[]{:S(2)}) collective-permute-start(f32[40,128]{1,0:T(8,128)S(1)} %shard_map.41.refs_0_), channel_id=1, source_target_pairs={{0,16},{16,0},{32,48},{48,32},{64,80},{80,64},{96,112},{112,96},{1... | collective-permute-start | bytes 61448 | tf_op jit(solution)/shard_map/ppermute | solution.py:45
  8.2 0.8 collective-permute-done.refs_1_
  9.1 3.0 %collective-permute-start.4 = (f32[40,128]{1,0:T(8,128)S(1)}, f32[40,128]{1,0:T(8,128)S(1)}, u32[]{:S(2)}, u32[]{:S(2)}) collective-permute-start(f32[40,128]{1,0:T(8,128)S(1)} %shard_map.42.refs_0_), channel_id=1, source_target_pairs={{0,96},{16,112},{32,0},{48,16},{64,32},{80,48},{96,64},{112,80},{1... | collective-permute-start | bytes 61448 | tf_op jit(solution)/shard_map/ppermute | solution.py:45
  12.1 4.3 %collective-permute-done.4.refs_2_ = f32[40,128]{1,0:T(8,128)S(1)} collective-permute-done((f32[40,128]{1,0:T(8,128)S(1)}, f32[40,128]{1,0:T(8,128)S(1)}, u32[]{:S(2)}, u32[]{:S(2)}) %collective-permute-start.4) | collective-permute-done | bytes 20512 | tf_op jit(solution)/shard_map/ppermute | solution.py:45
  16.4 1.5 %collective-permute-start.9 = (bf16[2,128,1024]{2,1,0:T(8,128)(2,1)S(1)}, bf16[2,128,1024]{2,1,0:T(8,128)(2,1)S(1)}, u32[]{:S(2)}, u32[]{:S(2)}) collective-permute-start(bf16[2,128,1024]{2,1,0:T(8,128)(2,1)S(1)} %pad_maximum_fusion.views.refs_3_), channel_id=1, source_target_pairs={{0,16},{16,0},{32,48},{48,32},{64,80},{80,64},{96,112},{112,96},{1... | collective-permute-start | bytes 1572872 | tf_op jit(solution)/shard_map/ppermute | solution.py:45
  17.9 1.5 %collective-permute-done.3.refs_1_ = f32[40,128]{1,0:T(8,128)S(1)} collective-permute-done((f32[40,128]{1,0:T(8,128)S(1)}, f32[40,128]{1,0:T(8,128)S(1)}, u32[]{:S(2)}, u32[]{:S(2)}) %collective-permute-start.3) | collective-permute-done | bytes 20512 | tf_op jit(solution)/shard_map/ppermute | solution.py:45
  19.5 0.7 collective-permute-start.10
  20.2 2.2 %collective-permute-start.7 = (bf16[128,1024]{1,0:T(8,128)(2,1)S(1)}, bf16[128,1024]{1,0:T(8,128)(2,1)S(1)}, u32[]{:S(2)}, u32[]{:S(2)}) collective-permute-start(bf16[128,1024]{1,0:T(8,128)(2,1)S(1)} %slice_bitcast_fusion.1), channel_id=1, source_target_pairs={{0,96},{16,112},{32,0},{48,16},{64,32},{80,48},{96,64},{112,80},{1... | collective-permute-start | bytes 786440 | tf_op jit(solution)/shard_map/ppermute | solution.py:45
  22.4 0.9 collective-permute-done.6.refs_3_
  23.3 1.3 %collective-permute-start.8 = (f32[40,128]{1,0:T(8,128)S(1)}, f32[40,128]{1,0:T(8,128)S(1)}, u32[]{:S(2)}, u32[]{:S(2)}) collective-permute-start(f32[40,128]{1,0:T(8,128)S(1)} %shard_map.43.refs_0_), channel_id=1, source_target_pairs={{0,128},{16,144},{32,160},{48,176},{64,192},{80,208},{96,224},{112... | collective-permute-start | bytes 61448 | tf_op jit(solution)/shard_map/ppermute | solution.py:45
  24.7 0.8 collective-permute-start.13
  25.5 0.9 collective-permute-done.8.refs_1_
  26.4 1.8 %collective-permute-done.7.b.far_b = bf16[128,1024]{1,0:T(8,128)(2,1)S(1)} collective-permute-done((bf16[128,1024]{1,0:T(8,128)(2,1)S(1)}, bf16[128,1024]{1,0:T(8,128)(2,1)S(1)}, u32[]{:S(2)}, u32[]{:S(2)}) %collective-permute-start.7) | collective-permute-done | bytes 262176 | tf_op jit(solution)/shard_map/ppermute | solution.py:45
  28.2 1.5 %collective-permute-start.11 = (bf16[2,128,1024]{2,1,0:T(8,128)(2,1)S(1)}, bf16[2,128,1024]{2,1,0:T(8,128)(2,1)S(1)}, u32[]{:S(2)}, u32[]{:S(2)}) collective-permute-start(bf16[2,128,1024]{2,1,0:T(8,128)(2,1)S(1)} %shard_map.46), channel_id=1, source_target_pairs={{0,128},{16,144},{32,160},{48,176},{64,192},{80,208},{96,224},{112... | collective-permute-start | bytes 1572872 | tf_op jit(solution)/shard_map/ppermute | solution.py:45
  29.7 1.4 %shard_map.45 = (f32[5,1024]{1,0:T(8,128)S(1)}, bf16[2,256,1024]{2,1,0:T(8,128)(2,1)S(1)}, bf16[2,512,1024]{2,1,0:T(8,128)(2,1)S(1)}, bf16[2,256,512]{2,1,0:T(8,128)(2,1)S(1)}) custom-call(f32[40,128]{1,0:T(8,128)S(1)} %shard_map.43.refs_0_, f32[40,128]{1,0:T(8,128)S(1)} %collective-permute-done.8.refs_1_, ...), custom_call_target="tpu_custom_call" | custom-call | flops 536870912 | bytes 6352896 | tf_op jit(solution)/shard_map/pallas_call | solution.py:52
  31.1 7.1 %collective-permute-done.13.x_up = bf16[2,128,1024]{2,1,0:T(8,128)(2,1)S(1)} collective-permute-done((bf16[2,128,1024]{2,1,0:T(8,128)(2,1)S(1)}, bf16[2,128,1024]{2,1,0:T(8,128)(2,1)S(1)}, u32[]{:S(2)}, u32[]{:S(2)}) %collective-permute-start.13) | collective-permute-done | bytes 524320 | tf_op jit(solution)/shard_map/ppermute | solution.py:45
  38.2 1.0 shard_map.47
  39.3 0.5 shard_map.48
  39.8 1.7 %collective-permute-start.14 = (bf16[2,2,2,16,1024]{4,3,2,1,0:T(8,128)(2,1)S(1)}, bf16[2,2,2,16,1024]{4,3,2,1,0:T(8,128)(2,1)S(1)}, u32[]{:S(2)}, u32[]{:S(2)}) collective-permute-start(bf16[2,2,2,16,1024]{4,3,2,1,0:T(8,128)(2,1)S(1)} %get-tuple-element.42), channel_id=1, source_target_pairs={{0,1},{1,2},{2,3},{3,4},{4,5},{5,6},{6,7},{7,0},{8,9},{9,10},{10,1... | collective-permute-start | bytes 786440 | tf_op jit(solution)/shard_map/ppermute | solution.py:45
  41.5 4.0 %collective-permute-start.15 = (bf16[2,2,2,16,1024]{4,3,2,1,0:T(8,128)(2,1)S(1)}, bf16[2,2,2,16,1024]{4,3,2,1,0:T(8,128)(2,1)S(1)}, u32[]{:S(2)}, u32[]{:S(2)}) collective-permute-start(bf16[2,2,2,16,1024]{4,3,2,1,0:T(8,128)(2,1)S(1)} %get-tuple-element.43), channel_id=1, source_target_pairs={{0,7},{1,0},{2,1},{3,2},{4,3},{5,4},{6,5},{7,6},{8,15},{9,8},{10,9... | collective-permute-start | bytes 786440 | tf_op jit(solution)/shard_map/ppermute | solution.py:45
  45.5 3.6 %collective-permute-start.17 = (bf16[2,16,1024]{2,1,0:T(8,128)(2,1)S(1)}, bf16[2,16,1024]{2,1,0:T(8,128)(2,1)S(1)}, u32[]{:S(2)}, u32[]{:S(2)}) collective-permute-start(bf16[2,16,1024]{2,1,0:T(8,128)(2,1)S(1)} %get-tuple-element.45), channel_id=1, source_target_pairs={{0,6},{1,7},{2,0},{3,1},{4,2},{5,3},{6,4},{7,5},{8,14},{9,15},{10,... | collective-permute-start | bytes 196616 | tf_op jit(solution)/shard_map/ppermute | solution.py:45
  49.1 2.5 %collective-permute-done.16.half_a = bf16[2,16,1024]{2,1,0:T(8,128)(2,1)S(1)} collective-permute-done((bf16[2,16,1024]{2,1,0:T(8,128)(2,1)S(1)}, bf16[2,16,1024]{2,1,0:T(8,128)(2,1)S(1)}, u32[]{:S(2)}, u32[]{:S(2)}) %collective-permute-start.16) | collective-permute-done | bytes 65568 | tf_op jit(solution)/shard_map/ppermute | solution.py:45
  51.7 1.4 %collective-permute-done.17.half_b = bf16[2,16,1024]{2,1,0:T(8,128)(2,1)S(1)} collective-permute-done((bf16[2,16,1024]{2,1,0:T(8,128)(2,1)S(1)}, bf16[2,16,1024]{2,1,0:T(8,128)(2,1)S(1)}, u32[]{:S(2)}, u32[]{:S(2)}) %collective-permute-start.17) | collective-permute-done | bytes 65568 | tf_op jit(solution)/shard_map/ppermute | solution.py:45
  53.2 2.2 %collective-permute-start.18 = (bf16[2,2,16,1024]{3,2,1,0:T(8,128)(2,1)S(1)}, bf16[2,2,16,1024]{3,2,1,0:T(8,128)(2,1)S(1)}, u32[]{:S(2)}, u32[]{:S(2)}) collective-permute-start(bf16[2,2,16,1024]{3,2,1,0:T(8,128)(2,1)S(1)} %get-tuple-element.48), channel_id=1, source_target_pairs={{0,2},{1,3},{2,4},{3,5},{4,6},{5,7},{6,0},{7,1},{8,10},{9,11},{10,... | collective-permute-start | bytes 393224 | tf_op jit(solution)/shard_map/ppermute | solution.py:45
  55.4 1.4 %collective-permute-start.19 = (bf16[2,2,16,1024]{3,2,1,0:T(8,128)(2,1)S(1)}, bf16[2,2,16,1024]{3,2,1,0:T(8,128)(2,1)S(1)}, u32[]{:S(2)}, u32[]{:S(2)}) collective-permute-start(bf16[2,2,16,1024]{3,2,1,0:T(8,128)(2,1)S(1)} %get-tuple-element.49), channel_id=1, source_target_pairs={{0,6},{1,7},{2,0},{3,1},{4,2},{5,3},{6,4},{7,5},{8,14},{9,15},{10,... | collective-permute-start | bytes 393224 | tf_op jit(solution)/shard_map/ppermute | solution.py:45
  56.8 2.7 %collective-permute-done.18.far_up = bf16[2,2,16,1024]{3,2,1,0:T(8,128)(2,1)S(1)} collective-permute-done((bf16[2,2,16,1024]{3,2,1,0:T(8,128)(2,1)S(1)}, bf16[2,2,16,1024]{3,2,1,0:T(8,128)(2,1)S(1)}, u32[]{:S(2)}, u32[]{:S(2)}) %collective-permute-start.18) | collective-permute-done | bytes 131104 | tf_op jit(solution)/shard_map/ppermute | solution.py:45
  59.5 1.5 %collective-permute-done.19.far_down = bf16[2,2,16,1024]{3,2,1,0:T(8,128)(2,1)S(1)} collective-permute-done((bf16[2,2,16,1024]{3,2,1,0:T(8,128)(2,1)S(1)}, bf16[2,2,16,1024]{3,2,1,0:T(8,128)(2,1)S(1)}, u32[]{:S(2)}, u32[]{:S(2)}) %collective-permute-start.19) | collective-permute-done | bytes 131104 | tf_op jit(solution)/shard_map/ppermute | solution.py:45
  61.0 0.1 shard_map.50.a
  61.1 3.8 %collective-permute-start.20 = (bf16[2,2,16,1024]{3,2,1,0:T(8,128)(2,1)S(1)}, bf16[2,2,16,1024]{3,2,1,0:T(8,128)(2,1)S(1)}, u32[]{:S(2)}, u32[]{:S(2)}) collective-permute-start(bf16[2,2,16,1024]{3,2,1,0:T(8,128)(2,1)S(1)} %shard_map.50.a), channel_id=1, source_target_pairs={{0,8},{1,9},{2,10},{3,11},{4,12},{5,13},{6,14},{7,15},{8,0},{9,1},... | collective-permute-start | bytes 393224 | tf_op jit(solution)/shard_map/ppermute | solution.py:45
  64.8 2.4 %collective-permute-done.20.b = bf16[2,2,16,1024]{3,2,1,0:T(8,128)(2,1)S(1)} collective-permute-done((bf16[2,2,16,1024]{3,2,1,0:T(8,128)(2,1)S(1)}, bf16[2,2,16,1024]{3,2,1,0:T(8,128)(2,1)S(1)}, u32[]{:S(2)}, u32[]{:S(2)}) %collective-permute-start.20) | collective-permute-done | bytes 131104 | tf_op jit(solution)/shard_map/ppermute | solution.py:45
  67.2 1.6 %collective-permute-start.24 = (bf16[2,2,16,1024]{3,2,1,0:T(8,128)(2,1)S(1)}, bf16[2,2,16,1024]{3,2,1,0:T(8,128)(2,1)S(1)}, u32[]{:S(2)}, u32[]{:S(2)}) collective-permute-start(bf16[2,2,16,1024]{3,2,1,0:T(8,128)(2,1)S(1)} %shard_map.51.refs_0_), channel_id=1, source_target_pairs={{0,6},{1,7},{2,0},{3,1},{4,2},{5,3},{6,4},{7,5},{8,14},{9,15},{10,... | collective-permute-start | bytes 393224 | tf_op jit(solution)/shard_map/ppermute | solution.py:45
  68.8 0.9 collective-permute-start.22
  69.7 1.5 %collective-permute-start.21 = (bf16[2,2,16,1024]{3,2,1,0:T(8,128)(2,1)S(1)}, bf16[2,2,16,1024]{3,2,1,0:T(8,128)(2,1)S(1)}, u32[]{:S(2)}, u32[]{:S(2)}) collective-permute-start(bf16[2,2,16,1024]{3,2,1,0:T(8,128)(2,1)S(1)} %shard_map.51.refs_0_), channel_id=1, source_target_pairs={{0,1},{1,2},{2,3},{3,4},{4,5},{5,6},{6,7},{7,0},{8,9},{9,10},{10,1... | collective-permute-start | bytes 393224 | tf_op jit(solution)/shard_map/ppermute | solution.py:45
  71.1 1.9 %collective-permute-done.24.refs_5_ = bf16[2,2,16,1024]{3,2,1,0:T(8,128)(2,1)S(1)} collective-permute-done((bf16[2,2,16,1024]{3,2,1,0:T(8,128)(2,1)S(1)}, bf16[2,2,16,1024]{3,2,1,0:T(8,128)(2,1)S(1)}, u32[]{:S(2)}, u32[]{:S(2)}) %collective-permute-start.24) | collective-permute-done | bytes 131104 | tf_op jit(solution)/shard_map/ppermute | solution.py:45
  73.1 1.9 %collective-permute-start.28 = (bf16[2,16,1024]{2,1,0:T(8,128)(2,1)S(1)}, bf16[2,16,1024]{2,1,0:T(8,128)(2,1)S(1)}, u32[]{:S(2)}, u32[]{:S(2)}) collective-permute-start(bf16[2,16,1024]{2,1,0:T(8,128)(2,1)S(1)} %slice_bitcast_fusion.2), channel_id=1, source_target_pairs={{0,6},{1,7},{2,0},{3,1},{4,2},{5,3},{6,4},{7,5},{8,14},{9,15},{10,... | collective-permute-start | bytes 196616 | tf_op jit(solution)/shard_map/ppermute | solution.py:45
  75.0 0.9 collective-permute-done.22.refs_2_
  76.0 1.6 %collective-permute-start.23 = (bf16[2,2,16,1024]{3,2,1,0:T(8,128)(2,1)S(1)}, bf16[2,2,16,1024]{3,2,1,0:T(8,128)(2,1)S(1)}, u32[]{:S(2)}, u32[]{:S(2)}) collective-permute-start(bf16[2,2,16,1024]{3,2,1,0:T(8,128)(2,1)S(1)} %collective-permute-done.22.refs_2_), channel_id=1, source_target_pairs={{0,1},{1,2},{2,3},{3,4},{4,5},{5,6},{6,7},{7,0},{8,9},{9,10},{10,1... | collective-permute-start | bytes 393224 | tf_op jit(solution)/shard_map/ppermute | solution.py:45
  77.6 0.2 collective-permute-start.27
  77.8 2.6 %collective-permute-done.28.refs_8_ = bf16[2,16,1024]{2,1,0:T(8,128)(2,1)S(1)} collective-permute-done((bf16[2,16,1024]{2,1,0:T(8,128)(2,1)S(1)}, bf16[2,16,1024]{2,1,0:T(8,128)(2,1)S(1)}, u32[]{:S(2)}, u32[]{:S(2)}) %collective-permute-start.28) | collective-permute-done | bytes 65568 | tf_op jit(solution)/shard_map/ppermute | solution.py:45
  80.4 3.9 %collective-permute-done.27.refs_7_ = bf16[2,16,1024]{2,1,0:T(8,128)(2,1)S(1)} collective-permute-done((bf16[2,16,1024]{2,1,0:T(8,128)(2,1)S(1)}, bf16[2,16,1024]{2,1,0:T(8,128)(2,1)S(1)}, u32[]{:S(2)}, u32[]{:S(2)}) %collective-permute-start.27) | collective-permute-done | bytes 65568 | tf_op jit(solution)/shard_map/ppermute | solution.py:45
  84.3 2.0 %shard_map.52 = (f32[2,128,1024]{2,1,0:T(8,128)S(1)}, f32[2,128,1024]{2,1,0:T(8,128)S(1)}, f32[16,4,1024]{2,1,0:T(4,128)S(1)}) custom-call(bf16[2,2,16,1024]{3,2,1,0:T(8,128)(2,1)S(1)} %shard_map.51.refs_0_, bf16[2,2,16,1024]{3,2,1,0:T(8,128)(2,1)S(1)} %collective-permute-done.21.refs_1_, bf16[2,2,16,1024]{3,2,1,0:T(8,128)(2,1)S(1)} %collective-permute-done.22.refs_2_, ...), custom_call_target="tpu_custom_call" | custom-call | flops 1073741824 | bytes 8671232 | tf_op jit(solution)/shard_map/pallas_call | solution.py:52
  86.3 10.4 %collective-permute-start.29 = (f32[2,128,1024]{2,1,0:T(8,128)S(1)}, f32[2,128,1024]{2,1,0:T(8,128)S(1)}, u32[]{:S(2)}, u32[]{:S(2)}) collective-permute-start(f32[2,128,1024]{2,1,0:T(8,128)S(1)} %get-tuple-element.54), channel_id=1, source_target_pairs={{0,16},{16,0},{32,48},{48,32},{64,80},{80,64},{96,112},{112,96},{1... | collective-permute-start | bytes 3145736 | tf_op jit(solution)/shard_map/ppermute | solution.py:45
  96.7 11.8 %all_to_all.5.sums = f32[16,4,1024]{2,1,0:T(4,128)S(1)} all-to-all(f32[16,4,1024]{2,1,0:T(4,128)S(1)} %get-tuple-element.55), channel_id=1, replica_groups=mesh['dp'=16,'feat'=16] {'dp'}, dimensions={0} | all-to-all | bytes 524288 | tf_op jit(solution)/shard_map/all_to_all | solution.py:360
  108.4 1.0 shard_map.53
  (31 shorter events, 0.3 us)
Async XLA Ops:
  1.7 17.8 %collective-permute-start.2 = (bf16[2,128,1024]{2,1,0:T(8,128)(2,1)S(1)}, bf16[2,128,1024]{2,1,0:T(8,128)(2,1)S(1)}, u32[]{:S(2)}, u32[]{:S(2)}) collective-permute-start(bf16[2,128,1024]{2,1,0:T(8,128)(2,1)S(1)} %pad_maximum_fusion.views.refs_3_), channel_id=1, source_target_pairs={{0,96},{16,112},{32,0},{48,16},{64,32},{80,48},{96,64},{112,80},{1... | collective-permute-start | bytes 1572872 | tf_op jit(solution)/shard_map/ppermute | solution.py:45
  5.4 14.1 %collective-permute-start.1 = (bf16[2,128,1024]{2,1,0:T(8,128)(2,1)S(1)}, bf16[2,128,1024]{2,1,0:T(8,128)(2,1)S(1)}, u32[]{:S(2)}, u32[]{:S(2)}) collective-permute-start(bf16[2,128,1024]{2,1,0:T(8,128)(2,1)S(1)} %pad_maximum_fusion.views.refs_3_), channel_id=1, source_target_pairs={{0,32},{16,48},{32,64},{48,80},{64,96},{80,112},{96,0},{112,16},{1... | collective-permute-start | bytes 1572872 | tf_op jit(solution)/shard_map/ppermute | solution.py:45
  5.4 17.0 %collective-permute-start.5 = (bf16[2,128,1024]{2,1,0:T(8,128)(2,1)S(1)}, bf16[2,128,1024]{2,1,0:T(8,128)(2,1)S(1)}, u32[]{:S(2)}, u32[]{:S(2)}) collective-permute-start(bf16[2,128,1024]{2,1,0:T(8,128)(2,1)S(1)} %pad_maximum_fusion.views.refs_3_), channel_id=1, source_target_pairs={{0,128},{16,144},{32,160},{48,176},{64,192},{80,208},{96,224},{112... | collective-permute-start | bytes 1572872 | tf_op jit(solution)/shard_map/ppermute | solution.py:45
  6.9 2.2 %collective-permute-start = (f32[40,128]{1,0:T(8,128)S(1)}, f32[40,128]{1,0:T(8,128)S(1)}, u32[]{:S(2)}, u32[]{:S(2)}) collective-permute-start(f32[40,128]{1,0:T(8,128)S(1)} %shard_map.41.refs_0_), channel_id=1, source_target_pairs={{0,16},{16,0},{32,48},{48,32},{64,80},{80,64},{96,112},{112,96},{1... | collective-permute-start | bytes 61448 | tf_op jit(solution)/shard_map/ppermute | solution.py:45
  9.1 7.3 %collective-permute-start.4 = (f32[40,128]{1,0:T(8,128)S(1)}, f32[40,128]{1,0:T(8,128)S(1)}, u32[]{:S(2)}, u32[]{:S(2)}) collective-permute-start(f32[40,128]{1,0:T(8,128)S(1)} %shard_map.42.refs_0_), channel_id=1, source_target_pairs={{0,96},{16,112},{32,0},{48,16},{64,32},{80,48},{96,64},{112,80},{1... | collective-permute-start | bytes 61448 | tf_op jit(solution)/shard_map/ppermute | solution.py:45
  12.1 7.4 %collective-permute-start.3 = (f32[40,128]{1,0:T(8,128)S(1)}, f32[40,128]{1,0:T(8,128)S(1)}, u32[]{:S(2)}, u32[]{:S(2)}) collective-permute-start(f32[40,128]{1,0:T(8,128)S(1)} %shard_map.42.refs_0_), channel_id=1, source_target_pairs={{0,32},{16,48},{32,64},{48,80},{64,96},{80,112},{96,0},{112,16},{1... | collective-permute-start | bytes 61448 | tf_op jit(solution)/shard_map/ppermute | solution.py:45
  16.4 13.3 %collective-permute-start.9 = (bf16[2,128,1024]{2,1,0:T(8,128)(2,1)S(1)}, bf16[2,128,1024]{2,1,0:T(8,128)(2,1)S(1)}, u32[]{:S(2)}, u32[]{:S(2)}) collective-permute-start(bf16[2,128,1024]{2,1,0:T(8,128)(2,1)S(1)} %pad_maximum_fusion.views.refs_3_), channel_id=1, source_target_pairs={{0,16},{16,0},{32,48},{48,32},{64,80},{80,64},{96,112},{112,96},{1... | collective-permute-start | bytes 1572872 | tf_op jit(solution)/shard_map/ppermute | solution.py:45
  19.5 3.8 %collective-permute-start.6 = (f32[40,128]{1,0:T(8,128)S(1)}, f32[40,128]{1,0:T(8,128)S(1)}, u32[]{:S(2)}, u32[]{:S(2)}) collective-permute-start(f32[40,128]{1,0:T(8,128)S(1)} %collective-permute-done.3.refs_1_), channel_id=1, source_target_pairs={{0,32},{16,48},{32,64},{48,80},{64,96},{80,112},{96,0},{112,16},{1... | collective-permute-start | bytes 61448 | tf_op jit(solution)/shard_map/ppermute | solution.py:45
  19.5 8.6 %collective-permute-start.10 = (bf16[128,1024]{1,0:T(8,128)(2,1)S(1)}, bf16[128,1024]{1,0:T(8,128)(2,1)S(1)}, u32[]{:S(2)}, u32[]{:S(2)}) collective-permute-start(bf16[128,1024]{1,0:T(8,128)(2,1)S(1)} %slice_bitcast_fusion), channel_id=1, source_target_pairs={{0,32},{16,48},{32,64},{48,80},{64,96},{80,112},{96,0},{112,16},{1... | collective-permute-start | bytes 786440 | tf_op jit(solution)/shard_map/ppermute | solution.py:45
  20.2 8.0 %collective-permute-start.7 = (bf16[128,1024]{1,0:T(8,128)(2,1)S(1)}, bf16[128,1024]{1,0:T(8,128)(2,1)S(1)}, u32[]{:S(2)}, u32[]{:S(2)}) collective-permute-start(bf16[128,1024]{1,0:T(8,128)(2,1)S(1)} %slice_bitcast_fusion.1), channel_id=1, source_target_pairs={{0,96},{16,112},{32,0},{48,16},{64,32},{80,48},{96,64},{112,80},{1... | collective-permute-start | bytes 786440 | tf_op jit(solution)/shard_map/ppermute | solution.py:45
  23.3 3.0 %collective-permute-start.8 = (f32[40,128]{1,0:T(8,128)S(1)}, f32[40,128]{1,0:T(8,128)S(1)}, u32[]{:S(2)}, u32[]{:S(2)}) collective-permute-start(f32[40,128]{1,0:T(8,128)S(1)} %shard_map.43.refs_0_), channel_id=1, source_target_pairs={{0,128},{16,144},{32,160},{48,176},{64,192},{80,208},{96,224},{112... | collective-permute-start | bytes 61448 | tf_op jit(solution)/shard_map/ppermute | solution.py:45
  24.7 13.5 %collective-permute-start.13 = (bf16[2,128,1024]{2,1,0:T(8,128)(2,1)S(1)}, bf16[2,128,1024]{2,1,0:T(8,128)(2,1)S(1)}, u32[]{:S(2)}, u32[]{:S(2)}) collective-permute-start(bf16[2,128,1024]{2,1,0:T(8,128)(2,1)S(1)} %shard_map.44.refs_6_), channel_id=1, source_target_pairs={{0,96},{16,112},{32,0},{48,16},{64,32},{80,48},{96,64},{112,80},{1... | collective-permute-start | bytes 1572872 | tf_op jit(solution)/shard_map/ppermute | solution.py:45
  26.4 11.9 %collective-permute-start.12 = (bf16[2,128,1024]{2,1,0:T(8,128)(2,1)S(1)}, bf16[2,128,1024]{2,1,0:T(8,128)(2,1)S(1)}, u32[]{:S(2)}, u32[]{:S(2)}) collective-permute-start(bf16[2,128,1024]{2,1,0:T(8,128)(2,1)S(1)} %shard_map.44.refs_6_), channel_id=1, source_target_pairs={{0,32},{16,48},{32,64},{48,80},{64,96},{80,112},{96,0},{112,16},{1... | collective-permute-start | bytes 1572872 | tf_op jit(solution)/shard_map/ppermute | solution.py:45
  28.2 11.0 %collective-permute-start.11 = (bf16[2,128,1024]{2,1,0:T(8,128)(2,1)S(1)}, bf16[2,128,1024]{2,1,0:T(8,128)(2,1)S(1)}, u32[]{:S(2)}, u32[]{:S(2)}) collective-permute-start(bf16[2,128,1024]{2,1,0:T(8,128)(2,1)S(1)} %shard_map.46), channel_id=1, source_target_pairs={{0,128},{16,144},{32,160},{48,176},{64,192},{80,208},{96,224},{112... | collective-permute-start | bytes 1572872 | tf_op jit(solution)/shard_map/ppermute | solution.py:45
  39.8 13.3 %collective-permute-start.14 = (bf16[2,2,2,16,1024]{4,3,2,1,0:T(8,128)(2,1)S(1)}, bf16[2,2,2,16,1024]{4,3,2,1,0:T(8,128)(2,1)S(1)}, u32[]{:S(2)}, u32[]{:S(2)}) collective-permute-start(bf16[2,2,2,16,1024]{4,3,2,1,0:T(8,128)(2,1)S(1)} %get-tuple-element.42), channel_id=1, source_target_pairs={{0,1},{1,2},{2,3},{3,4},{4,5},{5,6},{6,7},{7,0},{8,9},{9,10},{10,1... | collective-permute-start | bytes 786440 | tf_op jit(solution)/shard_map/ppermute | solution.py:45
  41.5 11.6 %collective-permute-start.15 = (bf16[2,2,2,16,1024]{4,3,2,1,0:T(8,128)(2,1)S(1)}, bf16[2,2,2,16,1024]{4,3,2,1,0:T(8,128)(2,1)S(1)}, u32[]{:S(2)}, u32[]{:S(2)}) collective-permute-start(bf16[2,2,2,16,1024]{4,3,2,1,0:T(8,128)(2,1)S(1)} %get-tuple-element.43), channel_id=1, source_target_pairs={{0,7},{1,0},{2,1},{3,2},{4,3},{5,4},{6,5},{7,6},{8,15},{9,8},{10,9... | collective-permute-start | bytes 786440 | tf_op jit(solution)/shard_map/ppermute | solution.py:45
  45.5 6.1 %collective-permute-start.16 = (bf16[2,16,1024]{2,1,0:T(8,128)(2,1)S(1)}, bf16[2,16,1024]{2,1,0:T(8,128)(2,1)S(1)}, u32[]{:S(2)}, u32[]{:S(2)}) collective-permute-start(bf16[2,16,1024]{2,1,0:T(8,128)(2,1)S(1)} %get-tuple-element.44), channel_id=1, source_target_pairs={{0,2},{1,3},{2,4},{3,5},{4,6},{5,7},{6,0},{7,1},{8,10},{9,11},{10,... | collective-permute-start | bytes 196616 | tf_op jit(solution)/shard_map/ppermute | solution.py:45
  45.5 7.5 %collective-permute-start.17 = (bf16[2,16,1024]{2,1,0:T(8,128)(2,1)S(1)}, bf16[2,16,1024]{2,1,0:T(8,128)(2,1)S(1)}, u32[]{:S(2)}, u32[]{:S(2)}) collective-permute-start(bf16[2,16,1024]{2,1,0:T(8,128)(2,1)S(1)} %get-tuple-element.45), channel_id=1, source_target_pairs={{0,6},{1,7},{2,0},{3,1},{4,2},{5,3},{6,4},{7,5},{8,14},{9,15},{10,... | collective-permute-start | bytes 196616 | tf_op jit(solution)/shard_map/ppermute | solution.py:45
  53.2 6.3 %collective-permute-start.18 = (bf16[2,2,16,1024]{3,2,1,0:T(8,128)(2,1)S(1)}, bf16[2,2,16,1024]{3,2,1,0:T(8,128)(2,1)S(1)}, u32[]{:S(2)}, u32[]{:S(2)}) collective-permute-start(bf16[2,2,16,1024]{3,2,1,0:T(8,128)(2,1)S(1)} %get-tuple-element.48), channel_id=1, source_target_pairs={{0,2},{1,3},{2,4},{3,5},{4,6},{5,7},{6,0},{7,1},{8,10},{9,11},{10,... | collective-permute-start | bytes 393224 | tf_op jit(solution)/shard_map/ppermute | solution.py:45
  55.4 5.6 %collective-permute-start.19 = (bf16[2,2,16,1024]{3,2,1,0:T(8,128)(2,1)S(1)}, bf16[2,2,16,1024]{3,2,1,0:T(8,128)(2,1)S(1)}, u32[]{:S(2)}, u32[]{:S(2)}) collective-permute-start(bf16[2,2,16,1024]{3,2,1,0:T(8,128)(2,1)S(1)} %get-tuple-element.49), channel_id=1, source_target_pairs={{0,6},{1,7},{2,0},{3,1},{4,2},{5,3},{6,4},{7,5},{8,14},{9,15},{10,... | collective-permute-start | bytes 393224 | tf_op jit(solution)/shard_map/ppermute | solution.py:45
  61.1 6.1 %collective-permute-start.20 = (bf16[2,2,16,1024]{3,2,1,0:T(8,128)(2,1)S(1)}, bf16[2,2,16,1024]{3,2,1,0:T(8,128)(2,1)S(1)}, u32[]{:S(2)}, u32[]{:S(2)}) collective-permute-start(bf16[2,2,16,1024]{3,2,1,0:T(8,128)(2,1)S(1)} %shard_map.50.a), channel_id=1, source_target_pairs={{0,8},{1,9},{2,10},{3,11},{4,12},{5,13},{6,14},{7,15},{8,0},{9,1},... | collective-permute-start | bytes 393224 | tf_op jit(solution)/shard_map/ppermute | solution.py:45
  67.2 5.9 %collective-permute-start.24 = (bf16[2,2,16,1024]{3,2,1,0:T(8,128)(2,1)S(1)}, bf16[2,2,16,1024]{3,2,1,0:T(8,128)(2,1)S(1)}, u32[]{:S(2)}, u32[]{:S(2)}) collective-permute-start(bf16[2,2,16,1024]{3,2,1,0:T(8,128)(2,1)S(1)} %shard_map.51.refs_0_), channel_id=1, source_target_pairs={{0,6},{1,7},{2,0},{3,1},{4,2},{5,3},{6,4},{7,5},{8,14},{9,15},{10,... | collective-permute-start | bytes 393224 | tf_op jit(solution)/shard_map/ppermute | solution.py:45
  68.8 8.8 %collective-permute-start.26 = (bf16[2,2,16,1024]{3,2,1,0:T(8,128)(2,1)S(1)}, bf16[2,2,16,1024]{3,2,1,0:T(8,128)(2,1)S(1)}, u32[]{:S(2)}, u32[]{:S(2)}) collective-permute-start(bf16[2,2,16,1024]{3,2,1,0:T(8,128)(2,1)S(1)} %shard_map.51.refs_0_), channel_id=1, source_target_pairs={{0,7},{1,0},{2,1},{3,2},{4,3},{5,4},{6,5},{7,6},{8,15},{9,8},{10,9... | collective-permute-start | bytes 393224 | tf_op jit(solution)/shard_map/ppermute | solution.py:45
  68.8 7.2 %collective-permute-start.22 = (bf16[2,2,16,1024]{3,2,1,0:T(8,128)(2,1)S(1)}, bf16[2,2,16,1024]{3,2,1,0:T(8,128)(2,1)S(1)}, u32[]{:S(2)}, u32[]{:S(2)}) collective-permute-start(bf16[2,2,16,1024]{3,2,1,0:T(8,128)(2,1)S(1)} %shard_map.51.refs_0_), channel_id=1, source_target_pairs={{0,2},{1,3},{2,4},{3,5},{4,6},{5,7},{6,0},{7,1},{8,10},{9,11},{10,... | collective-permute-start | bytes 393224 | tf_op jit(solution)/shard_map/ppermute | solution.py:45
  69.7 8.1 %collective-permute-start.21 = (bf16[2,2,16,1024]{3,2,1,0:T(8,128)(2,1)S(1)}, bf16[2,2,16,1024]{3,2,1,0:T(8,128)(2,1)S(1)}, u32[]{:S(2)}, u32[]{:S(2)}) collective-permute-start(bf16[2,2,16,1024]{3,2,1,0:T(8,128)(2,1)S(1)} %shard_map.51.refs_0_), channel_id=1, source_target_pairs={{0,1},{1,2},{2,3},{3,4},{4,5},{5,6},{6,7},{7,0},{8,9},{9,10},{10,1... | collective-permute-start | bytes 393224 | tf_op jit(solution)/shard_map/ppermute | solution.py:45
  73.1 7.3 %collective-permute-start.28 = (bf16[2,16,1024]{2,1,0:T(8,128)(2,1)S(1)}, bf16[2,16,1024]{2,1,0:T(8,128)(2,1)S(1)}, u32[]{:S(2)}, u32[]{:S(2)}) collective-permute-start(bf16[2,16,1024]{2,1,0:T(8,128)(2,1)S(1)} %slice_bitcast_fusion.2), channel_id=1, source_target_pairs={{0,6},{1,7},{2,0},{3,1},{4,2},{5,3},{6,4},{7,5},{8,14},{9,15},{10,... | collective-permute-start | bytes 196616 | tf_op jit(solution)/shard_map/ppermute | solution.py:45
  75.0 9.3 %collective-permute-start.25 = (bf16[2,2,16,1024]{3,2,1,0:T(8,128)(2,1)S(1)}, bf16[2,2,16,1024]{3,2,1,0:T(8,128)(2,1)S(1)}, u32[]{:S(2)}, u32[]{:S(2)}) collective-permute-start(bf16[2,2,16,1024]{3,2,1,0:T(8,128)(2,1)S(1)} %collective-permute-done.24.refs_5_), channel_id=1, source_target_pairs={{0,7},{1,0},{2,1},{3,2},{4,3},{5,4},{6,5},{7,6},{8,15},{9,8},{10,9... | collective-permute-start | bytes 393224 | tf_op jit(solution)/shard_map/ppermute | solution.py:45
  76.0 8.4 %collective-permute-start.23 = (bf16[2,2,16,1024]{3,2,1,0:T(8,128)(2,1)S(1)}, bf16[2,2,16,1024]{3,2,1,0:T(8,128)(2,1)S(1)}, u32[]{:S(2)}, u32[]{:S(2)}) collective-permute-start(bf16[2,2,16,1024]{3,2,1,0:T(8,128)(2,1)S(1)} %collective-permute-done.22.refs_2_), channel_id=1, source_target_pairs={{0,1},{1,2},{2,3},{3,4},{4,5},{5,6},{6,7},{7,0},{8,9},{9,10},{10,1... | collective-permute-start | bytes 393224 | tf_op jit(solution)/shard_map/ppermute | solution.py:45
  77.6 6.8 %collective-permute-start.27 = (bf16[2,16,1024]{2,1,0:T(8,128)(2,1)S(1)}, bf16[2,16,1024]{2,1,0:T(8,128)(2,1)S(1)}, u32[]{:S(2)}, u32[]{:S(2)}) collective-permute-start(bf16[2,16,1024]{2,1,0:T(8,128)(2,1)S(1)} %slice_bitcast_fusion.3), channel_id=1, source_target_pairs={{0,2},{1,3},{2,4},{3,5},{4,6},{5,7},{6,0},{7,1},{8,10},{9,11},{10,... | collective-permute-start | bytes 196616 | tf_op jit(solution)/shard_map/ppermute | solution.py:45
  86.3 22.1 %collective-permute-start.29 = (f32[2,128,1024]{2,1,0:T(8,128)S(1)}, f32[2,128,1024]{2,1,0:T(8,128)S(1)}, u32[]{:S(2)}, u32[]{:S(2)}) collective-permute-start(f32[2,128,1024]{2,1,0:T(8,128)S(1)} %get-tuple-element.54), channel_id=1, source_target_pairs={{0,16},{16,0},{32,48},{48,32},{64,80},{80,64},{96,112},{112,96},{1... | collective-permute-start | bytes 3145736 | tf_op jit(solution)/shard_map/ppermute | solution.py:45

commit v7 on v6

--- a/solution.py
+++ b/solution.py
@@ -151,25 +151,20 @@
     multiply(lead, split_views(pairs), stats, normed, gram)
 
 
-def far_body(lead, stats, far_a, far_b, x_down, x_up, normed, gram):
-    pieces = split_views([x_down, x_up])
-    multiply(lead, [[far_a, *pieces[0]], [far_b, *pieces[1]]], stats, normed, gram)
-
-
-def last_body(lead, stats, x_far, gram_near, gram_far, *outs):
+def last_body(lead, stats, opp_a, opp_b, x_down, x_up, x_far, gram_near, *outs):
     normed, mine, up_2, down_2, up_1, down_1, far_a, far_b, gram = outs
     rows, part = x_far.shape[1], mine.shape[2]
-    near, far = gram_near.shape[2], gram_near.shape[2] + gram_far.shape[2]
-    multiply(lead, split_views([x_far]), stats, normed, gram)
+    middle = gram_near.shape[2]
+    pieces = split_views([x_down, x_up, x_far])
+    multiply(lead, [[opp_a, *pieces[0]], [opp_b, *pieces[1]]], stats, normed, gram)
     z = lax.rem(lax.axis_index("feat"), Z)
 
     def store(ahead, v, out):
         start = lax.rem(z + ahead, Z) * part
         for h in range(X_HI):
             r = pl.ds(pl.multiple_of(start + h * rows, part), part)
-            out[h, :, 0:near] = gram_near[v, r, :]
-            out[h, :, near:far] = gram_far[v, r, :]
-            out[h, :, far:] = gram[v, r, :]
+            out[h, :, 0:middle] = gram_near[v, r, :]
+            out[h, :, middle:] = gram[v, r, :]
 
     for v in range(2):
         store(0, v, mine.at[v])
@@ -229,7 +224,7 @@
 
 
 def apply_body(scale, *refs):
-    *blocks, from_4a, from_4b, near, far, last, lead, stats, own, other, sums, gram = refs
+    *blocks, from_4a, from_4b, near, last, lead, stats, own, other, sums, gram = refs
     rows, part = own.shape[1], blocks[0].shape[2]
     z = lax.rem(lax.axis_index("feat"), Z)
 
@@ -243,13 +238,13 @@
             load(back, v, block.at[v])
         load(4, v, (from_4a, from_4b)[v])
     diag = stats[4:5, :]
-    ends = (0, near.shape[1], near.shape[1] + far.shape[1], gram.shape[2])
+    ends = (0, near.shape[1], gram.shape[2])
     for v in range(2):
         first = second = 0.0
         for h, out in enumerate((own, other)):
             r = slice(h * rows, (h + 1) * rows)
             up = 0.0
-            for i, normed in enumerate((near, far, last)):
+            for i, normed in enumerate((near, last)):
                 left = gram[1 - v, r, ends[i] : ends[i + 1]]
                 up = up + jnp.dot(left, normed[v], preferred_element_type=f32)
             up = scale * up
@@ -327,22 +322,22 @@
         from_x,
         flops=work // 2,
     )
-    far, gram_far = call(
-        far_body, results(3), lead, stats, far_a, far_b, x_down, x_up, flops=work * 3 // 8
-    )
     one = shape(X_HI, part, half, dtype=bf16)
     both = shape(2, *one.shape, dtype=bf16)
     four = shape(2, *both.shape, dtype=bf16)
     last, *chunks = call(
         last_body,
-        (results(1)[0], both, both, both, four, four, one, one),
+        (results(4)[0], both, both, both, four, four, one, one),
         lead,
         stats,
+        far_a,
+        far_b,
+        x_down,
+        x_up,
         x_far,
         gram_near,
-        gram_far,
-        flops=work // 8,
-        scratch=[pltpu.VMEM(results(1)[1].shape, bf16)],
+        flops=work // 2,
+        scratch=[pltpu.VMEM(results(4)[1].shape, bf16)],
     )
     blocks = spread_rows(reduce_rows(*chunks))
     own, other, sums = call(
@@ -350,7 +345,6 @@
         (shape(2, rows, cols), shape(2, rows, cols), shape(dp_count, 4, cols)),
         *blocks,
         near,
-        far,
         last,
         lead,
         stats,

time: 110 us -> 109 us (level)
    pallas_call x13 -> x12, Pallas kernels: 6.42 us -> 5.9 us  [call(): pl.pallas_call(body, out_shape=outs, in_specs=[pl.BlockSpec(memory_space=...]
  transfers between devices with their start and end apart: 30 -> 30, of which waited for: 16 -> 17; matrix products, arithmetic and copies ran while one was open for 0% -> 0% of each run, Pallas kernels for 3% -> 2%
where the time goes in v7:
time: 109 us
  starting transfers between devices  51.6 us (47%)
  waiting for transfers between devices  37.8 us (35%)
  blocking collectives  11.6 us (11%)
  Pallas kernels  5.9 us (5%)
    ppermute x30, starting transfers between devices, send(): return lax.ppermute(x, axis, to)  51.6 us
    ppermute x30, waiting for transfers between devices, send(): return lax.ppermute(x, axis, to)  37.8 us
    all_to_all x1, blocking collectives, on_device(): sums = lax.all_to_all(sums, 'dp', 0, 0)  11.6 us
    pallas_call x12, Pallas kernels, call(): pl.pallas_call(body, out_shape=outs, in_specs=[pl.BlockSpec(memory_space=...  5.9 us
  transfers between devices with their start and end apart: 30, of which 17 were waited for; matrix products, arithmetic and copies ran while one was open for 0% of the time, Pallas kernels for 2%

profile of v7, /device:TPU:1, one launch (start us, length us, event | category | flops | bytes accessed | tf_op | source)
XLA Modules:
  0.0 108.8 jit_solution(7787329167238736039)
XLA Ops:
  0.6 1.1 pad_maximum_fusion.views.refs_3_
  1.7 3.6 %collective-permute-start.2 = (bf16[2,128,1024]{2,1,0:T(8,128)(2,1)S(1)}, bf16[2,128,1024]{2,1,0:T(8,128)(2,1)S(1)}, u32[]{:S(2)}, u32[]{:S(2)}) collective-permute-start(bf16[2,128,1024]{2,1,0:T(8,128)(2,1)S(1)} %pad_maximum_fusion.views.refs_3_), channel_id=1, source_target_pairs={{0,96},{16,112},{32,0},{48,16},{64,32},{80,48},{96,64},{112,80},{1... | collective-permute-start | bytes 1572872 | tf_op jit(solution)/shard_map/ppermute | solution.py:45
  5.4 1.2 %collective-permute-start.5 = (bf16[2,128,1024]{2,1,0:T(8,128)(2,1)S(1)}, bf16[2,128,1024]{2,1,0:T(8,128)(2,1)S(1)}, u32[]{:S(2)}, u32[]{:S(2)}) collective-permute-start(bf16[2,128,1024]{2,1,0:T(8,128)(2,1)S(1)} %pad_maximum_fusion.views.refs_3_), channel_id=1, source_target_pairs={{0,128},{16,144},{32,160},{48,176},{64,192},{80,208},{96,224},{112... | collective-permute-start | bytes 1572872 | tf_op jit(solution)/shard_map/ppermute | solution.py:45
  6.6 0.3 shard_map.41.refs_0_
  6.9 1.3 %collective-permute-start = (f32[40,128]{1,0:T(8,128)S(1)}, f32[40,128]{1,0:T(8,128)S(1)}, u32[]{:S(2)}, u32[]{:S(2)}) collective-permute-start(f32[40,128]{1,0:T(8,128)S(1)} %shard_map.41.refs_0_), channel_id=1, source_target_pairs={{0,16},{16,0},{32,48},{48,32},{64,80},{80,64},{96,112},{112,96},{1... | collective-permute-start | bytes 61448 | tf_op jit(solution)/shard_map/ppermute | solution.py:45
  8.2 0.8 collective-permute-done.refs_1_
  9.1 3.0 %collective-permute-start.4 = (f32[40,128]{1,0:T(8,128)S(1)}, f32[40,128]{1,0:T(8,128)S(1)}, u32[]{:S(2)}, u32[]{:S(2)}) collective-permute-start(f32[40,128]{1,0:T(8,128)S(1)} %shard_map.42.refs_0_), channel_id=1, source_target_pairs={{0,96},{16,112},{32,0},{48,16},{64,32},{80,48},{96,64},{112,80},{1... | collective-permute-start | bytes 61448 | tf_op jit(solution)/shard_map/ppermute | solution.py:45
  12.1 4.3 %collective-permute-done.4.refs_2_ = f32[40,128]{1,0:T(8,128)S(1)} collective-permute-done((f32[40,128]{1,0:T(8,128)S(1)}, f32[40,128]{1,0:T(8,128)S(1)}, u32[]{:S(2)}, u32[]{:S(2)}) %collective-permute-start.4) | collective-permute-done | bytes 20512 | tf_op jit(solution)/shard_map/ppermute | solution.py:45
  16.4 1.5 %collective-permute-start.9 = (bf16[2,128,1024]{2,1,0:T(8,128)(2,1)S(1)}, bf16[2,128,1024]{2,1,0:T(8,128)(2,1)S(1)}, u32[]{:S(2)}, u32[]{:S(2)}) collective-permute-start(bf16[2,128,1024]{2,1,0:T(8,128)(2,1)S(1)} %pad_maximum_fusion.views.refs_3_), channel_id=1, source_target_pairs={{0,16},{16,0},{32,48},{48,32},{64,80},{80,64},{96,112},{112,96},{1... | collective-permute-start | bytes 1572872 | tf_op jit(solution)/shard_map/ppermute | solution.py:45
  17.9 1.5 %collective-permute-done.3.refs_1_ = f32[40,128]{1,0:T(8,128)S(1)} collective-permute-done((f32[40,128]{1,0:T(8,128)S(1)}, f32[40,128]{1,0:T(8,128)S(1)}, u32[]{:S(2)}, u32[]{:S(2)}) %collective-permute-start.3) | collective-permute-done | bytes 20512 | tf_op jit(solution)/shard_map/ppermute | solution.py:45
  19.5 0.7 collective-permute-start.10
  20.2 2.2 %collective-permute-start.7 = (bf16[128,1024]{1,0:T(8,128)(2,1)S(1)}, bf16[128,1024]{1,0:T(8,128)(2,1)S(1)}, u32[]{:S(2)}, u32[]{:S(2)}) collective-permute-start(bf16[128,1024]{1,0:T(8,128)(2,1)S(1)} %slice_bitcast_fusion.1), channel_id=1, source_target_pairs={{0,96},{16,112},{32,0},{48,16},{64,32},{80,48},{96,64},{112,80},{1... | collective-permute-start | bytes 786440 | tf_op jit(solution)/shard_map/ppermute | solution.py:45
  22.4 0.9 collective-permute-done.6.refs_3_
  23.3 1.3 %collective-permute-start.8 = (f32[40,128]{1,0:T(8,128)S(1)}, f32[40,128]{1,0:T(8,128)S(1)}, u32[]{:S(2)}, u32[]{:S(2)}) collective-permute-start(f32[40,128]{1,0:T(8,128)S(1)} %shard_map.43.refs_0_), channel_id=1, source_target_pairs={{0,128},{16,144},{32,160},{48,176},{64,192},{80,208},{96,224},{112... | collective-permute-start | bytes 61448 | tf_op jit(solution)/shard_map/ppermute | solution.py:45
  24.7 0.8 collective-permute-start.12
  25.5 0.9 collective-permute-done.8.refs_1_
  26.4 1.8 %collective-permute-done.7.b.opp_b = bf16[128,1024]{1,0:T(8,128)(2,1)S(1)} collective-permute-done((bf16[128,1024]{1,0:T(8,128)(2,1)S(1)}, bf16[128,1024]{1,0:T(8,128)(2,1)S(1)}, u32[]{:S(2)}, u32[]{:S(2)}) %collective-permute-start.7) | collective-permute-done | bytes 262176 | tf_op jit(solution)/shard_map/ppermute | solution.py:45
  28.2 1.5 %collective-permute-start.13 = (bf16[2,128,1024]{2,1,0:T(8,128)(2,1)S(1)}, bf16[2,128,1024]{2,1,0:T(8,128)(2,1)S(1)}, u32[]{:S(2)}, u32[]{:S(2)}) collective-permute-start(bf16[2,128,1024]{2,1,0:T(8,128)(2,1)S(1)} %shard_map.46), channel_id=1, source_target_pairs={{0,128},{16,144},{32,160},{48,176},{64,192},{80,208},{96,224},{112... | collective-permute-start | bytes 1572872 | tf_op jit(solution)/shard_map/ppermute | solution.py:45
  29.7 1.4 %shard_map.45 = (f32[5,1024]{1,0:T(8,128)S(1)}, bf16[2,256,1024]{2,1,0:T(8,128)(2,1)S(1)}, bf16[2,512,1024]{2,1,0:T(8,128)(2,1)S(1)}, bf16[2,256,512]{2,1,0:T(8,128)(2,1)S(1)}) custom-call(f32[40,128]{1,0:T(8,128)S(1)} %shard_map.43.refs_0_, f32[40,128]{1,0:T(8,128)S(1)} %collective-permute-done.8.refs_1_, ...), custom_call_target="tpu_custom_call" | custom-call | flops 536870912 | bytes 6352896 | tf_op jit(solution)/shard_map/pallas_call | solution.py:52
  31.1 7.1 %collective-permute-done.12.x_up = bf16[2,128,1024]{2,1,0:T(8,128)(2,1)S(1)} collective-permute-done((bf16[2,128,1024]{2,1,0:T(8,128)(2,1)S(1)}, bf16[2,128,1024]{2,1,0:T(8,128)(2,1)S(1)}, u32[]{:S(2)}, u32[]{:S(2)}) %collective-permute-start.12) | collective-permute-done | bytes 524320 | tf_op jit(solution)/shard_map/ppermute | solution.py:45
  38.2 0.5 collective-permute-done.13.x_far
  38.7 1.3 %shard_map.47 = (bf16[2,512,1024]{2,1,0:T(8,128)(2,1)S(1)}, bf16[2,2,16,1024]{3,2,1,0:T(8,128)(2,1)S(1)}, bf16[2,2,16,1024]{3,2,1,0:T(8,128)(2,1)S(1)}, bf16[2,2...) custom-call(bf16[2,256,1024]{2,1,0:T(8,128)(2,1)S(1)} %get-tuple-ele, ...), custom_call_target="tpu_custom_call" | custom-call | flops 536870912 | bytes 6836224 | tf_op jit(solution)/shard_map/pallas_call | solution.py:52
  40.1 1.7 %collective-permute-start.14 = (bf16[2,2,2,16,1024]{4,3,2,1,0:T(8,128)(2,1)S(1)}, bf16[2,2,2,16,1024]{4,3,2,1,0:T(8,128)(2,1)S(1)}, u32[]{:S(2)}, u32[]{:S(2)}) collective-permute-start(bf16[2,2,2,16,1024]{4,3,2,1,0:T(8,128)(2,1)S(1)} %get-tuple-element.39), channel_id=1, source_target_pairs={{0,1},{1,2},{2,3},{3,4},{4,5},{5,6},{6,7},{7,0},{8,9},{9,10},{10,1... | collective-permute-start | bytes 786440 | tf_op jit(solution)/shard_map/ppermute | solution.py:45
  41.8 4.0 %collective-permute-start.15 = (bf16[2,2,2,16,1024]{4,3,2,1,0:T(8,128)(2,1)S(1)}, bf16[2,2,2,16,1024]{4,3,2,1,0:T(8,128)(2,1)S(1)}, u32[]{:S(2)}, u32[]{:S(2)}) collective-permute-start(bf16[2,2,2,16,1024]{4,3,2,1,0:T(8,128)(2,1)S(1)} %get-tuple-element.40), channel_id=1, source_target_pairs={{0,7},{1,0},{2,1},{3,2},{4,3},{5,4},{6,5},{7,6},{8,15},{9,8},{10,9... | collective-permute-start | bytes 786440 | tf_op jit(solution)/shard_map/ppermute | solution.py:45
  45.8 3.6 %collective-permute-start.17 = (bf16[2,16,1024]{2,1,0:T(8,128)(2,1)S(1)}, bf16[2,16,1024]{2,1,0:T(8,128)(2,1)S(1)}, u32[]{:S(2)}, u32[]{:S(2)}) collective-permute-start(bf16[2,16,1024]{2,1,0:T(8,128)(2,1)S(1)} %get-tuple-element.42), channel_id=1, source_target_pairs={{0,6},{1,7},{2,0},{3,1},{4,2},{5,3},{6,4},{7,5},{8,14},{9,15},{10,... | collective-permute-start | bytes 196616 | tf_op jit(solution)/shard_map/ppermute | solution.py:45
  49.4 2.5 %collective-permute-done.16.half_a = bf16[2,16,1024]{2,1,0:T(8,128)(2,1)S(1)} collective-permute-done((bf16[2,16,1024]{2,1,0:T(8,128)(2,1)S(1)}, bf16[2,16,1024]{2,1,0:T(8,128)(2,1)S(1)}, u32[]{:S(2)}, u32[]{:S(2)}) %collective-permute-start.16) | collective-permute-done | bytes 65568 | tf_op jit(solution)/shard_map/ppermute | solution.py:45
  51.9 1.4 %collective-permute-done.17.half_b = bf16[2,16,1024]{2,1,0:T(8,128)(2,1)S(1)} collective-permute-done((bf16[2,16,1024]{2,1,0:T(8,128)(2,1)S(1)}, bf16[2,16,1024]{2,1,0:T(8,128)(2,1)S(1)}, u32[]{:S(2)}, u32[]{:S(2)}) %collective-permute-start.17) | collective-permute-done | bytes 65568 | tf_op jit(solution)/shard_map/ppermute | solution.py:45
  53.4 2.3 %collective-permute-start.18 = (bf16[2,2,16,1024]{3,2,1,0:T(8,128)(2,1)S(1)}, bf16[2,2,16,1024]{3,2,1,0:T(8,128)(2,1)S(1)}, u32[]{:S(2)}, u32[]{:S(2)}) collective-permute-start(bf16[2,2,16,1024]{3,2,1,0:T(8,128)(2,1)S(1)} %get-tuple-element.45), channel_id=1, source_target_pairs={{0,2},{1,3},{2,4},{3,5},{4,6},{5,7},{6,0},{7,1},{8,10},{9,11},{10,... | collective-permute-start | bytes 393224 | tf_op jit(solution)/shard_map/ppermute | solution.py:45
  55.7 1.3 %collective-permute-start.19 = (bf16[2,2,16,1024]{3,2,1,0:T(8,128)(2,1)S(1)}, bf16[2,2,16,1024]{3,2,1,0:T(8,128)(2,1)S(1)}, u32[]{:S(2)}, u32[]{:S(2)}) collective-permute-start(bf16[2,2,16,1024]{3,2,1,0:T(8,128)(2,1)S(1)} %get-tuple-element.46), channel_id=1, source_target_pairs={{0,6},{1,7},{2,0},{3,1},{4,2},{5,3},{6,4},{7,5},{8,14},{9,15},{10,... | collective-permute-start | bytes 393224 | tf_op jit(solution)/shard_map/ppermute | solution.py:45
  57.0 3.0 %collective-permute-done.18.far_up = bf16[2,2,16,1024]{3,2,1,0:T(8,128)(2,1)S(1)} collective-permute-done((bf16[2,2,16,1024]{3,2,1,0:T(8,128)(2,1)S(1)}, bf16[2,2,16,1024]{3,2,1,0:T(8,128)(2,1)S(1)}, u32[]{:S(2)}, u32[]{:S(2)}) %collective-permute-start.18) | collective-permute-done | bytes 131104 | tf_op jit(solution)/shard_map/ppermute | solution.py:45
  60.0 1.0 collective-permute-done.19.far_down
  61.0 0.1 shard_map.49.a
  61.1 2.7 %collective-permute-start.20 = (bf16[2,2,16,1024]{3,2,1,0:T(8,128)(2,1)S(1)}, bf16[2,2,16,1024]{3,2,1,0:T(8,128)(2,1)S(1)}, u32[]{:S(2)}, u32[]{:S(2)}) collective-permute-start(bf16[2,2,16,1024]{3,2,1,0:T(8,128)(2,1)S(1)} %shard_map.49.a), channel_id=1, source_target_pairs={{0,8},{1,9},{2,10},{3,11},{4,12},{5,13},{6,14},{7,15},{8,0},{9,1},... | collective-permute-start | bytes 393224 | tf_op jit(solution)/shard_map/ppermute | solution.py:45
  63.8 2.7 %collective-permute-done.20.b = bf16[2,2,16,1024]{3,2,1,0:T(8,128)(2,1)S(1)} collective-permute-done((bf16[2,2,16,1024]{3,2,1,0:T(8,128)(2,1)S(1)}, bf16[2,2,16,1024]{3,2,1,0:T(8,128)(2,1)S(1)}, u32[]{:S(2)}, u32[]{:S(2)}) %collective-permute-start.20) | collective-permute-done | bytes 131104 | tf_op jit(solution)/shard_map/ppermute | solution.py:45
  66.6 2.6 %collective-permute-start.24 = (bf16[2,2,16,1024]{3,2,1,0:T(8,128)(2,1)S(1)}, bf16[2,2,16,1024]{3,2,1,0:T(8,128)(2,1)S(1)}, u32[]{:S(2)}, u32[]{:S(2)}) collective-permute-start(bf16[2,2,16,1024]{3,2,1,0:T(8,128)(2,1)S(1)} %shard_map.50.refs_0_), channel_id=1, source_target_pairs={{0,6},{1,7},{2,0},{3,1},{4,2},{5,3},{6,4},{7,5},{8,14},{9,15},{10,... | collective-permute-start | bytes 393224 | tf_op jit(solution)/shard_map/ppermute | solution.py:45
  69.2 0.3 collective-permute-start.22
  69.6 1.4 %collective-permute-start.21 = (bf16[2,2,16,1024]{3,2,1,0:T(8,128)(2,1)S(1)}, bf16[2,2,16,1024]{3,2,1,0:T(8,128)(2,1)S(1)}, u32[]{:S(2)}, u32[]{:S(2)}) collective-permute-start(bf16[2,2,16,1024]{3,2,1,0:T(8,128)(2,1)S(1)} %shard_map.50.refs_0_), channel_id=1, source_target_pairs={{0,1},{1,2},{2,3},{3,4},{4,5},{5,6},{6,7},{7,0},{8,9},{9,10},{10,1... | collective-permute-start | bytes 393224 | tf_op jit(solution)/shard_map/ppermute | solution.py:45
  70.9 2.3 %collective-permute-done.24.refs_5_ = bf16[2,2,16,1024]{3,2,1,0:T(8,128)(2,1)S(1)} collective-permute-done((bf16[2,2,16,1024]{3,2,1,0:T(8,128)(2,1)S(1)}, bf16[2,2,16,1024]{3,2,1,0:T(8,128)(2,1)S(1)}, u32[]{:S(2)}, u32[]{:S(2)}) %collective-permute-start.24) | collective-permute-done | bytes 131104 | tf_op jit(solution)/shard_map/ppermute | solution.py:45
  73.2 2.3 %collective-permute-start.28 = (bf16[2,16,1024]{2,1,0:T(8,128)(2,1)S(1)}, bf16[2,16,1024]{2,1,0:T(8,128)(2,1)S(1)}, u32[]{:S(2)}, u32[]{:S(2)}) collective-permute-start(bf16[2,16,1024]{2,1,0:T(8,128)(2,1)S(1)} %slice_bitcast_fusion.2), channel_id=1, source_target_pairs={{0,6},{1,7},{2,0},{3,1},{4,2},{5,3},{6,4},{7,5},{8,14},{9,15},{10,... | collective-permute-start | bytes 196616 | tf_op jit(solution)/shard_map/ppermute | solution.py:45
  75.5 0.5 collective-permute-done.22.refs_2_
  76.0 1.8 %collective-permute-start.23 = (bf16[2,2,16,1024]{3,2,1,0:T(8,128)(2,1)S(1)}, bf16[2,2,16,1024]{3,2,1,0:T(8,128)(2,1)S(1)}, u32[]{:S(2)}, u32[]{:S(2)}) collective-permute-start(bf16[2,2,16,1024]{3,2,1,0:T(8,128)(2,1)S(1)} %collective-permute-done.22.refs_2_), channel_id=1, source_target_pairs={{0,1},{1,2},{2,3},{3,4},{4,5},{5,6},{6,7},{7,0},{8,9},{9,10},{10,1... | collective-permute-start | bytes 393224 | tf_op jit(solution)/shard_map/ppermute | solution.py:45
  77.8 1.1 collective-permute-start.27
  78.8 1.6 %collective-permute-done.28.refs_8_ = bf16[2,16,1024]{2,1,0:T(8,128)(2,1)S(1)} collective-permute-done((bf16[2,16,1024]{2,1,0:T(8,128)(2,1)S(1)}, bf16[2,16,1024]{2,1,0:T(8,128)(2,1)S(1)}, u32[]{:S(2)}, u32[]{:S(2)}) %collective-permute-start.28) | collective-permute-done | bytes 65568 | tf_op jit(solution)/shard_map/ppermute | solution.py:45
  80.4 4.9 %collective-permute-done.27.refs_7_ = bf16[2,16,1024]{2,1,0:T(8,128)(2,1)S(1)} collective-permute-done((bf16[2,16,1024]{2,1,0:T(8,128)(2,1)S(1)}, bf16[2,16,1024]{2,1,0:T(8,128)(2,1)S(1)}, u32[]{:S(2)}, u32[]{:S(2)}) %collective-permute-start.27) | collective-permute-done | bytes 65568 | tf_op jit(solution)/shard_map/ppermute | solution.py:45
  85.2 1.6 %shard_map.51 = (f32[2,128,1024]{2,1,0:T(8,128)S(1)}, f32[2,128,1024]{2,1,0:T(8,128)S(1)}, f32[16,4,1024]{2,1,0:T(4,128)S(1)}) custom-call(bf16[2,2,16,1024]{3,2,1,0:T(8,128)(2,1)S(1)} %shard_map.50.refs_0_, bf16[2,2,16,1024]{3,2,1,0:T(8,128)(2,1)S(1)} %collective-permute-done.21.refs_1_, bf16[2,2,16,1024]{3,2,1,0:T(8,128)(2,1)S(1)} %collective-permute-done.22.refs_2_, ...), custom_call_target="tpu_custom_call" | custom-call | flops 1073741824 | bytes 8671232 | tf_op jit(solution)/shard_map/pallas_call | solution.py:52
  86.9 9.3 %collective-permute-start.29 = (f32[2,128,1024]{2,1,0:T(8,128)S(1)}, f32[2,128,1024]{2,1,0:T(8,128)S(1)}, u32[]{:S(2)}, u32[]{:S(2)}) collective-permute-start(f32[2,128,1024]{2,1,0:T(8,128)S(1)} %get-tuple-element.50), channel_id=1, source_target_pairs={{0,16},{16,0},{32,48},{48,32},{64,80},{80,64},{96,112},{112,96},{1... | collective-permute-start | bytes 3145736 | tf_op jit(solution)/shard_map/ppermute | solution.py:45
  96.2 11.6 %all_to_all.5.sums = f32[16,4,1024]{2,1,0:T(4,128)S(1)} all-to-all(f32[16,4,1024]{2,1,0:T(4,128)S(1)} %get-tuple-element.51), channel_id=1, replica_groups=mesh['dp'=16,'feat'=16] {'dp'}, dimensions={0} | all-to-all | bytes 524288 | tf_op jit(solution)/shard_map/all_to_all | solution.py:354
  107.8 1.0 shard_map.52
  (30 shorter events, 0.3 us)
Async XLA Ops:
  1.7 17.8 %collective-permute-start.2 = (bf16[2,128,1024]{2,1,0:T(8,128)(2,1)S(1)}, bf16[2,128,1024]{2,1,0:T(8,128)(2,1)S(1)}, u32[]{:S(2)}, u32[]{:S(2)}) collective-permute-start(bf16[2,128,1024]{2,1,0:T(8,128)(2,1)S(1)} %pad_maximum_fusion.views.refs_3_), channel_id=1, source_target_pairs={{0,96},{16,112},{32,0},{48,16},{64,32},{80,48},{96,64},{112,80},{1... | collective-permute-start | bytes 1572872 | tf_op jit(solution)/shard_map/ppermute | solution.py:45
  5.4 14.1 %collective-permute-start.1 = (bf16[2,128,1024]{2,1,0:T(8,128)(2,1)S(1)}, bf16[2,128,1024]{2,1,0:T(8,128)(2,1)S(1)}, u32[]{:S(2)}, u32[]{:S(2)}) collective-permute-start(bf16[2,128,1024]{2,1,0:T(8,128)(2,1)S(1)} %pad_maximum_fusion.views.refs_3_), channel_id=1, source_target_pairs={{0,32},{16,48},{32,64},{48,80},{64,96},{80,112},{96,0},{112,16},{1... | collective-permute-start | bytes 1572872 | tf_op jit(solution)/shard_map/ppermute | solution.py:45
  5.4 17.0 %collective-permute-start.5 = (bf16[2,128,1024]{2,1,0:T(8,128)(2,1)S(1)}, bf16[2,128,1024]{2,1,0:T(8,128)(2,1)S(1)}, u32[]{:S(2)}, u32[]{:S(2)}) collective-permute-start(bf16[2,128,1024]{2,1,0:T(8,128)(2,1)S(1)} %pad_maximum_fusion.views.refs_3_), channel_id=1, source_target_pairs={{0,128},{16,144},{32,160},{48,176},{64,192},{80,208},{96,224},{112... | collective-permute-start | bytes 1572872 | tf_op jit(solution)/shard_map/ppermute | solution.py:45
  6.9 2.2 %collective-permute-start = (f32[40,128]{1,0:T(8,128)S(1)}, f32[40,128]{1,0:T(8,128)S(1)}, u32[]{:S(2)}, u32[]{:S(2)}) collective-permute-start(f32[40,128]{1,0:T(8,128)S(1)} %shard_map.41.refs_0_), channel_id=1, source_target_pairs={{0,16},{16,0},{32,48},{48,32},{64,80},{80,64},{96,112},{112,96},{1... | collective-permute-start | bytes 61448 | tf_op jit(solution)/shard_map/ppermute | solution.py:45
  9.1 7.3 %collective-permute-start.4 = (f32[40,128]{1,0:T(8,128)S(1)}, f32[40,128]{1,0:T(8,128)S(1)}, u32[]{:S(2)}, u32[]{:S(2)}) collective-permute-start(f32[40,128]{1,0:T(8,128)S(1)} %shard_map.42.refs_0_), channel_id=1, source_target_pairs={{0,96},{16,112},{32,0},{48,16},{64,32},{80,48},{96,64},{112,80},{1... | collective-permute-start | bytes 61448 | tf_op jit(solution)/shard_map/ppermute | solution.py:45
  12.1 7.4 %collective-permute-start.3 = (f32[40,128]{1,0:T(8,128)S(1)}, f32[40,128]{1,0:T(8,128)S(1)}, u32[]{:S(2)}, u32[]{:S(2)}) collective-permute-start(f32[40,128]{1,0:T(8,128)S(1)} %shard_map.42.refs_0_), channel_id=1, source_target_pairs={{0,32},{16,48},{32,64},{48,80},{64,96},{80,112},{96,0},{112,16},{1... | collective-permute-start | bytes 61448 | tf_op jit(solution)/shard_map/ppermute | solution.py:45
  16.4 13.3 %collective-permute-start.9 = (bf16[2,128,1024]{2,1,0:T(8,128)(2,1)S(1)}, bf16[2,128,1024]{2,1,0:T(8,128)(2,1)S(1)}, u32[]{:S(2)}, u32[]{:S(2)}) collective-permute-start(bf16[2,128,1024]{2,1,0:T(8,128)(2,1)S(1)} %pad_maximum_fusion.views.refs_3_), channel_id=1, source_target_pairs={{0,16},{16,0},{32,48},{48,32},{64,80},{80,64},{96,112},{112,96},{1... | collective-permute-start | bytes 1572872 | tf_op jit(solution)/shard_map/ppermute | solution.py:45
  19.5 3.8 %collective-permute-start.6 = (f32[40,128]{1,0:T(8,128)S(1)}, f32[40,128]{1,0:T(8,128)S(1)}, u32[]{:S(2)}, u32[]{:S(2)}) collective-permute-start(f32[40,128]{1,0:T(8,128)S(1)} %collective-permute-done.3.refs_1_), channel_id=1, source_target_pairs={{0,32},{16,48},{32,64},{48,80},{64,96},{80,112},{96,0},{112,16},{1... | collective-permute-start | bytes 61448 | tf_op jit(solution)/shard_map/ppermute | solution.py:45
  19.5 8.6 %collective-permute-start.10 = (bf16[128,1024]{1,0:T(8,128)(2,1)S(1)}, bf16[128,1024]{1,0:T(8,128)(2,1)S(1)}, u32[]{:S(2)}, u32[]{:S(2)}) collective-permute-start(bf16[128,1024]{1,0:T(8,128)(2,1)S(1)} %slice_bitcast_fusion), channel_id=1, source_target_pairs={{0,32},{16,48},{32,64},{48,80},{64,96},{80,112},{96,0},{112,16},{1... | collective-permute-start | bytes 786440 | tf_op jit(solution)/shard_map/ppermute | solution.py:45
  20.2 8.0 %collective-permute-start.7 = (bf16[128,1024]{1,0:T(8,128)(2,1)S(1)}, bf16[128,1024]{1,0:T(8,128)(2,1)S(1)}, u32[]{:S(2)}, u32[]{:S(2)}) collective-permute-start(bf16[128,1024]{1,0:T(8,128)(2,1)S(1)} %slice_bitcast_fusion.1), channel_id=1, source_target_pairs={{0,96},{16,112},{32,0},{48,16},{64,32},{80,48},{96,64},{112,80},{1... | collective-permute-start | bytes 786440 | tf_op jit(solution)/shard_map/ppermute | solution.py:45
  23.3 3.0 %collective-permute-start.8 = (f32[40,128]{1,0:T(8,128)S(1)}, f32[40,128]{1,0:T(8,128)S(1)}, u32[]{:S(2)}, u32[]{:S(2)}) collective-permute-start(f32[40,128]{1,0:T(8,128)S(1)} %shard_map.43.refs_0_), channel_id=1, source_target_pairs={{0,128},{16,144},{32,160},{48,176},{64,192},{80,208},{96,224},{112... | collective-permute-start | bytes 61448 | tf_op jit(solution)/shard_map/ppermute | solution.py:45
  24.7 13.5 %collective-permute-start.12 = (bf16[2,128,1024]{2,1,0:T(8,128)(2,1)S(1)}, bf16[2,128,1024]{2,1,0:T(8,128)(2,1)S(1)}, u32[]{:S(2)}, u32[]{:S(2)}) collective-permute-start(bf16[2,128,1024]{2,1,0:T(8,128)(2,1)S(1)} %shard_map.44.refs_6_), channel_id=1, source_target_pairs={{0,96},{16,112},{32,0},{48,16},{64,32},{80,48},{96,64},{112,80},{1... | collective-permute-start | bytes 1572872 | tf_op jit(solution)/shard_map/ppermute | solution.py:45
  26.4 11.9 %collective-permute-start.11 = (bf16[2,128,1024]{2,1,0:T(8,128)(2,1)S(1)}, bf16[2,128,1024]{2,1,0:T(8,128)(2,1)S(1)}, u32[]{:S(2)}, u32[]{:S(2)}) collective-permute-start(bf16[2,128,1024]{2,1,0:T(8,128)(2,1)S(1)} %shard_map.44.refs_6_), channel_id=1, source_target_pairs={{0,32},{16,48},{32,64},{48,80},{64,96},{80,112},{96,0},{112,16},{1... | collective-permute-start | bytes 1572872 | tf_op jit(solution)/shard_map/ppermute | solution.py:45
  28.2 10.5 %collective-permute-start.13 = (bf16[2,128,1024]{2,1,0:T(8,128)(2,1)S(1)}, bf16[2,128,1024]{2,1,0:T(8,128)(2,1)S(1)}, u32[]{:S(2)}, u32[]{:S(2)}) collective-permute-start(bf16[2,128,1024]{2,1,0:T(8,128)(2,1)S(1)} %shard_map.46), channel_id=1, source_target_pairs={{0,128},{16,144},{32,160},{48,176},{64,192},{80,208},{96,224},{112... | collective-permute-start | bytes 1572872 | tf_op jit(solution)/shard_map/ppermute | solution.py:45
  40.1 13.2 %collective-permute-start.14 = (bf16[2,2,2,16,1024]{4,3,2,1,0:T(8,128)(2,1)S(1)}, bf16[2,2,2,16,1024]{4,3,2,1,0:T(8,128)(2,1)S(1)}, u32[]{:S(2)}, u32[]{:S(2)}) collective-permute-start(bf16[2,2,2,16,1024]{4,3,2,1,0:T(8,128)(2,1)S(1)} %get-tuple-element.39), channel_id=1, source_target_pairs={{0,1},{1,2},{2,3},{3,4},{4,5},{5,6},{6,7},{7,0},{8,9},{9,10},{10,1... | collective-permute-start | bytes 786440 | tf_op jit(solution)/shard_map/ppermute | solution.py:45
  41.8 11.5 %collective-permute-start.15 = (bf16[2,2,2,16,1024]{4,3,2,1,0:T(8,128)(2,1)S(1)}, bf16[2,2,2,16,1024]{4,3,2,1,0:T(8,128)(2,1)S(1)}, u32[]{:S(2)}, u32[]{:S(2)}) collective-permute-start(bf16[2,2,2,16,1024]{4,3,2,1,0:T(8,128)(2,1)S(1)} %get-tuple-element.40), channel_id=1, source_target_pairs={{0,7},{1,0},{2,1},{3,2},{4,3},{5,4},{6,5},{7,6},{8,15},{9,8},{10,9... | collective-permute-start | bytes 786440 | tf_op jit(solution)/shard_map/ppermute | solution.py:45
  45.8 6.1 %collective-permute-start.16 = (bf16[2,16,1024]{2,1,0:T(8,128)(2,1)S(1)}, bf16[2,16,1024]{2,1,0:T(8,128)(2,1)S(1)}, u32[]{:S(2)}, u32[]{:S(2)}) collective-permute-start(bf16[2,16,1024]{2,1,0:T(8,128)(2,1)S(1)} %get-tuple-element.41), channel_id=1, source_target_pairs={{0,2},{1,3},{2,4},{3,5},{4,6},{5,7},{6,0},{7,1},{8,10},{9,11},{10,... | collective-permute-start | bytes 196616 | tf_op jit(solution)/shard_map/ppermute | solution.py:45
  45.8 7.5 %collective-permute-start.17 = (bf16[2,16,1024]{2,1,0:T(8,128)(2,1)S(1)}, bf16[2,16,1024]{2,1,0:T(8,128)(2,1)S(1)}, u32[]{:S(2)}, u32[]{:S(2)}) collective-permute-start(bf16[2,16,1024]{2,1,0:T(8,128)(2,1)S(1)} %get-tuple-element.42), channel_id=1, source_target_pairs={{0,6},{1,7},{2,0},{3,1},{4,2},{5,3},{6,4},{7,5},{8,14},{9,15},{10,... | collective-permute-start | bytes 196616 | tf_op jit(solution)/shard_map/ppermute | solution.py:45
  53.4 6.6 %collective-permute-start.18 = (bf16[2,2,16,1024]{3,2,1,0:T(8,128)(2,1)S(1)}, bf16[2,2,16,1024]{3,2,1,0:T(8,128)(2,1)S(1)}, u32[]{:S(2)}, u32[]{:S(2)}) collective-permute-start(bf16[2,2,16,1024]{3,2,1,0:T(8,128)(2,1)S(1)} %get-tuple-element.45), channel_id=1, source_target_pairs={{0,2},{1,3},{2,4},{3,5},{4,6},{5,7},{6,0},{7,1},{8,10},{9,11},{10,... | collective-permute-start | bytes 393224 | tf_op jit(solution)/shard_map/ppermute | solution.py:45
  55.7 5.3 %collective-permute-start.19 = (bf16[2,2,16,1024]{3,2,1,0:T(8,128)(2,1)S(1)}, bf16[2,2,16,1024]{3,2,1,0:T(8,128)(2,1)S(1)}, u32[]{:S(2)}, u32[]{:S(2)}) collective-permute-start(bf16[2,2,16,1024]{3,2,1,0:T(8,128)(2,1)S(1)} %get-tuple-element.46), channel_id=1, source_target_pairs={{0,6},{1,7},{2,0},{3,1},{4,2},{5,3},{6,4},{7,5},{8,14},{9,15},{10,... | collective-permute-start | bytes 393224 | tf_op jit(solution)/shard_map/ppermute | solution.py:45
  61.1 5.4 %collective-permute-start.20 = (bf16[2,2,16,1024]{3,2,1,0:T(8,128)(2,1)S(1)}, bf16[2,2,16,1024]{3,2,1,0:T(8,128)(2,1)S(1)}, u32[]{:S(2)}, u32[]{:S(2)}) collective-permute-start(bf16[2,2,16,1024]{3,2,1,0:T(8,128)(2,1)S(1)} %shard_map.49.a), channel_id=1, source_target_pairs={{0,8},{1,9},{2,10},{3,11},{4,12},{5,13},{6,14},{7,15},{8,0},{9,1},... | collective-permute-start | bytes 393224 | tf_op jit(solution)/shard_map/ppermute | solution.py:45
  66.6 6.6 %collective-permute-start.24 = (bf16[2,2,16,1024]{3,2,1,0:T(8,128)(2,1)S(1)}, bf16[2,2,16,1024]{3,2,1,0:T(8,128)(2,1)S(1)}, u32[]{:S(2)}, u32[]{:S(2)}) collective-permute-start(bf16[2,2,16,1024]{3,2,1,0:T(8,128)(2,1)S(1)} %shard_map.50.refs_0_), channel_id=1, source_target_pairs={{0,6},{1,7},{2,0},{3,1},{4,2},{5,3},{6,4},{7,5},{8,14},{9,15},{10,... | collective-permute-start | bytes 393224 | tf_op jit(solution)/shard_map/ppermute | solution.py:45
  69.2 8.5 %collective-permute-start.26 = (bf16[2,2,16,1024]{3,2,1,0:T(8,128)(2,1)S(1)}, bf16[2,2,16,1024]{3,2,1,0:T(8,128)(2,1)S(1)}, u32[]{:S(2)}, u32[]{:S(2)}) collective-permute-start(bf16[2,2,16,1024]{3,2,1,0:T(8,128)(2,1)S(1)} %shard_map.50.refs_0_), channel_id=1, source_target_pairs={{0,7},{1,0},{2,1},{3,2},{4,3},{5,4},{6,5},{7,6},{8,15},{9,8},{10,9... | collective-permute-start | bytes 393224 | tf_op jit(solution)/shard_map/ppermute | solution.py:45
  69.2 6.8 %collective-permute-start.22 = (bf16[2,2,16,1024]{3,2,1,0:T(8,128)(2,1)S(1)}, bf16[2,2,16,1024]{3,2,1,0:T(8,128)(2,1)S(1)}, u32[]{:S(2)}, u32[]{:S(2)}) collective-permute-start(bf16[2,2,16,1024]{3,2,1,0:T(8,128)(2,1)S(1)} %shard_map.50.refs_0_), channel_id=1, source_target_pairs={{0,2},{1,3},{2,4},{3,5},{4,6},{5,7},{6,0},{7,1},{8,10},{9,11},{10,... | collective-permute-start | bytes 393224 | tf_op jit(solution)/shard_map/ppermute | solution.py:45
  69.6 9.3 %collective-permute-start.21 = (bf16[2,2,16,1024]{3,2,1,0:T(8,128)(2,1)S(1)}, bf16[2,2,16,1024]{3,2,1,0:T(8,128)(2,1)S(1)}, u32[]{:S(2)}, u32[]{:S(2)}) collective-permute-start(bf16[2,2,16,1024]{3,2,1,0:T(8,128)(2,1)S(1)} %shard_map.50.refs_0_), channel_id=1, source_target_pairs={{0,1},{1,2},{2,3},{3,4},{4,5},{5,6},{6,7},{7,0},{8,9},{9,10},{10,1... | collective-permute-start | bytes 393224 | tf_op jit(solution)/shard_map/ppermute | solution.py:45
  73.2 7.2 %collective-permute-start.28 = (bf16[2,16,1024]{2,1,0:T(8,128)(2,1)S(1)}, bf16[2,16,1024]{2,1,0:T(8,128)(2,1)S(1)}, u32[]{:S(2)}, u32[]{:S(2)}) collective-permute-start(bf16[2,16,1024]{2,1,0:T(8,128)(2,1)S(1)} %slice_bitcast_fusion.2), channel_id=1, source_target_pairs={{0,6},{1,7},{2,0},{3,1},{4,2},{5,3},{6,4},{7,5},{8,14},{9,15},{10,... | collective-permute-start | bytes 196616 | tf_op jit(solution)/shard_map/ppermute | solution.py:45
  75.5 9.8 %collective-permute-start.25 = (bf16[2,2,16,1024]{3,2,1,0:T(8,128)(2,1)S(1)}, bf16[2,2,16,1024]{3,2,1,0:T(8,128)(2,1)S(1)}, u32[]{:S(2)}, u32[]{:S(2)}) collective-permute-start(bf16[2,2,16,1024]{3,2,1,0:T(8,128)(2,1)S(1)} %collective-permute-done.24.refs_5_), channel_id=1, source_target_pairs={{0,7},{1,0},{2,1},{3,2},{4,3},{5,4},{6,5},{7,6},{8,15},{9,8},{10,9... | collective-permute-start | bytes 393224 | tf_op jit(solution)/shard_map/ppermute | solution.py:45
  76.0 9.3 %collective-permute-start.23 = (bf16[2,2,16,1024]{3,2,1,0:T(8,128)(2,1)S(1)}, bf16[2,2,16,1024]{3,2,1,0:T(8,128)(2,1)S(1)}, u32[]{:S(2)}, u32[]{:S(2)}) collective-permute-start(bf16[2,2,16,1024]{3,2,1,0:T(8,128)(2,1)S(1)} %collective-permute-done.22.refs_2_), channel_id=1, source_target_pairs={{0,1},{1,2},{2,3},{3,4},{4,5},{5,6},{6,7},{7,0},{8,9},{9,10},{10,1... | collective-permute-start | bytes 393224 | tf_op jit(solution)/shard_map/ppermute | solution.py:45
  77.8 7.5 %collective-permute-start.27 = (bf16[2,16,1024]{2,1,0:T(8,128)(2,1)S(1)}, bf16[2,16,1024]{2,1,0:T(8,128)(2,1)S(1)}, u32[]{:S(2)}, u32[]{:S(2)}) collective-permute-start(bf16[2,16,1024]{2,1,0:T(8,128)(2,1)S(1)} %slice_bitcast_fusion.3), channel_id=1, source_target_pairs={{0,2},{1,3},{2,4},{3,5},{4,6},{5,7},{6,0},{7,1},{8,10},{9,11},{10,... | collective-permute-start | bytes 196616 | tf_op jit(solution)/shard_map/ppermute | solution.py:45
  86.9 20.9 %collective-permute-start.29 = (f32[2,128,1024]{2,1,0:T(8,128)S(1)}, f32[2,128,1024]{2,1,0:T(8,128)S(1)}, u32[]{:S(2)}, u32[]{:S(2)}) collective-permute-start(f32[2,128,1024]{2,1,0:T(8,128)S(1)} %get-tuple-element.50), channel_id=1, source_target_pairs={{0,16},{16,0},{32,48},{48,32},{64,80},{80,64},{96,112},{112,96},{1... | collective-permute-start | bytes 3145736 | tf_op jit(solution)/shard_map/ppermute | solution.py:45

commit v8 on v7

--- a/solution.py
+++ b/solution.py
@@ -218,13 +218,12 @@
     from_6 = send(block, z_shift(-2), z)
     from_3 = send(from_2, z_shift(1), z)
     from_5 = send(from_6, z_shift(-1), z)
-    from_4a = send(from_2[0], z_shift(2), z)
-    from_4b = send(from_6[1], z_shift(-2), z)
-    return [block, from_1, from_2, from_3, from_5, from_6, from_7, from_4a, from_4b]
+    from_4 = send(from_2, z_shift(2), z)
+    return [block, from_1, from_2, from_3, from_4, from_5, from_6, from_7]
 
 
 def apply_body(scale, *refs):
-    *blocks, from_4a, from_4b, near, last, lead, stats, own, other, sums, gram = refs
+    *blocks, near, last, lead, stats, own, other, sums, gram = refs
     rows, part = own.shape[1], blocks[0].shape[2]
     z = lax.rem(lax.axis_index("feat"), Z)
 
@@ -234,9 +233,8 @@
             gram[v, pl.ds(pl.multiple_of(start + h * rows, part), part), :] = block[h]
 
     for v in range(2):
-        for back, block in zip((0, 1, 2, 3, 5, 6, 7), blocks):
+        for back, block in enumerate(blocks):
             load(back, v, block.at[v])
-        load(4, v, (from_4a, from_4b)[v])
     diag = stats[4:5, :]
     ends = (0, near.shape[1], gram.shape[2])
     for v in range(2):

time: 109 us -> 110 us (level)
  waiting for transfers between devices: 37.8 us -> 39.8 us
    ppermute x30 -> x29, waiting for transfers between devices: 37.8 us -> 39.8 us  [send(): return lax.ppermute(x, axis, to)]
    ppermute x30 -> x29, starting transfers between devices: 51.6 us -> 50.7 us  [send(): return lax.ppermute(x, axis, to)]
  transfers between devices with their start and end apart: 30 -> 29, of which waited for: 17 -> 17; matrix products, arithmetic and copies ran while one was open for 0% -> 0% of each run, Pallas kernels for 2% -> 2%
where the time goes in v8:
time: 110 us
  starting transfers between devices  50.7 us (46%)
  waiting for transfers between devices  39.8 us (36%)
  blocking collectives  11.3 us (10%)
  Pallas kernels  5.9 us (5%)
    ppermute x29, starting transfers between devices, send(): return lax.ppermute(x, axis, to)  50.7 us
    ppermute x29, waiting for transfers between devices, send(): return lax.ppermute(x, axis, to)  39.8 us
    all_to_all x1, blocking collectives, on_device(): sums = lax.all_to_all(sums, 'dp', 0, 0)  11.3 us
    pallas_call x12, Pallas kernels, call(): pl.pallas_call(body, out_shape=outs, in_specs=[pl.BlockSpec(memory_space=...  5.9 us
  transfers between devices with their start and end apart: 29, of which 17 were waited for; matrix products, arithmetic and copies ran while one was open for 0% of the time, Pallas kernels for 2%

profile of v8, /device:TPU:1, one launch (start us, length us, event | category | flops | bytes accessed | tf_op | source)
XLA Modules:
  0.0 109.5 jit_solution(15604456217463897183)
XLA Ops:
  0.6 1.1 pad_maximum_fusion.views.refs_3_
  1.7 3.6 %collective-permute-start.2 = (bf16[2,128,1024]{2,1,0:T(8,128)(2,1)S(1)}, bf16[2,128,1024]{2,1,0:T(8,128)(2,1)S(1)}, u32[]{:S(2)}, u32[]{:S(2)}) collective-permute-start(bf16[2,128,1024]{2,1,0:T(8,128)(2,1)S(1)} %pad_maximum_fusion.views.refs_3_), channel_id=1, source_target_pairs={{0,96},{16,112},{32,0},{48,16},{64,32},{80,48},{96,64},{112,80},{1... | collective-permute-start | bytes 1572872 | tf_op jit(solution)/shard_map/ppermute | solution.py:45
  5.4 1.2 %collective-permute-start.5 = (bf16[2,128,1024]{2,1,0:T(8,128)(2,1)S(1)}, bf16[2,128,1024]{2,1,0:T(8,128)(2,1)S(1)}, u32[]{:S(2)}, u32[]{:S(2)}) collective-permute-start(bf16[2,128,1024]{2,1,0:T(8,128)(2,1)S(1)} %pad_maximum_fusion.views.refs_3_), channel_id=1, source_target_pairs={{0,128},{16,144},{32,160},{48,176},{64,192},{80,208},{96,224},{112... | collective-permute-start | bytes 1572872 | tf_op jit(solution)/shard_map/ppermute | solution.py:45
  6.6 0.3 shard_map.41.refs_0_
  6.9 1.3 %collective-permute-start = (f32[40,128]{1,0:T(8,128)S(1)}, f32[40,128]{1,0:T(8,128)S(1)}, u32[]{:S(2)}, u32[]{:S(2)}) collective-permute-start(f32[40,128]{1,0:T(8,128)S(1)} %shard_map.41.refs_0_), channel_id=1, source_target_pairs={{0,16},{16,0},{32,48},{48,32},{64,80},{80,64},{96,112},{112,96},{1... | collective-permute-start | bytes 61448 | tf_op jit(solution)/shard_map/ppermute | solution.py:45
  8.2 0.8 collective-permute-done.refs_1_
  9.1 3.0 %collective-permute-start.4 = (f32[40,128]{1,0:T(8,128)S(1)}, f32[40,128]{1,0:T(8,128)S(1)}, u32[]{:S(2)}, u32[]{:S(2)}) collective-permute-start(f32[40,128]{1,0:T(8,128)S(1)} %shard_map.42.refs_0_), channel_id=1, source_target_pairs={{0,96},{16,112},{32,0},{48,16},{64,32},{80,48},{96,64},{112,80},{1... | collective-permute-start | bytes 61448 | tf_op jit(solution)/shard_map/ppermute | solution.py:45
  12.1 4.3 %collective-permute-done.4.refs_2_ = f32[40,128]{1,0:T(8,128)S(1)} collective-permute-done((f32[40,128]{1,0:T(8,128)S(1)}, f32[40,128]{1,0:T(8,128)S(1)}, u32[]{:S(2)}, u32[]{:S(2)}) %collective-permute-start.4) | collective-permute-done | bytes 20512 | tf_op jit(solution)/shard_map/ppermute | solution.py:45
  16.4 1.5 %collective-permute-start.9 = (bf16[2,128,1024]{2,1,0:T(8,128)(2,1)S(1)}, bf16[2,128,1024]{2,1,0:T(8,128)(2,1)S(1)}, u32[]{:S(2)}, u32[]{:S(2)}) collective-permute-start(bf16[2,128,1024]{2,1,0:T(8,128)(2,1)S(1)} %pad_maximum_fusion.views.refs_3_), channel_id=1, source_target_pairs={{0,16},{16,0},{32,48},{48,32},{64,80},{80,64},{96,112},{112,96},{1... | collective-permute-start | bytes 1572872 | tf_op jit(solution)/shard_map/ppermute | solution.py:45
  17.9 1.5 %collective-permute-done.3.refs_1_ = f32[40,128]{1,0:T(8,128)S(1)} collective-permute-done((f32[40,128]{1,0:T(8,128)S(1)}, f32[40,128]{1,0:T(8,128)S(1)}, u32[]{:S(2)}, u32[]{:S(2)}) %collective-permute-start.3) | collective-permute-done | bytes 20512 | tf_op jit(solution)/shard_map/ppermute | solution.py:45
  19.5 0.7 collective-permute-start.10
  20.2 2.2 %collective-permute-start.7 = (bf16[128,1024]{1,0:T(8,128)(2,1)S(1)}, bf16[128,1024]{1,0:T(8,128)(2,1)S(1)}, u32[]{:S(2)}, u32[]{:S(2)}) collective-permute-start(bf16[128,1024]{1,0:T(8,128)(2,1)S(1)} %slice_bitcast_fusion.1), channel_id=1, source_target_pairs={{0,96},{16,112},{32,0},{48,16},{64,32},{80,48},{96,64},{112,80},{1... | collective-permute-start | bytes 786440 | tf_op jit(solution)/shard_map/ppermute | solution.py:45
  22.4 0.9 collective-permute-done.6.refs_3_
  23.3 1.3 %collective-permute-start.8 = (f32[40,128]{1,0:T(8,128)S(1)}, f32[40,128]{1,0:T(8,128)S(1)}, u32[]{:S(2)}, u32[]{:S(2)}) collective-permute-start(f32[40,128]{1,0:T(8,128)S(1)} %shard_map.43.refs_0_), channel_id=1, source_target_pairs={{0,128},{16,144},{32,160},{48,176},{64,192},{80,208},{96,224},{112... | collective-permute-start | bytes 61448 | tf_op jit(solution)/shard_map/ppermute | solution.py:45
  24.7 0.8 collective-permute-start.12
  25.5 0.9 collective-permute-done.8.refs_1_
  26.4 1.8 %collective-permute-done.7.b.opp_b = bf16[128,1024]{1,0:T(8,128)(2,1)S(1)} collective-permute-done((bf16[128,1024]{1,0:T(8,128)(2,1)S(1)}, bf16[128,1024]{1,0:T(8,128)(2,1)S(1)}, u32[]{:S(2)}, u32[]{:S(2)}) %collective-permute-start.7) | collective-permute-done | bytes 262176 | tf_op jit(solution)/shard_map/ppermute | solution.py:45
  28.2 1.5 %collective-permute-start.13 = (bf16[2,128,1024]{2,1,0:T(8,128)(2,1)S(1)}, bf16[2,128,1024]{2,1,0:T(8,128)(2,1)S(1)}, u32[]{:S(2)}, u32[]{:S(2)}) collective-permute-start(bf16[2,128,1024]{2,1,0:T(8,128)(2,1)S(1)} %shard_map.46), channel_id=1, source_target_pairs={{0,128},{16,144},{32,160},{48,176},{64,192},{80,208},{96,224},{112... | collective-permute-start | bytes 1572872 | tf_op jit(solution)/shard_map/ppermute | solution.py:45
  29.7 1.4 %shard_map.45 = (f32[5,1024]{1,0:T(8,128)S(1)}, bf16[2,256,1024]{2,1,0:T(8,128)(2,1)S(1)}, bf16[2,512,1024]{2,1,0:T(8,128)(2,1)S(1)}, bf16[2,256,512]{2,1,0:T(8,128)(2,1)S(1)}) custom-call(f32[40,128]{1,0:T(8,128)S(1)} %shard_map.43.refs_0_, f32[40,128]{1,0:T(8,128)S(1)} %collective-permute-done.8.refs_1_, ...), custom_call_target="tpu_custom_call" | custom-call | flops 536870912 | bytes 6352896 | tf_op jit(solution)/shard_map/pallas_call | solution.py:52
  31.1 7.1 %collective-permute-done.12.x_up = bf16[2,128,1024]{2,1,0:T(8,128)(2,1)S(1)} collective-permute-done((bf16[2,128,1024]{2,1,0:T(8,128)(2,1)S(1)}, bf16[2,128,1024]{2,1,0:T(8,128)(2,1)S(1)}, u32[]{:S(2)}, u32[]{:S(2)}) %collective-permute-start.12) | collective-permute-done | bytes 524320 | tf_op jit(solution)/shard_map/ppermute | solution.py:45
  38.2 0.5 collective-permute-done.13.x_far
  38.7 1.3 %shard_map.47 = (bf16[2,512,1024]{2,1,0:T(8,128)(2,1)S(1)}, bf16[2,2,16,1024]{3,2,1,0:T(8,128)(2,1)S(1)}, bf16[2,2,16,1024]{3,2,1,0:T(8,128)(2,1)S(1)}, bf16[2,2...) custom-call(bf16[2,256,1024]{2,1,0:T(8,128)(2,1)S(1)} %get-tuple-ele, ...), custom_call_target="tpu_custom_call" | custom-call | flops 536870912 | bytes 6836224 | tf_op jit(solution)/shard_map/pallas_call | solution.py:52
  40.1 1.7 %collective-permute-start.14 = (bf16[2,2,2,16,1024]{4,3,2,1,0:T(8,128)(2,1)S(1)}, bf16[2,2,2,16,1024]{4,3,2,1,0:T(8,128)(2,1)S(1)}, u32[]{:S(2)}, u32[]{:S(2)}) collective-permute-start(bf16[2,2,2,16,1024]{4,3,2,1,0:T(8,128)(2,1)S(1)} %get-tuple-element.39), channel_id=1, source_target_pairs={{0,1},{1,2},{2,3},{3,4},{4,5},{5,6},{6,7},{7,0},{8,9},{9,10},{10,1... | collective-permute-start | bytes 786440 | tf_op jit(solution)/shard_map/ppermute | solution.py:45
  41.8 4.0 %collective-permute-start.15 = (bf16[2,2,2,16,1024]{4,3,2,1,0:T(8,128)(2,1)S(1)}, bf16[2,2,2,16,1024]{4,3,2,1,0:T(8,128)(2,1)S(1)}, u32[]{:S(2)}, u32[]{:S(2)}) collective-permute-start(bf16[2,2,2,16,1024]{4,3,2,1,0:T(8,128)(2,1)S(1)} %get-tuple-element.40), channel_id=1, source_target_pairs={{0,7},{1,0},{2,1},{3,2},{4,3},{5,4},{6,5},{7,6},{8,15},{9,8},{10,9... | collective-permute-start | bytes 786440 | tf_op jit(solution)/shard_map/ppermute | solution.py:45
  45.8 3.6 %collective-permute-start.17 = (bf16[2,16,1024]{2,1,0:T(8,128)(2,1)S(1)}, bf16[2,16,1024]{2,1,0:T(8,128)(2,1)S(1)}, u32[]{:S(2)}, u32[]{:S(2)}) collective-permute-start(bf16[2,16,1024]{2,1,0:T(8,128)(2,1)S(1)} %get-tuple-element.42), channel_id=1, source_target_pairs={{0,6},{1,7},{2,0},{3,1},{4,2},{5,3},{6,4},{7,5},{8,14},{9,15},{10,... | collective-permute-start | bytes 196616 | tf_op jit(solution)/shard_map/ppermute | solution.py:45
  49.4 2.5 %collective-permute-done.16.half_a = bf16[2,16,1024]{2,1,0:T(8,128)(2,1)S(1)} collective-permute-done((bf16[2,16,1024]{2,1,0:T(8,128)(2,1)S(1)}, bf16[2,16,1024]{2,1,0:T(8,128)(2,1)S(1)}, u32[]{:S(2)}, u32[]{:S(2)}) %collective-permute-start.16) | collective-permute-done | bytes 65568 | tf_op jit(solution)/shard_map/ppermute | solution.py:45
  51.9 1.4 %collective-permute-done.17.half_b = bf16[2,16,1024]{2,1,0:T(8,128)(2,1)S(1)} collective-permute-done((bf16[2,16,1024]{2,1,0:T(8,128)(2,1)S(1)}, bf16[2,16,1024]{2,1,0:T(8,128)(2,1)S(1)}, u32[]{:S(2)}, u32[]{:S(2)}) %collective-permute-start.17) | collective-permute-done | bytes 65568 | tf_op jit(solution)/shard_map/ppermute | solution.py:45
  53.4 2.3 %collective-permute-start.18 = (bf16[2,2,16,1024]{3,2,1,0:T(8,128)(2,1)S(1)}, bf16[2,2,16,1024]{3,2,1,0:T(8,128)(2,1)S(1)}, u32[]{:S(2)}, u32[]{:S(2)}) collective-permute-start(bf16[2,2,16,1024]{3,2,1,0:T(8,128)(2,1)S(1)} %get-tuple-element.45), channel_id=1, source_target_pairs={{0,2},{1,3},{2,4},{3,5},{4,6},{5,7},{6,0},{7,1},{8,10},{9,11},{10,... | collective-permute-start | bytes 393224 | tf_op jit(solution)/shard_map/ppermute | solution.py:45
  55.7 1.3 %collective-permute-start.19 = (bf16[2,2,16,1024]{3,2,1,0:T(8,128)(2,1)S(1)}, bf16[2,2,16,1024]{3,2,1,0:T(8,128)(2,1)S(1)}, u32[]{:S(2)}, u32[]{:S(2)}) collective-permute-start(bf16[2,2,16,1024]{3,2,1,0:T(8,128)(2,1)S(1)} %get-tuple-element.46), channel_id=1, source_target_pairs={{0,6},{1,7},{2,0},{3,1},{4,2},{5,3},{6,4},{7,5},{8,14},{9,15},{10,... | collective-permute-start | bytes 393224 | tf_op jit(solution)/shard_map/ppermute | solution.py:45
  57.0 3.0 %collective-permute-done.18.far_up = bf16[2,2,16,1024]{3,2,1,0:T(8,128)(2,1)S(1)} collective-permute-done((bf16[2,2,16,1024]{3,2,1,0:T(8,128)(2,1)S(1)}, bf16[2,2,16,1024]{3,2,1,0:T(8,128)(2,1)S(1)}, u32[]{:S(2)}, u32[]{:S(2)}) %collective-permute-start.18) | collective-permute-done | bytes 131104 | tf_op jit(solution)/shard_map/ppermute | solution.py:45
  60.0 1.0 collective-permute-done.19.far_down
  61.1 2.7 %collective-permute-start.20 = (bf16[2,2,16,1024]{3,2,1,0:T(8,128)(2,1)S(1)}, bf16[2,2,16,1024]{3,2,1,0:T(8,128)(2,1)S(1)}, u32[]{:S(2)}, u32[]{:S(2)}) collective-permute-start(bf16[2,2,16,1024]{3,2,1,0:T(8,128)(2,1)S(1)} %shard_map.49.a), channel_id=1, source_target_pairs={{0,8},{1,9},{2,10},{3,11},{4,12},{5,13},{6,14},{7,15},{8,0},{9,1},... | collective-permute-start | bytes 393224 | tf_op jit(solution)/shard_map/ppermute | solution.py:45
  63.8 2.7 %collective-permute-done.20.b = bf16[2,2,16,1024]{3,2,1,0:T(8,128)(2,1)S(1)} collective-permute-done((bf16[2,2,16,1024]{3,2,1,0:T(8,128)(2,1)S(1)}, bf16[2,2,16,1024]{3,2,1,0:T(8,128)(2,1)S(1)}, u32[]{:S(2)}, u32[]{:S(2)}) %collective-permute-start.20) | collective-permute-done | bytes 131104 | tf_op jit(solution)/shard_map/ppermute | solution.py:45
  66.6 2.6 %collective-permute-start.25 = (bf16[2,2,16,1024]{3,2,1,0:T(8,128)(2,1)S(1)}, bf16[2,2,16,1024]{3,2,1,0:T(8,128)(2,1)S(1)}, u32[]{:S(2)}, u32[]{:S(2)}) collective-permute-start(bf16[2,2,16,1024]{3,2,1,0:T(8,128)(2,1)S(1)} %shard_map.50.refs_0_), channel_id=1, source_target_pairs={{0,6},{1,7},{2,0},{3,1},{4,2},{5,3},{6,4},{7,5},{8,14},{9,15},{10,... | collective-permute-start | bytes 393224 | tf_op jit(solution)/shard_map/ppermute | solution.py:45
  69.2 0.3 collective-permute-start.22
  69.5 1.0 collective-permute-start.27
  70.5 0.4 collective-permute-start.21
  70.9 2.3 %collective-permute-done.25.refs_6_ = bf16[2,2,16,1024]{3,2,1,0:T(8,128)(2,1)S(1)} collective-permute-done((bf16[2,2,16,1024]{3,2,1,0:T(8,128)(2,1)S(1)}, bf16[2,2,16,1024]{3,2,1,0:T(8,128)(2,1)S(1)}, u32[]{:S(2)}, u32[]{:S(2)}) %collective-permute-start.25) | collective-permute-done | bytes 131104 | tf_op jit(solution)/shard_map/ppermute | solution.py:45
  73.2 0.3 collective-permute-start.26
  73.5 1.9 %collective-permute-done.22.refs_2_ = bf16[2,2,16,1024]{3,2,1,0:T(8,128)(2,1)S(1)} collective-permute-done((bf16[2,2,16,1024]{3,2,1,0:T(8,128)(2,1)S(1)}, bf16[2,2,16,1024]{3,2,1,0:T(8,128)(2,1)S(1)}, u32[]{:S(2)}, u32[]{:S(2)}) %collective-permute-start.22) | collective-permute-done | bytes 131104 | tf_op jit(solution)/shard_map/ppermute | solution.py:45
  75.4 1.5 %collective-permute-start.24 = (bf16[2,2,16,1024]{3,2,1,0:T(8,128)(2,1)S(1)}, bf16[2,2,16,1024]{3,2,1,0:T(8,128)(2,1)S(1)}, u32[]{:S(2)}, u32[]{:S(2)}) collective-permute-start(bf16[2,2,16,1024]{3,2,1,0:T(8,128)(2,1)S(1)} %collective-permute-done.22.refs_2_), channel_id=1, source_target_pairs={{0,2},{1,3},{2,4},{3,5},{4,6},{5,7},{6,0},{7,1},{8,10},{9,11},{10,... | collective-permute-start | bytes 393224 | tf_op jit(solution)/shard_map/ppermute | solution.py:45
  77.0 1.5 %collective-permute-start.23 = (bf16[2,2,16,1024]{3,2,1,0:T(8,128)(2,1)S(1)}, bf16[2,2,16,1024]{3,2,1,0:T(8,128)(2,1)S(1)}, u32[]{:S(2)}, u32[]{:S(2)}) collective-permute-start(bf16[2,2,16,1024]{3,2,1,0:T(8,128)(2,1)S(1)} %collective-permute-done.22.refs_2_), channel_id=1, source_target_pairs={{0,1},{1,2},{2,3},{3,4},{4,5},{5,6},{6,7},{7,0},{8,9},{9,10},{10,1... | collective-permute-start | bytes 393224 | tf_op jit(solution)/shard_map/ppermute | solution.py:45
  78.4 4.5 %collective-permute-done.24.refs_4_ = bf16[2,2,16,1024]{3,2,1,0:T(8,128)(2,1)S(1)} collective-permute-done((bf16[2,2,16,1024]{3,2,1,0:T(8,128)(2,1)S(1)}, bf16[2,2,16,1024]{3,2,1,0:T(8,128)(2,1)S(1)}, u32[]{:S(2)}, u32[]{:S(2)}) %collective-permute-start.24) | collective-permute-done | bytes 131104 | tf_op jit(solution)/shard_map/ppermute | solution.py:45
  82.9 2.5 %collective-permute-done.23.refs_3_ = bf16[2,2,16,1024]{3,2,1,0:T(8,128)(2,1)S(1)} collective-permute-done((bf16[2,2,16,1024]{3,2,1,0:T(8,128)(2,1)S(1)}, bf16[2,2,16,1024]{3,2,1,0:T(8,128)(2,1)S(1)}, u32[]{:S(2)}, u32[]{:S(2)}) %collective-permute-start.23) | collective-permute-done | bytes 131104 | tf_op jit(solution)/shard_map/ppermute | solution.py:45
  85.5 1.6 %shard_map.51 = (f32[2,128,1024]{2,1,0:T(8,128)S(1)}, f32[2,128,1024]{2,1,0:T(8,128)S(1)}, f32[16,4,1024]{2,1,0:T(4,128)S(1)}) custom-call(bf16[2,2,16,1024]{3,2,1,0:T(8,128)(2,1)S(1)} %shard_map.50.refs_0_, bf16[2,2,16,1024]{3,2,1,0:T(8,128)(2,1)S(1)} %collective-permute-done.21.refs_1_, bf16[2,2,16,1024]{3,2,1,0:T(8,128)(2,1)S(1)} %collective-permute-done.22.refs_2_, ...), custom_call_target="tpu_custom_call" | custom-call | flops 1073741824 | bytes 8671232 | tf_op jit(solution)/shard_map/pallas_call | solution.py:52
  87.1 10.2 %collective-permute-start.28 = (f32[2,128,1024]{2,1,0:T(8,128)S(1)}, f32[2,128,1024]{2,1,0:T(8,128)S(1)}, u32[]{:S(2)}, u32[]{:S(2)}) collective-permute-start(f32[2,128,1024]{2,1,0:T(8,128)S(1)} %get-tuple-element.50), channel_id=1, source_target_pairs={{0,16},{16,0},{32,48},{48,32},{64,80},{80,64},{96,112},{112,96},{1... | collective-permute-start | bytes 3145736 | tf_op jit(solution)/shard_map/ppermute | solution.py:45
  97.3 11.3 %all_to_all.5.sums = f32[16,4,1024]{2,1,0:T(4,128)S(1)} all-to-all(f32[16,4,1024]{2,1,0:T(4,128)S(1)} %get-tuple-element.51), channel_id=1, replica_groups=mesh['dp'=16,'feat'=16] {'dp'}, dimensions={0} | all-to-all | bytes 524288 | tf_op jit(solution)/shard_map/all_to_all | solution.py:352
  108.6 1.0 shard_map.52
  (26 shorter events, 0.4 us)
Async XLA Ops:
  1.7 17.8 %collective-permute-start.2 = (bf16[2,128,1024]{2,1,0:T(8,128)(2,1)S(1)}, bf16[2,128,1024]{2,1,0:T(8,128)(2,1)S(1)}, u32[]{:S(2)}, u32[]{:S(2)}) collective-permute-start(bf16[2,128,1024]{2,1,0:T(8,128)(2,1)S(1)} %pad_maximum_fusion.views.refs_3_), channel_id=1, source_target_pairs={{0,96},{16,112},{32,0},{48,16},{64,32},{80,48},{96,64},{112,80},{1... | collective-permute-start | bytes 1572872 | tf_op jit(solution)/shard_map/ppermute | solution.py:45
  5.4 14.1 %collective-permute-start.1 = (bf16[2,128,1024]{2,1,0:T(8,128)(2,1)S(1)}, bf16[2,128,1024]{2,1,0:T(8,128)(2,1)S(1)}, u32[]{:S(2)}, u32[]{:S(2)}) collective-permute-start(bf16[2,128,1024]{2,1,0:T(8,128)(2,1)S(1)} %pad_maximum_fusion.views.refs_3_), channel_id=1, source_target_pairs={{0,32},{16,48},{32,64},{48,80},{64,96},{80,112},{96,0},{112,16},{1... | collective-permute-start | bytes 1572872 | tf_op jit(solution)/shard_map/ppermute | solution.py:45
  5.4 17.0 %collective-permute-start.5 = (bf16[2,128,1024]{2,1,0:T(8,128)(2,1)S(1)}, bf16[2,128,1024]{2,1,0:T(8,128)(2,1)S(1)}, u32[]{:S(2)}, u32[]{:S(2)}) collective-permute-start(bf16[2,128,1024]{2,1,0:T(8,128)(2,1)S(1)} %pad_maximum_fusion.views.refs_3_), channel_id=1, source_target_pairs={{0,128},{16,144},{32,160},{48,176},{64,192},{80,208},{96,224},{112... | collective-permute-start | bytes 1572872 | tf_op jit(solution)/shard_map/ppermute | solution.py:45
  6.9 2.2 %collective-permute-start = (f32[40,128]{1,0:T(8,128)S(1)}, f32[40,128]{1,0:T(8,128)S(1)}, u32[]{:S(2)}, u32[]{:S(2)}) collective-permute-start(f32[40,128]{1,0:T(8,128)S(1)} %shard_map.41.refs_0_), channel_id=1, source_target_pairs={{0,16},{16,0},{32,48},{48,32},{64,80},{80,64},{96,112},{112,96},{1... | collective-permute-start | bytes 61448 | tf_op jit(solution)/shard_map/ppermute | solution.py:45
  9.1 7.3 %collective-permute-start.4 = (f32[40,128]{1,0:T(8,128)S(1)}, f32[40,128]{1,0:T(8,128)S(1)}, u32[]{:S(2)}, u32[]{:S(2)}) collective-permute-start(f32[40,128]{1,0:T(8,128)S(1)} %shard_map.42.refs_0_), channel_id=1, source_target_pairs={{0,96},{16,112},{32,0},{48,16},{64,32},{80,48},{96,64},{112,80},{1... | collective-permute-start | bytes 61448 | tf_op jit(solution)/shard_map/ppermute | solution.py:45
  12.1 7.4 %collective-permute-start.3 = (f32[40,128]{1,0:T(8,128)S(1)}, f32[40,128]{1,0:T(8,128)S(1)}, u32[]{:S(2)}, u32[]{:S(2)}) collective-permute-start(f32[40,128]{1,0:T(8,128)S(1)} %shard_map.42.refs_0_), channel_id=1, source_target_pairs={{0,32},{16,48},{32,64},{48,80},{64,96},{80,112},{96,0},{112,16},{1... | collective-permute-start | bytes 61448 | tf_op jit(solution)/shard_map/ppermute | solution.py:45
  16.4 13.3 %collective-permute-start.9 = (bf16[2,128,1024]{2,1,0:T(8,128)(2,1)S(1)}, bf16[2,128,1024]{2,1,0:T(8,128)(2,1)S(1)}, u32[]{:S(2)}, u32[]{:S(2)}) collective-permute-start(bf16[2,128,1024]{2,1,0:T(8,128)(2,1)S(1)} %pad_maximum_fusion.views.refs_3_), channel_id=1, source_target_pairs={{0,16},{16,0},{32,48},{48,32},{64,80},{80,64},{96,112},{112,96},{1... | collective-permute-start | bytes 1572872 | tf_op jit(solution)/shard_map/ppermute | solution.py:45
  19.5 3.8 %collective-permute-start.6 = (f32[40,128]{1,0:T(8,128)S(1)}, f32[40,128]{1,0:T(8,128)S(1)}, u32[]{:S(2)}, u32[]{:S(2)}) collective-permute-start(f32[40,128]{1,0:T(8,128)S(1)} %collective-permute-done.3.refs_1_), channel_id=1, source_target_pairs={{0,32},{16,48},{32,64},{48,80},{64,96},{80,112},{96,0},{112,16},{1... | collective-permute-start | bytes 61448 | tf_op jit(solution)/shard_map/ppermute | solution.py:45
  19.5 8.6 %collective-permute-start.10 = (bf16[128,1024]{1,0:T(8,128)(2,1)S(1)}, bf16[128,1024]{1,0:T(8,128)(2,1)S(1)}, u32[]{:S(2)}, u32[]{:S(2)}) collective-permute-start(bf16[128,1024]{1,0:T(8,128)(2,1)S(1)} %slice_bitcast_fusion), channel_id=1, source_target_pairs={{0,32},{16,48},{32,64},{48,80},{64,96},{80,112},{96,0},{112,16},{1... | collective-permute-start | bytes 786440 | tf_op jit(solution)/shard_map/ppermute | solution.py:45
  20.2 8.0 %collective-permute-start.7 = (bf16[128,1024]{1,0:T(8,128)(2,1)S(1)}, bf16[128,1024]{1,0:T(8,128)(2,1)S(1)}, u32[]{:S(2)}, u32[]{:S(2)}) collective-permute-start(bf16[128,1024]{1,0:T(8,128)(2,1)S(1)} %slice_bitcast_fusion.1), channel_id=1, source_target_pairs={{0,96},{16,112},{32,0},{48,16},{64,32},{80,48},{96,64},{112,80},{1... | collective-permute-start | bytes 786440 | tf_op jit(solution)/shard_map/ppermute | solution.py:45
  23.3 3.0 %collective-permute-start.8 = (f32[40,128]{1,0:T(8,128)S(1)}, f32[40,128]{1,0:T(8,128)S(1)}, u32[]{:S(2)}, u32[]{:S(2)}) collective-permute-start(f32[40,128]{1,0:T(8,128)S(1)} %shard_map.43.refs_0_), channel_id=1, source_target_pairs={{0,128},{16,144},{32,160},{48,176},{64,192},{80,208},{96,224},{112... | collective-permute-start | bytes 61448 | tf_op jit(solution)/shard_map/ppermute | solution.py:45
  24.7 13.5 %collective-permute-start.12 = (bf16[2,128,1024]{2,1,0:T(8,128)(2,1)S(1)}, bf16[2,128,1024]{2,1,0:T(8,128)(2,1)S(1)}, u32[]{:S(2)}, u32[]{:S(2)}) collective-permute-start(bf16[2,128,1024]{2,1,0:T(8,128)(2,1)S(1)} %shard_map.44.refs_6_), channel_id=1, source_target_pairs={{0,96},{16,112},{32,0},{48,16},{64,32},{80,48},{96,64},{112,80},{1... | collective-permute-start | bytes 1572872 | tf_op jit(solution)/shard_map/ppermute | solution.py:45
  26.4 11.9 %collective-permute-start.11 = (bf16[2,128,1024]{2,1,0:T(8,128)(2,1)S(1)}, bf16[2,128,1024]{2,1,0:T(8,128)(2,1)S(1)}, u32[]{:S(2)}, u32[]{:S(2)}) collective-permute-start(bf16[2,128,1024]{2,1,0:T(8,128)(2,1)S(1)} %shard_map.44.refs_6_), channel_id=1, source_target_pairs={{0,32},{16,48},{32,64},{48,80},{64,96},{80,112},{96,0},{112,16},{1... | collective-permute-start | bytes 1572872 | tf_op jit(solution)/shard_map/ppermute | solution.py:45
  28.2 10.5 %collective-permute-start.13 = (bf16[2,128,1024]{2,1,0:T(8,128)(2,1)S(1)}, bf16[2,128,1024]{2,1,0:T(8,128)(2,1)S(1)}, u32[]{:S(2)}, u32[]{:S(2)}) collective-permute-start(bf16[2,128,1024]{2,1,0:T(8,128)(2,1)S(1)} %shard_map.46), channel_id=1, source_target_pairs={{0,128},{16,144},{32,160},{48,176},{64,192},{80,208},{96,224},{112... | collective-permute-start | bytes 1572872 | tf_op jit(solution)/shard_map/ppermute | solution.py:45
  40.1 13.2 %collective-permute-start.14 = (bf16[2,2,2,16,1024]{4,3,2,1,0:T(8,128)(2,1)S(1)}, bf16[2,2,2,16,1024]{4,3,2,1,0:T(8,128)(2,1)S(1)}, u32[]{:S(2)}, u32[]{:S(2)}) collective-permute-start(bf16[2,2,2,16,1024]{4,3,2,1,0:T(8,128)(2,1)S(1)} %get-tuple-element.39), channel_id=1, source_target_pairs={{0,1},{1,2},{2,3},{3,4},{4,5},{5,6},{6,7},{7,0},{8,9},{9,10},{10,1... | collective-permute-start | bytes 786440 | tf_op jit(solution)/shard_map/ppermute | solution.py:45
  41.8 11.5 %collective-permute-start.15 = (bf16[2,2,2,16,1024]{4,3,2,1,0:T(8,128)(2,1)S(1)}, bf16[2,2,2,16,1024]{4,3,2,1,0:T(8,128)(2,1)S(1)}, u32[]{:S(2)}, u32[]{:S(2)}) collective-permute-start(bf16[2,2,2,16,1024]{4,3,2,1,0:T(8,128)(2,1)S(1)} %get-tuple-element.40), channel_id=1, source_target_pairs={{0,7},{1,0},{2,1},{3,2},{4,3},{5,4},{6,5},{7,6},{8,15},{9,8},{10,9... | collective-permute-start | bytes 786440 | tf_op jit(solution)/shard_map/ppermute | solution.py:45
  45.8 6.1 %collective-permute-start.16 = (bf16[2,16,1024]{2,1,0:T(8,128)(2,1)S(1)}, bf16[2,16,1024]{2,1,0:T(8,128)(2,1)S(1)}, u32[]{:S(2)}, u32[]{:S(2)}) collective-permute-start(bf16[2,16,1024]{2,1,0:T(8,128)(2,1)S(1)} %get-tuple-element.41), channel_id=1, source_target_pairs={{0,2},{1,3},{2,4},{3,5},{4,6},{5,7},{6,0},{7,1},{8,10},{9,11},{10,... | collective-permute-start | bytes 196616 | tf_op jit(solution)/shard_map/ppermute | solution.py:45
  45.8 7.5 %collective-permute-start.17 = (bf16[2,16,1024]{2,1,0:T(8,128)(2,1)S(1)}, bf16[2,16,1024]{2,1,0:T(8,128)(2,1)S(1)}, u32[]{:S(2)}, u32[]{:S(2)}) collective-permute-start(bf16[2,16,1024]{2,1,0:T(8,128)(2,1)S(1)} %get-tuple-element.42), channel_id=1, source_target_pairs={{0,6},{1,7},{2,0},{3,1},{4,2},{5,3},{6,4},{7,5},{8,14},{9,15},{10,... | collective-permute-start | bytes 196616 | tf_op jit(solution)/shard_map/ppermute | solution.py:45
  53.4 6.6 %collective-permute-start.18 = (bf16[2,2,16,1024]{3,2,1,0:T(8,128)(2,1)S(1)}, bf16[2,2,16,1024]{3,2,1,0:T(8,128)(2,1)S(1)}, u32[]{:S(2)}, u32[]{:S(2)}) collective-permute-start(bf16[2,2,16,1024]{3,2,1,0:T(8,128)(2,1)S(1)} %get-tuple-element.45), channel_id=1, source_target_pairs={{0,2},{1,3},{2,4},{3,5},{4,6},{5,7},{6,0},{7,1},{8,10},{9,11},{10,... | collective-permute-start | bytes 393224 | tf_op jit(solution)/shard_map/ppermute | solution.py:45
  55.7 5.3 %collective-permute-start.19 = (bf16[2,2,16,1024]{3,2,1,0:T(8,128)(2,1)S(1)}, bf16[2,2,16,1024]{3,2,1,0:T(8,128)(2,1)S(1)}, u32[]{:S(2)}, u32[]{:S(2)}) collective-permute-start(bf16[2,2,16,1024]{3,2,1,0:T(8,128)(2,1)S(1)} %get-tuple-element.46), channel_id=1, source_target_pairs={{0,6},{1,7},{2,0},{3,1},{4,2},{5,3},{6,4},{7,5},{8,14},{9,15},{10,... | collective-permute-start | bytes 393224 | tf_op jit(solution)/shard_map/ppermute | solution.py:45
  61.1 5.4 %collective-permute-start.20 = (bf16[2,2,16,1024]{3,2,1,0:T(8,128)(2,1)S(1)}, bf16[2,2,16,1024]{3,2,1,0:T(8,128)(2,1)S(1)}, u32[]{:S(2)}, u32[]{:S(2)}) collective-permute-start(bf16[2,2,16,1024]{3,2,1,0:T(8,128)(2,1)S(1)} %shard_map.49.a), channel_id=1, source_target_pairs={{0,8},{1,9},{2,10},{3,11},{4,12},{5,13},{6,14},{7,15},{8,0},{9,1},... | collective-permute-start | bytes 393224 | tf_op jit(solution)/shard_map/ppermute | solution.py:45
  66.6 6.6 %collective-permute-start.25 = (bf16[2,2,16,1024]{3,2,1,0:T(8,128)(2,1)S(1)}, bf16[2,2,16,1024]{3,2,1,0:T(8,128)(2,1)S(1)}, u32[]{:S(2)}, u32[]{:S(2)}) collective-permute-start(bf16[2,2,16,1024]{3,2,1,0:T(8,128)(2,1)S(1)} %shard_map.50.refs_0_), channel_id=1, source_target_pairs={{0,6},{1,7},{2,0},{3,1},{4,2},{5,3},{6,4},{7,5},{8,14},{9,15},{10,... | collective-permute-start | bytes 393224 | tf_op jit(solution)/shard_map/ppermute | solution.py:45
  69.2 6.2 %collective-permute-start.22 = (bf16[2,2,16,1024]{3,2,1,0:T(8,128)(2,1)S(1)}, bf16[2,2,16,1024]{3,2,1,0:T(8,128)(2,1)S(1)}, u32[]{:S(2)}, u32[]{:S(2)}) collective-permute-start(bf16[2,2,16,1024]{3,2,1,0:T(8,128)(2,1)S(1)} %shard_map.50.refs_0_), channel_id=1, source_target_pairs={{0,2},{1,3},{2,4},{3,5},{4,6},{5,7},{6,0},{7,1},{8,10},{9,11},{10,... | collective-permute-start | bytes 393224 | tf_op jit(solution)/shard_map/ppermute | solution.py:45
  69.5 9.0 %collective-permute-start.27 = (bf16[2,2,16,1024]{3,2,1,0:T(8,128)(2,1)S(1)}, bf16[2,2,16,1024]{3,2,1,0:T(8,128)(2,1)S(1)}, u32[]{:S(2)}, u32[]{:S(2)}) collective-permute-start(bf16[2,2,16,1024]{3,2,1,0:T(8,128)(2,1)S(1)} %shard_map.50.refs_0_), channel_id=1, source_target_pairs={{0,7},{1,0},{2,1},{3,2},{4,3},{5,4},{6,5},{7,6},{8,15},{9,8},{10,9... | collective-permute-start | bytes 393224 | tf_op jit(solution)/shard_map/ppermute | solution.py:45
  70.5 7.9 %collective-permute-start.21 = (bf16[2,2,16,1024]{3,2,1,0:T(8,128)(2,1)S(1)}, bf16[2,2,16,1024]{3,2,1,0:T(8,128)(2,1)S(1)}, u32[]{:S(2)}, u32[]{:S(2)}) collective-permute-start(bf16[2,2,16,1024]{3,2,1,0:T(8,128)(2,1)S(1)} %shard_map.50.refs_0_), channel_id=1, source_target_pairs={{0,1},{1,2},{2,3},{3,4},{4,5},{5,6},{6,7},{7,0},{8,9},{9,10},{10,1... | collective-permute-start | bytes 393224 | tf_op jit(solution)/shard_map/ppermute | solution.py:45
  73.2 5.2 %collective-permute-start.26 = (bf16[2,2,16,1024]{3,2,1,0:T(8,128)(2,1)S(1)}, bf16[2,2,16,1024]{3,2,1,0:T(8,128)(2,1)S(1)}, u32[]{:S(2)}, u32[]{:S(2)}) collective-permute-start(bf16[2,2,16,1024]{3,2,1,0:T(8,128)(2,1)S(1)} %collective-permute-done.25.refs_6_), channel_id=1, source_target_pairs={{0,7},{1,0},{2,1},{3,2},{4,3},{5,4},{6,5},{7,6},{8,15},{9,8},{10,9... | collective-permute-start | bytes 393224 | tf_op jit(solution)/shard_map/ppermute | solution.py:45
  75.4 7.5 %collective-permute-start.24 = (bf16[2,2,16,1024]{3,2,1,0:T(8,128)(2,1)S(1)}, bf16[2,2,16,1024]{3,2,1,0:T(8,128)(2,1)S(1)}, u32[]{:S(2)}, u32[]{:S(2)}) collective-permute-start(bf16[2,2,16,1024]{3,2,1,0:T(8,128)(2,1)S(1)} %collective-permute-done.22.refs_2_), channel_id=1, source_target_pairs={{0,2},{1,3},{2,4},{3,5},{4,6},{5,7},{6,0},{7,1},{8,10},{9,11},{10,... | collective-permute-start | bytes 393224 | tf_op jit(solution)/shard_map/ppermute | solution.py:45
  77.0 8.5 %collective-permute-start.23 = (bf16[2,2,16,1024]{3,2,1,0:T(8,128)(2,1)S(1)}, bf16[2,2,16,1024]{3,2,1,0:T(8,128)(2,1)S(1)}, u32[]{:S(2)}, u32[]{:S(2)}) collective-permute-start(bf16[2,2,16,1024]{3,2,1,0:T(8,128)(2,1)S(1)} %collective-permute-done.22.refs_2_), channel_id=1, source_target_pairs={{0,1},{1,2},{2,3},{3,4},{4,5},{5,6},{6,7},{7,0},{8,9},{9,10},{10,1... | collective-permute-start | bytes 393224 | tf_op jit(solution)/shard_map/ppermute | solution.py:45
  87.1 21.5 %collective-permute-start.28 = (f32[2,128,1024]{2,1,0:T(8,128)S(1)}, f32[2,128,1024]{2,1,0:T(8,128)S(1)}, u32[]{:S(2)}, u32[]{:S(2)}) collective-permute-start(f32[2,128,1024]{2,1,0:T(8,128)S(1)} %get-tuple-element.50), channel_id=1, source_target_pairs={{0,16},{16,0},{32,48},{48,32},{64,80},{80,64},{96,112},{112,96},{1... | collective-permute-start | bytes 3145736 | tf_op jit(solution)/shard_map/ppermute | solution.py:45
